TPU v7x, 32 devices: a whole 2x2x4 slice. The times are simulated.
32 devices in a mesh: slab: 16 (over z, y, x), panel: 2 (over core).
Axes of the slice: x: 2, y: 2, z: 4, core: 2. Of those that a mesh axis runs over, the one named last changes fastest.
Arguments:
- weights: bfloat16 [5120, 8192], P('slab', 'panel'), may hold values from -6 to 6
- gain: float32 [8192], replicated, may hold values from 0.1 to 1.9
- rotation: float32 [8192, 8192], P('panel', 'slab'), may hold values from -0.0625 to 0.0625
- tokens: bfloat16 [512, 8192], P(None, 'slab'), may hold values from -1400 to 1400
Outputs:
- served: bfloat16 [2, 2560, 8192], P('panel', 'slab')
- qkv: bfloat16 [512, 5120], P('slab', 'panel')
All inputs are finite; a program needn't handle non-finite values.
Results may differ from a plain program's by a relative error of at most 0.0049.
Values may be sent and summed in bfloat16 or wider, within the bound.
No kernel may reach another device: no remote copies, remote signals or barrier semaphores. Data moves between devices by JAX's collectives and lax.ppermute only.
A program may use at most 192 MiB of HBM per device.

v0:
```python
import math

import jax
import jax.numpy as jnp
from jax import lax
from jax.sharding import PartitionSpec as P

D = 8192


EPS = 1e-05


def shards(weights, gain, rotation, tokens):
    width_rows = rotation.shape[0]
    gain_block = lax.dynamic_slice_in_dim(gain, lax.axis_index("panel") * width_rows, width_rows, 0)
    partial_value = jnp.dot(
        lax.all_gather(weights, "slab", axis=0, tiled=True).astype(jnp.float32)
        * gain_block[None, :],
        rotation,
        precision=lax.Precision.HIGHEST,
        preferred_element_type=jnp.float32,
    )
    folded = lax.psum_scatter(partial_value, "panel", scatter_dimension=0, tiled=True)
    exported = folded.astype(jnp.bfloat16)
    product = lax.dot_general(
        tokens, exported, (((1,), (1,)), ((), ())), preferred_element_type=jnp.float32
    )
    widened = tokens.astype(jnp.float32)
    squares = jnp.sum(widened * widened, axis=1)
    whole, whole_squares = lax.psum((product, squares), "slab")
    own_count = tokens.shape[0] // lax.axis_size("slab")
    first_token = lax.axis_index("slab") * own_count
    total = lax.dynamic_slice_in_dim(whole, first_token, own_count, 0)
    square_sum = lax.dynamic_slice_in_dim(whole_squares, first_token, own_count, 0)
    meansq = square_sum / D
    qkv = (total * lax.rsqrt(meansq + EPS)[:, None] / math.sqrt(D)).astype(jnp.bfloat16)
    whole_rows = lax.all_to_all(exported, "slab", split_axis=0, concat_axis=1, tiled=True)
    return (whole_rows[None], qkv)


def solution(mesh):
    placed = (P("slab", "panel"), P(), P("panel", "slab"), P(None, "slab"))
    return jax.shard_map(
        shards,
        mesh=mesh,
        in_specs=placed,
        out_specs=(P("panel", "slab", None), P("slab", "panel")),
        check_vma=False,
    )
```

profile of v0, /device:TPU:0, one launch (start us, length us, event | category | flops | bytes accessed | tf_op | source)
XLA Modules:
  0.0 860.2 jit_solution(16091345118098784542)
XLA Ops:
  7.2 0.0 all-gather.2.cloned.1.call-start
  7.2 0.7 all-gather.2.cloned.1.call-update
  7.9 0.0 reduce-scatter.2.cloned.1.call-start
  7.9 0.7 dynamic_slice.9
  8.7 434.8 %all-gather.2.cloned.1.call-done = bf16[5120,4096]{1,0:T(8,128)(2,1)} async-done(((bf16[320,4096]{1,0:T(8,128)(2,1)}), bf16[5120,4096]{1,0:T(8,128)(2,1)}) %all-gather.2.cloned.1.call-update) | async-done | bytes 41943056 | tf_op jit(solution)/shard_map/all_gather | solution.py:18
  443.5 139.9 %fusion = f32[5120,512]{1,0:T(8,128)} fusion(f32[4096,512]{1,0:T(8,128)} %param.6, bf16[5120,4096]{1,0:T(8,128)(2,1)} %all-gather.2.cloned.1.call-done, f32[4096]{0:T(1024)S(1)} %dynamic_slice.9), kind=kOutput, calls=%fused_computation | convolution fusion | flops 128890961920 | bytes 60833792 | tf_op jit(solution)/shard_map/dot_general | solution.py:17
  583.3 0.0 reduce-scatter.2.cloned.1.call-update
  583.4 0.0 copy-start
  583.4 0.0 all-reduce.2.cloned.1.call-start
  583.4 17.3 %reduce-scatter.2.cloned.1.call-done = f32[2560,512]{1,0:T(8,128)} async-done(((f32[5120,512]{1,0:T(8,128)}), f32[2560,512]{1,0:T(8,128)}) %reduce-scatter.2.cloned.1.call-update) | async-done | bytes 5242896 | tf_op jit(solution)/shard_map/reduce_scatter | solution.py:24
  600.7 4.3 convert_element_type.13
  605.0 0.0 copy-done
  605.0 5.6 convolution_bitcast_fusion
  610.7 0.0 all-reduce.2.cloned.1.call-update
  610.7 6.9 all-to-all-start
  617.6 0.2 multiply_reduce_fusion
  617.8 120.9 %psum.15 = f32[512]{0:T(512)S(1)} all-reduce(f32[512]{0:T(512)S(1)} %multiply_reduce_fusion), channel_id=1, replica_groups=mesh['slab'=16,'panel'=2] {'slab'}, use_global_device_ids=true, to_apply=%region_3.0 | all-reduce | flops 512 | bytes 4096 | tf_op jit(solution)/shard_map/psum | solution.py:31
  738.6 0.1 add_rsqrt_fusion
  738.7 0.0 all-to-all-done
  738.7 3.0 copy.6
  741.7 5.3 broadcast_in_dim.2
  746.9 104.1 %all-reduce.2.cloned.1.call-done = f32[512,2560]{0,1:T(8,128)} async-done(((f32[512,2560]{0,1:T(8,128)}), f32[512,2560]{0,1:T(8,128)}) %all-reduce.2.cloned.1.call-update) | async-done | bytes 5242896 | tf_op jit(solution)/shard_map/psum | solution.py:31
  851.0 1.7 multiply_convert_fusion
  852.7 0.9 copy.7
Async XLA Ops:
  7.2 436.3 %all-gather.2.cloned.1.call-start = ((), (), s32[]{:S(2)}) async-start(), calls=%async_computation.2 | async-start | bytes 44564480 | tf_op jit(solution)/shard_map/all_gather | solution.py:18
  7.9 592.8 %reduce-scatter.2.cloned.1.call-start = ((), (), s32[]{:S(2)}) async-start(), calls=%async_computation.3 | async-start | bytes 15728640 | tf_op jit(solution)/shard_map/reduce_scatter | solution.py:24
  583.4 21.7 %copy-start = (bf16[512,512]{1,0:T(8,128)(2,1)S(1)}, bf16[512,512]{1,0:T(8,128)(2,1)}, u32[]{:S(2)}) copy-start(bf16[512,512]{1,0:T(8,128)(2,1)} %param.7) | copy-start | bytes 1572868
  583.4 267.6 %all-reduce.2.cloned.1.call-start = ((), (), s32[]{:S(2)}) async-start(), calls=%async_computation.4 | async-start | bytes 10485760 | tf_op jit(solution)/shard_map/psum | solution.py:31
  610.7 128.0 %all-to-all-start = ((bf16[16,160,512]{2,1,0:T(8,128)(2,1)}), bf16[16,160,512]{2,1,0:T(8,128)(2,1)S(1)}, u32[]{:S(2)}, u32[]{:S(2)}) async-start(bf16[16,160,512]{2,1,0:T(8,128)(2,1)} %bitcast), calls=%async_computation.1 | async-start | bytes 5242880 | tf_op jit(solution)/shard_map/all_to_all | solution.py:38
Sparse Core Ops, SparseCore 0:
  10.7 432.7 all-gather.1
  583.5 17.2 reduce-scatter.1
  610.8 240.1 all-reduce.1
where the time goes:
time: 861 us; the launch traced here: 860 us
  waiting for transfers between devices  557 us (65%)
  matrix products  146 us (17%)
  blocking collectives  121 us (14%)
  between operations  13.8 us (2%)
  local copies, waits for them, and re-layouts  9.88 us (1%)
    all_gather x1, waiting for transfers between devices, shards(): lax.all_gather(weights, 'slab', axis=0, tiled=True).astype(jnp.float32)  435 us
    dot_general x1, matrix products, shards(): jnp.dot(lax.all_gather(weights, 'slab', axis=0, tiled=True).astype(jnp.fl...  140 us
    psum x1, blocking collectives, shards(): whole, whole_squares = lax.psum((product, squares), 'slab')  121 us
    psum x1, waiting for transfers between devices, shards(): whole, whole_squares = lax.psum((product, squares), 'slab')  104 us
    reduce_scatter x1, waiting for transfers between devices, shards(): lax.psum_scatter(partial_value, 'panel', scatter_dimension=0, tiled=True)  17.3 us
  transfers between devices with their start and end apart: 4, of which 3 were waited for; matrix products, arithmetic and copies ran while one was open for 1% of the time, Pallas kernels for 0%

commit v1 on v0

--- a/solution.py
+++ b/solution.py
@@ -1,8 +1,11 @@
+import functools
 import math
 
 import jax
 import jax.numpy as jnp
 from jax import lax
+from jax.experimental import pallas as pl
+from jax.experimental.pallas import tpu as pltpu
 from jax.sharding import PartitionSpec as P
 
 D = 8192
@@ -11,14 +14,12 @@
 EPS = 1e-05
 
 
-def shards(weights, gain, rotation, tokens):
+def general_shards(weights, gain, rotation, tokens):
     width_rows = rotation.shape[0]
     gain_block = lax.dynamic_slice_in_dim(gain, lax.axis_index("panel") * width_rows, width_rows, 0)
     partial_value = jnp.dot(
-        lax.all_gather(weights, "slab", axis=0, tiled=True).astype(jnp.float32)
-        * gain_block[None, :],
-        rotation,
-        precision=lax.Precision.HIGHEST,
+        lax.all_gather(weights, "slab", axis=0, tiled=True),
+        (rotation * gain_block[:, None]).astype(jnp.bfloat16),
         preferred_element_type=jnp.float32,
     )
     folded = lax.psum_scatter(partial_value, "panel", scatter_dimension=0, tiled=True)
@@ -39,10 +40,315 @@
     return (whole_rows[None], qkv)
 
 
+CHIPS = [(x, y, z) for z in range(4) for y in range(2) for x in range(2)]
+NEAR = [(dx, dy) for dy in range(2) for dx in range(2)]
+
+
+def slab_of(x, y, z):
+    return z * 4 + y * 2 + x
+
+
+def move(value, dx=0, dy=0, dz=0):
+    pairs = [(slab_of(x, y, z), slab_of(x ^ dx, y ^ dy, z ^ dz)) for x, y, z in CHIPS]
+    return lax.ppermute(value, "slab", pairs)
+
+
+def swap_cores(value):
+    return lax.ppermute(value, "panel", [(0, 1), (1, 0)])
+
+
+def send_rows(value, f, dx, dy):
+    pairs = []
+    for x, y, z in CHIPS:
+        for q in range(2):
+            target = slab_of(q, x ^ dx, 2 * (z % 2) + (y ^ dy)) * 2 + ((z // 2) ^ f)
+            pairs.append((slab_of(x, y, z) * 2 + q, target))
+    return lax.ppermute(value, ("slab", "panel"), pairs)
+
+
+def tie(values, *others):
+    return lax.optimization_barrier((values, others))[0]
+
+
+def fold_kernel(plan, turn_plan, n_chunks, given, *refs):
+    n_in = 1 + max(max(p[0] for p in plan), max(p[0] for turn in turn_plan for p in turn))
+    ins, before, refs = refs[:n_in], refs[n_in : n_in + given], refs[n_in + given :]
+    outs, (together, rows, held, sums, sems) = refs[:-5], refs[-5:]
+    n_rows, depth = rows.shape
+    width = held.shape[2]
+    size = n_rows // len(outs)
+    step = depth // n_chunks
+    copies, index = [], 0
+    for c in range(n_chunks):
+        group = []
+        for k, turn in enumerate(turn_plan):
+            for p, first, count, begin in turn:
+                low, high = max(begin, c * step), min(begin + count, (c + 1) * step)
+                if low < high:
+                    source = ins[p].at[pl.ds(first + low - begin, high - low)]
+                    group.append(pltpu.make_async_copy(source, held.at[k, pl.ds(low, high - low)], sems.at[index]))
+                    index += 1
+        for p, first, count, place in plan:
+            columns = pl.ds(c * step, step)
+            source = ins[p].at[pl.ds(first, count), columns]
+            group.append(pltpu.make_async_copy(source, rows.at[pl.ds(place, count), columns], sems.at[index]))
+            index += 1
+        copies.append(group)
+    shift = before[0].shape[1] if given else 0
+    for group in copies:
+        for copy in group:
+            copy.start()
+    for c, group in enumerate(copies):
+        for copy in group:
+            copy.wait()
+        if given and not c:
+            together[:, :shift] = before[0][...]
+            for i, out in enumerate(outs):
+                out[:, :shift] = before[0][i * size : (i + 1) * size]
+        for k in range(len(turn_plan)):
+            columns = slice(k * width, (k + 1) * width)
+            value = jnp.dot(
+                rows[:, c * step : (c + 1) * step],
+                held[k, c * step : (c + 1) * step],
+                preferred_element_type=jnp.float32,
+            )
+            if c:
+                value = value + sums[:, columns]
+            if c < n_chunks - 1:
+                sums[:, columns] = value
+            else:
+                value = value.astype(jnp.bfloat16)
+                columns = slice(shift + k * width, shift + (k + 1) * width)
+                together[:, columns] = value
+                for i, out in enumerate(outs):
+                    out[:, columns] = value[i * size : (i + 1) * size]
+
+
+def fold(blocks, turns, before=()):
+    arrays, plan, turn_plan, place = [], [], [], 0
+
+    def operand(value):
+        for i, other in enumerate(arrays):
+            if other is value:
+                return i
+        arrays.append(value)
+        return len(arrays) - 1
+
+    for block in blocks:
+        for value, first, count in block:
+            plan.append((operand(value), first, count, place))
+            place += count
+    for turn in turns:
+        begins = [sum(count for _, _, count in turn[:i]) for i in range(len(turn))]
+        turn_plan.append([(operand(v), first, count, begin) for (v, first, count), begin in zip(turn, begins)])
+    depth, width = blocks[0][0][0].shape[1], turns[0][0][0].shape[1]
+    n, t, n_chunks = len(blocks), len(turns), 8
+    all_width = t * width + sum(value.shape[1] for value in before)
+    n_copies = n_chunks * (len(plan) + 2 * sum(len(turn) for turn in turn_plan))
+    out = pl.pallas_call(
+        functools.partial(fold_kernel, plan, turn_plan, n_chunks, len(before)),
+        out_shape=[jax.ShapeDtypeStruct((place // n, all_width), jnp.bfloat16)] * n
+        + [jax.ShapeDtypeStruct((place, all_width), jnp.bfloat16)],
+        in_specs=[pl.BlockSpec(memory_space=pltpu.HBM)] * len(arrays)
+        + [pl.BlockSpec(memory_space=pltpu.VMEM)] * len(before),
+        out_specs=[pl.BlockSpec(memory_space=pltpu.VMEM)] * (n + 1),
+        scratch_shapes=[
+            pltpu.VMEM((place, depth), jnp.bfloat16),
+            pltpu.VMEM((t, depth, width), jnp.bfloat16),
+            pltpu.VMEM((place, t * width), jnp.float32),
+            pltpu.SemaphoreType.DMA((n_copies,)),
+        ],
+        compiler_params=pltpu.CompilerParams(vmem_limit_bytes=60 * 1024 * 1024),
+        cost_estimate=pl.CostEstimate(flops=1024, bytes_accessed=1024, transcendentals=0),
+    )(*arrays, *before)
+    return out[:-1], out[-1]
+
+
+def place_kernel(plan, width, *refs):
+    ins, out, sems = refs[:-2], refs[-2], refs[-1]
+    slab, core = lax.axis_index("slab"), lax.axis_index("panel")
+    x, y, z = slab % 2, (slab // 2) % 2, slab // 4
+    copies = []
+    for ref, (f, dx, dy) in zip(ins, plan):
+        for j in range(2):
+            z_source = (core + f) % 2 * 2 + (z // 2 + j) % 2
+            source = z_source * 4 + (z + dy) % 2 * 2 + (y + dx) % 2
+            target = out.at[:, pl.ds(pl.multiple_of(source * width, width), width)]
+            copies.append(pltpu.make_async_copy(ref.at[:, pl.ds(j * width, width)], target, sems.at[len(copies)]))
+    for copy in copies:
+        copy.start()
+    for copy in copies:
+        copy.wait()
+
+
+def whole_rows(pieces, width):
+    plan = [key for key, _ in pieces]
+    return pl.pallas_call(
+        functools.partial(place_kernel, plan, width),
+        out_shape=jax.ShapeDtypeStruct((pieces[0][1].shape[0], D), jnp.bfloat16),
+        in_specs=[pl.BlockSpec(memory_space=pl.ANY)] * len(pieces),
+        out_specs=pl.BlockSpec(memory_space=pltpu.VMEM),
+        scratch_shapes=[pltpu.SemaphoreType.DMA((2 * len(plan),))],
+        cost_estimate=pl.CostEstimate(flops=1024, bytes_accessed=1024, transcendentals=0),
+    )(*[value for _, value in pieces])
+
+
+def shards(weights, gain, rotation, tokens):
+    slab, core = lax.axis_index("slab"), lax.axis_index("panel")
+    x, y, z = slab % 2, (slab // 2) % 2, slab // 4
+    z_hi, z_lo = z // 2, z % 2
+    depth, width = rotation.shape
+    half = weights.shape[0] // 2
+    low = half // 2
+    n_tokens = tokens.shape[0]
+    own_count = n_tokens // 16
+
+    def split(value, axis, bit):
+        size = value.shape[axis] // 2
+        return [lax.dynamic_slice_in_dim(value, b * size, size, axis) for b in (bit, 1 - bit)]
+
+    mine, others = split(weights, 0, core)
+    rows = jnp.concatenate([mine, swap_cores(others)], axis=1)
+
+    ordered = tokens.reshape(2, 2, 2, 2, own_count, width).transpose(3, 2, 0, 1, 4, 5).reshape(n_tokens, width)
+    part = split(ordered, 0, core)[0]
+
+    gain_block = lax.dynamic_slice_in_dim(gain, core * depth, depth, 0)
+    turn = (rotation * gain_block[:, None]).astype(jnp.bfloat16)
+    cuts = [0, 3 * depth // 16, depth // 2, depth]
+    pieces = [turn[i:j] for i, j in zip(cuts, cuts[1:])]
+
+    def spread(values, f):
+        return [send_rows(value, f, *key) for value, key in zip(values, NEAR)]
+
+    def check(exported):
+        return lax.dot_general(exported, checks, (((1,), (1,)), ((), ())), preferred_element_type=jnp.float32)
+
+    def three_terms(values):
+        terms = []
+        for _ in range(3):
+            terms.append(values.astype(jnp.bfloat16).astype(jnp.float32))
+            values = values - terms[-1]
+        return jnp.concatenate([jnp.stack(terms), jnp.zeros((13, values.shape[0]), jnp.float32)])
+
+    def quarter(value, dx, dy):
+        size = n_tokens // 4
+        return lax.dynamic_slice_in_dim(value, ((x ^ dx) * 2 + (y ^ dy)) * size, size, 1)
+
+    def plane(values):
+        got = {}
+        for d in NEAR:
+            value = [quarter(v, *d) for v in values]
+            got[d] = move(jnp.concatenate([v.astype(jnp.bfloat16) for v in value]), *d) if any(d) else value
+        return got
+
+    def total(sums):
+        value = sums[0].reshape(2, 2, half, -1)
+        for (dx, dy), blocks in zip(NEAR[1:], sums[1:]):
+            blocks = blocks.astype(jnp.float32).reshape(2, 2, half, -1)
+            blocks = blocks[::-1] if dy else blocks
+            value = value + (blocks[:, ::-1] if dx else blocks)
+        return value.reshape(4 * half, -1)
+
+    near_x, near_y, far_low, piece_a, turn_swapped = tie(
+        (
+            move(rows, dx=1),
+            move(rows, dy=1),
+            move(rows[:low], dz=2),
+            move(jnp.concatenate([pieces[0], part]), dz=1),
+            swap_cores(turn),
+        )
+    )
+    by_x, by_y, far_high, piece_b, swapped_a = tie(
+        (
+            move(jnp.concatenate([near_y[low:], far_low]), dx=1),
+            move(jnp.concatenate([near_x[:low], far_low]), dy=1),
+            move(rows[low:], dz=2),
+            move(pieces[1], dz=1),
+            swap_cores(piece_a),
+        )
+    )
+    first = pieces[0].shape[0]
+    part, swapped = piece_a[first:], swapped_a[first:]
+    ordered_other = jnp.concatenate([jnp.where(core == 0, part, swapped), jnp.where(core == 0, swapped, part)])
+    checks = jnp.concatenate([ordered, ordered_other], axis=1)
+    widened = checks.astype(jnp.float32)
+    squares = jnp.sum(widened * widened, axis=1)
+    terms = three_terms(squares)
+    cut = 3 * low // 5
+    own_turn = [(turn, 0, depth), (turn_swapped, 0, depth)]
+    near = [
+        [(rows, 0, half)],
+        [(near_x, 0, half)],
+        [(near_y, 0, half)],
+        [(by_y, 0, low), (by_x, 0, low)],
+    ]
+    by_x3, by_y3, piece_c, swapped_b, near_own, checks, terms = tie(
+        (
+            move(jnp.concatenate([far_high, by_y[low + cut :]]), dx=1),
+            move(jnp.concatenate([far_high, by_x[low : low + cut]]), dy=1),
+            move(pieces[2], dz=1),
+            swap_cores(piece_b),
+            fold(near, [own_turn]),
+            checks,
+            terms,
+        )
+    )
+    swapped_c = swap_cores(piece_c)
+    arrived = [piece_a, piece_b, piece_c, swapped_a, swapped_b, swapped_c]
+    turn_other = [(v, 0, p.shape[0]) for v, p in zip(arrived, pieces + pieces)]
+    by_y4, by_x4, near_rows = tie(
+        (
+            move(by_x3[: low - cut], dy=1),
+            move(by_y3[low - cut : low], dx=1),
+            fold(near, [turn_other], [near_own[1]]),
+        )
+    )
+    far = [
+        [(far_low, 0, low), (far_high, 0, low)],
+        [(by_x, low, low), (by_x3, 0, low)],
+        [(by_y, low, low), (by_y3, 0, low)],
+        [(by_y3, low, cut), (by_x3, low, low - cut), (by_y4, 0, low - cut), (by_x4, 0, cut)],
+    ]
+    received_near, far_rows = tie((spread(near_rows[0], 0), fold(far, [own_turn, turn_other])))
+    sums = plane([check(near_rows[1]), check(far_rows[1]), terms])
+    received_far, sums = tie((spread(far_rows[0], 1), sums))
+    placed = [((f,) + d, v) for f, values in enumerate((received_near, received_far)) for d, v in zip(NEAR, values)]
+    served = whole_rows(placed, width)
+
+    rows_near, rows_far, own_squares = sums[0, 0]
+    kept = [rows_near, rows_far]
+    for f in range(2):
+        kept[f] = total([kept[f]] + [sums[d][4 * half * f : 4 * half * (f + 1)] for d in NEAR[1:]])
+    own_squares = own_squares + sum(sums[d][8 * half :].astype(jnp.float32) for d in NEAR[1:])
+    own_squares = jnp.sum(own_squares, axis=0)
+    near_keep, near_give = split(kept[0], 1, z_hi)
+    far_keep, far_give = split(kept[1], 1, z_hi)
+    keep_squares, give_squares = split(own_squares, 0, z_hi)
+    given = jnp.concatenate([near_give, far_give, three_terms(give_squares)]).astype(jnp.bfloat16)
+    got = move(given, dz=2).astype(jnp.float32)
+    own_scale = lax.rsqrt((keep_squares + jnp.sum(got[8 * half :], axis=0)) / D + EPS)
+    shape = (2, 2, half, 2 * own_count)
+    near_keep = (near_keep + got[4 * half : 8 * half]).reshape(shape)
+    far_keep = (far_keep + got[: 4 * half]).reshape(shape)
+    result = (jnp.stack([near_keep, far_keep]) * own_scale / math.sqrt(D)).astype(jnp.bfloat16)
+    keep = lax.dynamic_index_in_dim(result, z_hi ^ core, 0, keepdims=False)
+    got = swap_cores(lax.dynamic_index_in_dim(result, z_hi ^ 1 ^ core, 0, keepdims=False))
+    both = jnp.stack([keep, got], axis=2)
+    keep = lax.dynamic_slice_in_dim(both, z_lo * own_count, own_count, 4)
+    got = move(lax.dynamic_slice_in_dim(both, (1 - z_lo) * own_count, own_count, 4), dz=1)
+    whole = jnp.stack([keep, got]).reshape(16, half, own_count)
+    flip = ((z_lo * 2 + y) * 2 + x) * 2 + core
+    whole = jnp.take(whole, jnp.arange(16) ^ flip, axis=0)
+    qkv = whole.reshape(16 * half, own_count).T
+    return (served[None], qkv)
+
+
 def solution(mesh):
     placed = (P("slab", "panel"), P(), P("panel", "slab"), P(None, "slab"))
+    small = mesh.shape["slab"] == 16 and mesh.shape["panel"] == 2
     return jax.shard_map(
-        shards,
+        shards if small else general_shards,
         mesh=mesh,
         in_specs=placed,
         out_specs=(P("panel", "slab", None), P("slab", "panel")),

time: 861 us -> 320 us (0.37)
  waiting for transfers between devices: 557 us -> 176 us
  matrix products: 146 us -> 3.17 us
  blocking collectives: 121 us -> 0 us
  starting transfers between devices: 6.98 us -> 50.1 us
  Pallas kernels: 0 us -> 41.5 us
  local copies, waits for them, and re-layouts: 9.88 us -> 25.9 us
  other arithmetic: 6.29 us -> 21.9 us
  between operations: 13.8 us -> 1.26 us
    all_gather x1 -> x0, waiting for transfers between devices: 435 us -> none  [shards(): lax.all_gather(weights, 'slab', axis=0, tiled=True).astype(jnp.float32)]
    ppermute x0 -> x32, waiting for transfers between devices: none -> 176 us  [the longest x18 150 us: move(): return lax.ppermute(value, 'slab', pairs)]
    dot_general x2, matrix products: 146 us -> 3.17 us  [check(): lax.dot_general(exported, checks, (((1,), (1,)), ((), ())), preferred_ele...]
    psum x1 -> x0, blocking collectives: 121 us -> none  [shards(): whole, whole_squares = lax.psum((product, squares), 'slab')]
    psum x1 -> x0, waiting for transfers between devices: 104 us -> none  [shards(): whole, whole_squares = lax.psum((product, squares), 'slab')]
    ppermute x0 -> x32, starting transfers between devices: none -> 50.1 us  [the longest x8 24.9 us: send_rows(): return lax.ppermute(value, ('slab', 'panel'), pairs)]
    pallas_call x0 -> x4, Pallas kernels: none -> 41.5 us  [the longest x3 38.1 us: fold(): pl.pallas_call(functools.partial(fold_kernel, plan, turn_plan, n_chunks,...]
    reduce_scatter x1 -> x0, waiting for transfers between devices: 17.3 us -> none  [shards(): lax.psum_scatter(partial_value, 'panel', scatter_dimension=0, tiled=True)]
  transfers between devices with their start and end apart: 4 -> 32, of which waited for: 3 -> 15; matrix products, arithmetic and copies ran while one was open for 1% -> 9% of each run, Pallas kernels for 0% -> 13%
where the time goes in v1:
time: 320 us; the launch traced here: 319 us
  waiting for transfers between devices  176 us (55%)
  starting transfers between devices  50.1 us (16%)
  Pallas kernels  41.5 us (13%)
  local copies, waits for them, and re-layouts  25.9 us (8%)
  other arithmetic  21.9 us (7%)
    ppermute x18, waiting for transfers between devices, move(): return lax.ppermute(value, 'slab', pairs)  150 us
    pallas_call x3, Pallas kernels, fold(): pl.pallas_call(functools.partial(fold_kernel, plan, turn_plan, n_chunks,...  38.1 us
    ppermute x8, starting transfers between devices, send_rows(): return lax.ppermute(value, ('slab', 'panel'), pairs)  24.9 us
    ppermute x18, starting transfers between devices, move(): return lax.ppermute(value, 'slab', pairs)  24.5 us
    ppermute x8, waiting for transfers between devices, send_rows(): return lax.ppermute(value, ('slab', 'panel'), pairs)  24.2 us
    slice x3, local copies, waits for them, and re-layouts, shards(): pieces = [turn[i:j] for i, j in zip(cuts, cuts[1:])]  6.51 us
  transfers between devices with their start and end apart: 32, of which 15 were waited for; matrix products, arithmetic and copies ran while one was open for 9% of the time, Pallas kernels for 13%

profile of v1, /device:TPU:0, one launch (start us, length us, event | category | flops | bytes accessed | tf_op | source)
XLA Modules:
  0.0 319.4 jit_solution(18397491105488475542)
XLA Ops:
  0.6 3.0 constant_dynamic-slice_fusion.7
  4.1 5.3 %multiply_convert_fusion.refs_5_.refs_8_ = bf16[4096,512]{1,0:T(8,128)(2,1)} fusion(f32[4096,512]{1,0:T(8,128)} %param.6, f32[4096]{0:T(1024)S(1)} %dynamic_slice.81), kind=kLoop, calls=%fused_computation.1 | loop fusion | flops 4194304 | bytes 12599296 | tf_op jit(solution)/shard_map/convert_element_type | solution.py:217
  10.5 1.6 pad_maximum_fusion.refs_0_
  12.1 3.0 collective-permute-start.1
  15.1 1.5 collective-permute-start.2
  16.6 1.7 fusion.1
  18.4 2.6 collective-permute-start.3
  21.0 2.1 slice.104
  24.2 1.4 pad_maximum_fusion.5
  25.5 1.6 collective-permute-start.4
  27.2 44.2 %collective-permute-done.4.refs_5_.refs_10_ = bf16[1024,512]{1,0:T(8,128)(2,1)S(1)} collective-permute-done((bf16[1024,512]{1,0:T(8,128)(2,1)S(1)}, bf16[1024,512]{1,0:T(8,128)(2,1)S(1)}, u32[]{:S(2)}, u32[]{:S(2)}) %collective-permute-start.4) | collective-permute-done | bytes 1048608 | tf_op jit(solution)/shard_map/ppermute | solution.py:53
  71.3 6.5 %collective-permute-done.3.refs_0_ = bf16[80,8192]{1,0:T(8,128)(2,1)} collective-permute-done((bf16[80,8192]{1,0:T(8,128)(2,1)}, bf16[80,8192]{1,0:T(8,128)(2,1)}, u32[]{:S(2)}, u32[]{:S(2)}) %collective-permute-start.3) | collective-permute-done | bytes 1310752 | tf_op jit(solution)/shard_map/ppermute | solution.py:53
  77.8 1.4 slice.77
  79.2 1.4 slice.78
  80.7 1.9 pad_maximum_fusion.1
  83.8 1.4 slice.107
  85.9 3.4 %collective-permute-start.8 = (bf16[80,8192]{1,0:T(8,128)(2,1)S(1)}, bf16[80,8192]{1,0:T(8,128)(2,1)S(1)}, u32[]{:S(2)}, u32[]{:S(2)}) collective-permute-start(bf16[80,8192]{1,0:T(8,128)(2,1)S(1)} %copy-done.14), channel_id=1, source_target_pairs={{0,16},{2,18},{4,20},{6,22},{8,24},{10,26},{12,28},{14,30},{16,0},... | collective-permute-start | bytes 3932168 | tf_op jit(solution)/shard_map/ppermute | solution.py:53
  89.3 3.0 slice.108
  92.4 49.9 %collective-permute-done.9.refs_6_.refs_11_ = bf16[1280,512]{1,0:T(8,128)(2,1)S(1)} collective-permute-done((bf16[1280,512]{1,0:T(8,128)(2,1)S(1)}, bf16[1280,512]{1,0:T(8,128)(2,1)S(1)}, u32[]{:S(2)}, u32[]{:S(2)}) %collective-permute-start.9) | collective-permute-done | bytes 1310752 | tf_op jit(solution)/shard_map/ppermute | solution.py:53
  142.3 3.4 %collective-permute-done.8.refs_1_ = bf16[80,8192]{1,0:T(8,128)(2,1)S(1)} collective-permute-done((bf16[80,8192]{1,0:T(8,128)(2,1)S(1)}, bf16[80,8192]{1,0:T(8,128)(2,1)S(1)}, u32[]{:S(2)}, u32[]{:S(2)}) %collective-permute-start.8) | collective-permute-done | bytes 1310752 | tf_op jit(solution)/shard_map/ppermute | solution.py:53
  146.7 2.1 pad_maximum_fusion.3
  148.9 1.5 collective-permute-start.12
  150.4 1.4 pad_maximum_fusion.4
  151.7 1.5 collective-permute-start.11
  153.3 9.2 %shard_map.59 = (bf16[160,512]{1,0:T(8,128)(2,1)}, bf16[160,512]{1,0:T(8,128)(2,1)}, bf16[160,512]{1,0:T(8,128)(2,1)}, bf16[160,512]{1,0:T(8,128)(2,1)}, bf16[640,512]{1,0:T(8,128)(2,1)}) custom-call(bf16[160,8192]{1,0:T(8,128)(2,1)} %copy-done.2, bf16[160,8192]{1,0:T(8,128)(2,1)} %collective-permute-done.1.refs_1_, ...), custom_call_target="tpu_custom_call" | custom-call | flops 1024 | bytes 1024 | tf_op jit(solution)/shard_map/pallas_call | solution.py:148
  164.9 23.0 %collective-permute-done.13.refs_7_.refs_12_ = bf16[2048,512]{1,0:T(8,128)(2,1)} collective-permute-done((bf16[2048,512]{1,0:T(8,128)(2,1)}, bf16[2048,512]{1,0:T(8,128)(2,1)}, u32[]{:S(2)}, u32[]{:S(2)}) %collective-permute-start.13) | collective-permute-done | bytes 2097184 | tf_op jit(solution)/shard_map/ppermute | solution.py:53
  188.3 3.0 collective-permute-done.12.refs_5_
  192.5 1.5 collective-permute-start.16
  195.1 1.6 collective-permute-start.15
  196.7 1.4 copy-done.5
  198.0 11.3 %shard_map.60 = (bf16[160,1024]{1,0:T(8,128)(2,1)}, bf16[160,1024]{1,0:T(8,128)(2,1)}, bf16[160,1024]{1,0:T(8,128)(2,1)}, bf16[160,1024]{1,0:T(8,128)(2,1)}, bf16[640,1024]{1,0:T(8,128)(2,1)}) custom-call(bf16[160,8192]{1,0:T(8,128)(2,1)} %copy-done.2, bf16[160,8192]{1,0:T(8,128)(2,1)} %collective-permute-done.1.refs_1_, ...), custom_call_target="tpu_custom_call" | custom-call | flops 1024 | bytes 1024 | tf_op jit(solution)/shard_map/pallas_call | solution.py:148
  209.4 3.3 %collective-permute-done.16.refs_7_ = bf16[48,8192]{1,0:T(8,128)(2,1)} collective-permute-done((bf16[48,8192]{1,0:T(8,128)(2,1)S(1)}, bf16[48,8192]{1,0:T(8,128)(2,1)}, u32[]{:S(2)}, u32[]{:S(2)}) %collective-permute-start.16) | collective-permute-done | bytes 786464 | tf_op jit(solution)/shard_map/ppermute | solution.py:53
  212.6 1.6 collective-permute-start.18
  214.2 6.2 %collective-permute-start.19 = (bf16[160,1024]{1,0:T(8,128)(2,1)}, bf16[160,1024]{1,0:T(8,128)(2,1)S(1)}, u32[]{:S(2)}, u32[]{:S(2)}) collective-permute-start(bf16[160,1024]{1,0:T(8,128)(2,1)} %get-tuple-element.78), channel_id=1, source_target_pairs={{0,4},{1,6},{2,0},{3,2},{4,12},{5,14},{6,8},{7,10},{8,20},{9,22},{... | collective-permute-start | bytes 983048 | tf_op jit(solution)/shard_map/ppermute | solution.py:66
  221.3 5.7 %collective-permute-start.21 = (bf16[160,1024]{1,0:T(8,128)(2,1)}, bf16[160,1024]{1,0:T(8,128)(2,1)S(1)}, u32[]{:S(2)}, u32[]{:S(2)}) collective-permute-start(bf16[160,1024]{1,0:T(8,128)(2,1)} %get-tuple-element.80), channel_id=1, source_target_pairs={{0,12},{1,14},{2,8},{3,10},{4,4},{5,6},{6,0},{7,2},{8,28},{9,30},{... | collective-permute-start | bytes 983048 | tf_op jit(solution)/shard_map/ppermute | solution.py:66
  227.0 17.6 %shard_map.61 = (bf16[160,1024]{1,0:T(8,128)(2,1)}, bf16[160,1024]{1,0:T(8,128)(2,1)}, bf16[160,1024]{1,0:T(8,128)(2,1)}, bf16[160,1024]{1,0:T(8,128)(2,1)}, bf16[640,1024]{1,0:T(8,128)(2,1)}) custom-call(bf16[80,8192]{1,0:T(8,128)(2,1)} %collective-permute-done.3.refs_0_, bf16[80,8192]{1,0:T(8,128)(2,1)} %copy-done.4, bf16[160,8192]{1,0:T(8,128)(2,1)} %copy-done, ...), custom_call_target="tpu_custom_call" | custom-call | flops 1024 | bytes 1024 | tf_op jit(solution)/shard_map/pallas_call | solution.py:148
  244.6 2.3 fusion.12
  249.9 3.6 %collective-permute-start.22 = (bf16[160,1024]{1,0:T(8,128)(2,1)S(1)}, bf16[160,1024]{1,0:T(8,128)(2,1)}, u32[]{:S(2)}, u32[]{:S(2)}) collective-permute-start(bf16[160,1024]{1,0:T(8,128)(2,1)S(1)} %copy-done.23), channel_id=1, source_target_pairs={{0,1},{1,3},{2,5},{3,7},{4,9},{5,11},{6,13},{7,15},{8,17},{9,19},{... | collective-permute-start | bytes 983048 | tf_op jit(solution)/shard_map/ppermute | solution.py:66
  253.5 3.4 %collective-permute-start.23 = (bf16[160,1024]{1,0:T(8,128)(2,1)S(1)}, bf16[160,1024]{1,0:T(8,128)(2,1)}, u32[]{:S(2)}, u32[]{:S(2)}) collective-permute-start(bf16[160,1024]{1,0:T(8,128)(2,1)S(1)} %copy-done.22), channel_id=1, source_target_pairs={{0,5},{1,7},{2,1},{3,3},{4,13},{5,15},{6,9},{7,11},{8,21},{9,23},{... | collective-permute-start | bytes 983048 | tf_op jit(solution)/shard_map/ppermute | solution.py:66
  259.6 3.0 collective-permute-done.22.refs_4_
  262.7 3.5 %collective-permute-start.24 = (bf16[160,1024]{1,0:T(8,128)(2,1)}, bf16[160,1024]{1,0:T(8,128)(2,1)}, u32[]{:S(2)}, u32[]{:S(2)}) collective-permute-start(bf16[160,1024]{1,0:T(8,128)(2,1)} %get-tuple-element.94), channel_id=1, source_target_pairs={{0,9},{1,11},{2,13},{3,15},{4,1},{5,3},{6,5},{7,7},{8,25},{9,27},{... | collective-permute-start | bytes 983048 | tf_op jit(solution)/shard_map/ppermute | solution.py:66
  266.2 8.3 %collective-permute-done.23.refs_5_ = bf16[160,1024]{1,0:T(8,128)(2,1)} collective-permute-done((bf16[160,1024]{1,0:T(8,128)(2,1)S(1)}, bf16[160,1024]{1,0:T(8,128)(2,1)}, u32[]{:S(2)}, u32[]{:S(2)}) %collective-permute-start.23) | collective-permute-done | bytes 327712 | tf_op jit(solution)/shard_map/ppermute | solution.py:66
  274.7 3.2 %collective-permute-done.24.refs_6_ = bf16[160,1024]{1,0:T(8,128)(2,1)} collective-permute-done((bf16[160,1024]{1,0:T(8,128)(2,1)}, bf16[160,1024]{1,0:T(8,128)(2,1)}, u32[]{:S(2)}, u32[]{:S(2)}) %collective-permute-start.24) | collective-permute-done | bytes 327712 | tf_op jit(solution)/shard_map/ppermute | solution.py:66
  277.9 9.6 %collective-permute-done.25.refs_7_ = bf16[160,1024]{1,0:T(8,128)(2,1)} collective-permute-done((bf16[160,1024]{1,0:T(8,128)(2,1)}, bf16[160,1024]{1,0:T(8,128)(2,1)}, u32[]{:S(2)}, u32[]{:S(2)}) %collective-permute-start.25) | collective-permute-done | bytes 327712 | tf_op jit(solution)/shard_map/ppermute | solution.py:66
  291.4 3.1 collective-permute-start.29
  294.6 14.4 %collective-permute-done.29 = bf16[1296,64]{1,0:T(8,128)(2,1)S(1)} collective-permute-done((bf16[1296,64]{1,0:T(8,128)(2,1)S(1)}, bf16[1296,64]{1,0:T(8,128)(2,1)S(1)}, u32[]{:S(2)}, u32[]{:S(2)}) %collective-permute-start.29) | collective-permute-done | bytes 165920 | tf_op jit(solution)/shard_map/ppermute | solution.py:53
  312.0 3.5 %shard_map.62 = bf16[160,8192]{1,0:T(8,128)(2,1)} custom-call(bf16[160,1024]{1,0:T(8,128)(2,1)} %copy-done.16, bf16[160,1024]{1,0:T(8,128)(2,1)} %copy-done.17, bf16[160,1024]{1,0:T(8,128)(2,1)} %copy-done.18, bf16[160,1024]{1,0:T(8,128)(2,1)} %copy-done.19, bf16[160,1024]{1,0:T(8,128)(2,1)} %collective-permute-done.22.refs_4_, ...), custom_call_target="tpu_custom_call" | custom-call | flops 1024 | bytes 1024 | tf_op jit(solution)/shard_map/pallas_call | solution.py:186
  315.5 2.0 collective-permute-done.31
  (142 shorter events, 26.0 us)
Async XLA Ops:
  0.6 3.5 %copy-start.20 = (f32[8192]{0:T(1024)S(1)}, f32[8192]{0:T(1024)}, u32[]{:S(2)}) copy-start(f32[8192]{0:T(1024)} %param.5) | copy-start | bytes 98308
  3.7 5.8 %collective-permute-start = (bf16[160,4096]{1,0:T(8,128)(2,1)S(1)}, bf16[160,4096]{1,0:T(8,128)(2,1)S(1)}, u32[]{:S(2)}, u32[]{:S(2)}) collective-permute-start(bf16[160,4096]{1,0:T(8,128)(2,1)S(1)} %get-tuple-element.115), channel_id=1, source_target_pairs={{0,1},{1,0},{2,3},{3,2},{4,5},{5,4},{6,7},{7,6},{8,9},{9,8},{10,11... | collective-permute-start | bytes 3932168 | tf_op jit(solution)/shard_map/ppermute | solution.py:57
  4.1 6.4 %copy-start.3 = (bf16[160,4096]{1,0:T(8,128)(2,1)S(1)}, bf16[160,4096]{1,0:T(8,128)(2,1)}, u32[]{:S(2)}) copy-start(bf16[160,4096]{1,0:T(8,128)(2,1)} %get-tuple-element.114) | copy-start | bytes 3932164
  9.4 68.5 %collective-permute-start.5 = (bf16[4096,512]{1,0:T(8,128)(2,1)}, bf16[4096,512]{1,0:T(8,128)(2,1)}, u32[]{:S(2)}, u32[]{:S(2)}) collective-permute-start(bf16[4096,512]{1,0:T(8,128)(2,1)} %multiply_convert_fusion.refs_5_.refs_8_), channel_id=1, source_target_pairs={{0,1},{1,0},{2,3},{3,2},{4,5},{5,4},{6,7},{7,6},{8,9},{9,8},{10,11... | collective-permute-start | bytes 12582920 | tf_op jit(solution)/shard_map/ppermute | solution.py:57
  10.5 6.1 %copy-start.9 = (bf16[160,4096]{1,0:T(8,128)(2,1)S(1)}, bf16[160,4096]{1,0:T(8,128)(2,1)}, u32[]{:S(2)}) copy-start(bf16[160,4096]{1,0:T(8,128)(2,1)} %copy-done.8) | copy-start | bytes 3932164
  12.1 6.3 %copy-start.2 = (bf16[160,8192]{1,0:T(8,128)(2,1)}, bf16[160,8192]{1,0:T(8,128)(2,1)S(1)}, u32[]{:S(2)}) copy-start(bf16[160,8192]{1,0:T(8,128)(2,1)S(1)} %pad_maximum_fusion.refs_0_) | copy-start | bytes 7864324
  12.1 65.7 %collective-permute-start.1 = (bf16[160,8192]{1,0:T(8,128)(2,1)S(1)}, bf16[160,8192]{1,0:T(8,128)(2,1)}, u32[]{:S(2)}, u32[]{:S(2)}) collective-permute-start(bf16[160,8192]{1,0:T(8,128)(2,1)S(1)} %pad_maximum_fusion.refs_0_), channel_id=1, source_target_pairs={{0,2},{2,0},{4,6},{6,4},{8,10},{10,8},{12,14},{14,12},{16,18},{18,... | collective-permute-start | bytes 7864328 | tf_op jit(solution)/shard_map/ppermute | solution.py:53
  15.1 62.7 %collective-permute-start.2 = (bf16[160,8192]{1,0:T(8,128)(2,1)S(1)}, bf16[160,8192]{1,0:T(8,128)(2,1)}, u32[]{:S(2)}, u32[]{:S(2)}) collective-permute-start(bf16[160,8192]{1,0:T(8,128)(2,1)S(1)} %pad_maximum_fusion.refs_0_), channel_id=1, source_target_pairs={{0,4},{2,6},{4,0},{6,2},{8,12},{10,14},{12,8},{14,10},{16,20},{18,... | collective-permute-start | bytes 7864328 | tf_op jit(solution)/shard_map/ppermute | solution.py:53
  18.4 59.4 %collective-permute-start.3 = (bf16[80,8192]{1,0:T(8,128)(2,1)}, bf16[80,8192]{1,0:T(8,128)(2,1)}, u32[]{:S(2)}, u32[]{:S(2)}) collective-permute-start(bf16[80,8192]{1,0:T(8,128)(2,1)} %get-tuple-element.113), channel_id=1, source_target_pairs={{0,16},{2,18},{4,20},{6,22},{8,24},{10,26},{12,28},{14,30},{16,0},... | collective-permute-start | bytes 3932168 | tf_op jit(solution)/shard_map/ppermute | solution.py:53
  24.1 55.1 %copy-start.12 = (bf16[2,2,2,2,32,512]{5,4,1,0,2,3:T(8,128)(2,1)}, bf16[2,2,2,2,32,512]{5,4,1,0,2,3:T(8,128)(2,1)S(1)}, u32[]{:S(2)}) copy-start(bf16[2,2,2,2,32,512]{5,4,1,0,2,3:T(8,128)(2,1)S(1)} %copy.15) | copy-start | bytes 1572868
  25.5 45.8 %collective-permute-start.4 = (bf16[1024,512]{1,0:T(8,128)(2,1)S(1)}, bf16[1024,512]{1,0:T(8,128)(2,1)S(1)}, u32[]{:S(2)}, u32[]{:S(2)}) collective-permute-start(bf16[1024,512]{1,0:T(8,128)(2,1)S(1)} %pad_maximum_fusion.5), channel_id=1, source_target_pairs={{0,8},{2,10},{4,12},{6,14},{8,0},{10,2},{12,4},{14,6},{16,24},{18,... | collective-permute-start | bytes 3145736 | tf_op jit(solution)/shard_map/ppermute | solution.py:53
  71.3 18.0 %copy-start.6 = (bf16[1024,512]{1,0:T(8,128)(2,1)}, bf16[1024,512]{1,0:T(8,128)(2,1)S(1)}, u32[]{:S(2)}) copy-start(bf16[1024,512]{1,0:T(8,128)(2,1)S(1)} %collective-permute-done.4.refs_5_.refs_10_) | copy-start | bytes 3145732
  82.6 3.3 %copy-start.14 = (bf16[80,8192]{1,0:T(8,128)(2,1)S(1)}, bf16[80,8192]{1,0:T(8,128)(2,1)}, u32[]{:S(2)}) copy-start(bf16[80,8192]{1,0:T(8,128)(2,1)} %get-tuple-element.112) | copy-start | bytes 3932164
  82.6 63.1 %collective-permute-start.6 = (bf16[160,8192]{1,0:T(8,128)(2,1)S(1)}, bf16[160,8192]{1,0:T(8,128)(2,1)S(1)}, u32[]{:S(2)}, u32[]{:S(2)}) collective-permute-start(bf16[160,8192]{1,0:T(8,128)(2,1)S(1)} %get-tuple-element.125), channel_id=1, source_target_pairs={{0,2},{2,0},{4,6},{6,4},{8,10},{10,8},{12,14},{14,12},{16,18},{18,... | collective-permute-start | bytes 7864328 | tf_op jit(solution)/shard_map/ppermute | solution.py:53
  83.2 62.5 %collective-permute-start.7 = (bf16[160,8192]{1,0:T(8,128)(2,1)S(1)}, bf16[160,8192]{1,0:T(8,128)(2,1)S(1)}, u32[]{:S(2)}, u32[]{:S(2)}) collective-permute-start(bf16[160,8192]{1,0:T(8,128)(2,1)S(1)} %get-tuple-element.124), channel_id=1, source_target_pairs={{0,4},{2,6},{4,0},{6,2},{8,12},{10,14},{12,8},{14,10},{16,20},{18,... | collective-permute-start | bytes 7864328 | tf_op jit(solution)/shard_map/ppermute | solution.py:53
  85.2 57.0 %collective-permute-start.9 = (bf16[1280,512]{1,0:T(8,128)(2,1)S(1)}, bf16[1280,512]{1,0:T(8,128)(2,1)S(1)}, u32[]{:S(2)}, u32[]{:S(2)}) collective-permute-start(bf16[1280,512]{1,0:T(8,128)(2,1)S(1)} %slice.107), channel_id=1, source_target_pairs={{0,8},{2,10},{4,12},{6,14},{8,0},{10,2},{12,4},{14,6},{16,24},{18,... | collective-permute-start | bytes 3932168 | tf_op jit(solution)/shard_map/ppermute | solution.py:53
  85.9 59.7 %collective-permute-start.8 = (bf16[80,8192]{1,0:T(8,128)(2,1)S(1)}, bf16[80,8192]{1,0:T(8,128)(2,1)S(1)}, u32[]{:S(2)}, u32[]{:S(2)}) collective-permute-start(bf16[80,8192]{1,0:T(8,128)(2,1)S(1)} %copy-done.14), channel_id=1, source_target_pairs={{0,16},{2,18},{4,20},{6,22},{8,24},{10,26},{12,28},{14,30},{16,0},... | collective-permute-start | bytes 3932168 | tf_op jit(solution)/shard_map/ppermute | solution.py:53
  89.3 56.4 %collective-permute-start.10 = (bf16[1024,512]{1,0:T(8,128)(2,1)S(1)}, bf16[1024,512]{1,0:T(8,128)(2,1)S(1)}, u32[]{:S(2)}, u32[]{:S(2)}) collective-permute-start(bf16[1024,512]{1,0:T(8,128)(2,1)S(1)} %collective-permute-done.4.refs_5_.refs_10_), channel_id=1, source_target_pairs={{0,1},{1,0},{2,3},{3,2},{4,5},{5,4},{6,7},{7,6},{8,9},{9,8},{10,11... | collective-permute-start | bytes 3145736 | tf_op jit(solution)/shard_map/ppermute | solution.py:57
  142.2 20.3 %copy-start.10 = (bf16[1280,512]{1,0:T(8,128)(2,1)}, bf16[1280,512]{1,0:T(8,128)(2,1)S(1)}, u32[]{:S(2)}) copy-start(bf16[1280,512]{1,0:T(8,128)(2,1)S(1)} %collective-permute-done.9.refs_6_.refs_11_) | copy-start | bytes 3932164
  142.2 45.6 %collective-permute-start.13 = (bf16[2048,512]{1,0:T(8,128)(2,1)}, bf16[2048,512]{1,0:T(8,128)(2,1)}, u32[]{:S(2)}, u32[]{:S(2)}) collective-permute-start(bf16[2048,512]{1,0:T(8,128)(2,1)} %slice.108), channel_id=1, source_target_pairs={{0,8},{2,10},{4,12},{6,14},{8,0},{10,2},{12,4},{14,6},{16,24},{18,... | collective-permute-start | bytes 6291464 | tf_op jit(solution)/shard_map/ppermute | solution.py:53
  145.7 4.7 %copy-start.4 = (bf16[80,8192]{1,0:T(8,128)(2,1)}, bf16[80,8192]{1,0:T(8,128)(2,1)S(1)}, u32[]{:S(2)}) copy-start(bf16[80,8192]{1,0:T(8,128)(2,1)S(1)} %collective-permute-done.8.refs_1_) | copy-start | bytes 3932164
  145.7 3.2 copy-start
  146.7 3.6 %copy-start.1 = (bf16[160,8192]{1,0:T(8,128)(2,1)}, bf16[160,8192]{1,0:T(8,128)(2,1)S(1)}, u32[]{:S(2)}) copy-start(bf16[160,8192]{1,0:T(8,128)(2,1)S(1)} %collective-permute-done.7.refs_3_.refs_4_) | copy-start | bytes 7864324
  148.9 42.4 %collective-permute-start.12 = (bf16[128,8192]{1,0:T(8,128)(2,1)}, bf16[128,8192]{1,0:T(8,128)(2,1)}, u32[]{:S(2)}, u32[]{:S(2)}) collective-permute-start(bf16[128,8192]{1,0:T(8,128)(2,1)} %pad_maximum_fusion.3), channel_id=1, source_target_pairs={{0,4},{2,6},{4,0},{6,2},{8,12},{10,14},{12,8},{14,10},{16,20},{18,... | collective-permute-start | bytes 6291464 | tf_op jit(solution)/shard_map/ppermute | solution.py:53
  151.7 36.5 %collective-permute-start.11 = (bf16[112,8192]{1,0:T(8,128)(2,1)}, bf16[112,8192]{1,0:T(8,128)(2,1)}, u32[]{:S(2)}, u32[]{:S(2)}) collective-permute-start(bf16[112,8192]{1,0:T(8,128)(2,1)} %pad_maximum_fusion.4), channel_id=1, source_target_pairs={{0,2},{2,0},{4,6},{6,4},{8,10},{10,8},{12,14},{14,12},{16,18},{18,... | collective-permute-start | bytes 5505032 | tf_op jit(solution)/shard_map/ppermute | solution.py:53
  153.2 34.6 %collective-permute-start.14 = (bf16[1280,512]{1,0:T(8,128)(2,1)S(1)}, bf16[1280,512]{1,0:T(8,128)(2,1)S(1)}, u32[]{:S(2)}, u32[]{:S(2)}) collective-permute-start(bf16[1280,512]{1,0:T(8,128)(2,1)S(1)} %collective-permute-done.9.refs_6_.refs_11_), channel_id=1, source_target_pairs={{0,1},{1,0},{2,3},{3,2},{4,5},{5,4},{6,7},{7,6},{8,9},{9,8},{10,11... | collective-permute-start | bytes 3932168 | tf_op jit(solution)/shard_map/ppermute | solution.py:57
  153.3 10.3 %copy-start.13 = (bf16[2,2,2,2,32,512]{5,4,1,0,2,3:T(8,128)(2,1)S(1)}, bf16[2,2,2,2,32,512]{5,4,1,0,2,3:T(8,128)(2,1)}, u32[]{:S(2)}) copy-start(bf16[2,2,2,2,32,512]{5,4,1,0,2,3:T(8,128)(2,1)} %copy-done.12) | copy-start | bytes 1572868
  187.9 3.5 %copy-start.11 = (bf16[1280,512]{1,0:T(8,128)(2,1)}, bf16[1280,512]{1,0:T(8,128)(2,1)S(1)}, u32[]{:S(2)}) copy-start(bf16[1280,512]{1,0:T(8,128)(2,1)S(1)} %collective-permute-done.14.refs_9_.refs_14_) | copy-start | bytes 3932164
  191.3 5.3 %collective-permute-start.17 = (bf16[2048,512]{1,0:T(8,128)(2,1)}, bf16[2048,512]{1,0:T(8,128)(2,1)S(1)}, u32[]{:S(2)}, u32[]{:S(2)}) collective-permute-start(bf16[2048,512]{1,0:T(8,128)(2,1)} %collective-permute-done.13.refs_7_.refs_12_), channel_id=1, source_target_pairs={{0,1},{1,0},{2,3},{3,2},{4,5},{5,4},{6,7},{7,6},{8,9},{9,8},{10,11... | collective-permute-start | bytes 6291464 | tf_op jit(solution)/shard_map/ppermute | solution.py:57
  192.5 20.1 %collective-permute-start.16 = (bf16[48,8192]{1,0:T(8,128)(2,1)S(1)}, bf16[48,8192]{1,0:T(8,128)(2,1)}, u32[]{:S(2)}, u32[]{:S(2)}) collective-permute-start(bf16[48,8192]{1,0:T(8,128)(2,1)S(1)} %slice.87), channel_id=1, source_target_pairs={{0,2},{2,0},{4,6},{6,4},{8,10},{10,8},{12,14},{14,12},{16,18},{18,... | collective-permute-start | bytes 2359304 | tf_op jit(solution)/shard_map/ppermute | solution.py:53
  195.1 14.3 %collective-permute-start.15 = (bf16[32,8192]{1,0:T(8,128)(2,1)S(1)}, bf16[32,8192]{1,0:T(8,128)(2,1)}, u32[]{:S(2)}, u32[]{:S(2)}) collective-permute-start(bf16[32,8192]{1,0:T(8,128)(2,1)S(1)} %slice.86), channel_id=1, source_target_pairs={{0,4},{2,6},{4,0},{6,2},{8,12},{10,14},{12,8},{14,10},{16,20},{18,... | collective-permute-start | bytes 1572872 | tf_op jit(solution)/shard_map/ppermute | solution.py:53
  212.6 34.3 %collective-permute-start.18 = (bf16[160,1024]{1,0:T(8,128)(2,1)}, bf16[160,1024]{1,0:T(8,128)(2,1)S(1)}, u32[]{:S(2)}, u32[]{:S(2)}) collective-permute-start(bf16[160,1024]{1,0:T(8,128)(2,1)} %get-tuple-element.77), channel_id=1, source_target_pairs={{0,0},{1,2},{2,4},{3,6},{4,8},{5,10},{6,12},{7,14},{8,16},{9,18},{... | collective-permute-start | bytes 983048 | tf_op jit(solution)/shard_map/ppermute | solution.py:66
  214.2 32.7 %collective-permute-start.19 = (bf16[160,1024]{1,0:T(8,128)(2,1)}, bf16[160,1024]{1,0:T(8,128)(2,1)S(1)}, u32[]{:S(2)}, u32[]{:S(2)}) collective-permute-start(bf16[160,1024]{1,0:T(8,128)(2,1)} %get-tuple-element.78), channel_id=1, source_target_pairs={{0,4},{1,6},{2,0},{3,2},{4,12},{5,14},{6,8},{7,10},{8,20},{9,22},{... | collective-permute-start | bytes 983048 | tf_op jit(solution)/shard_map/ppermute | solution.py:66
  220.5 26.5 %collective-permute-start.20 = (bf16[160,1024]{1,0:T(8,128)(2,1)}, bf16[160,1024]{1,0:T(8,128)(2,1)S(1)}, u32[]{:S(2)}, u32[]{:S(2)}) collective-permute-start(bf16[160,1024]{1,0:T(8,128)(2,1)} %get-tuple-element.79), channel_id=1, source_target_pairs={{0,8},{1,10},{2,12},{3,14},{4,0},{5,2},{6,4},{7,6},{8,24},{9,26},{... | collective-permute-start | bytes 983048 | tf_op jit(solution)/shard_map/ppermute | solution.py:66
  221.3 25.7 %collective-permute-start.21 = (bf16[160,1024]{1,0:T(8,128)(2,1)}, bf16[160,1024]{1,0:T(8,128)(2,1)S(1)}, u32[]{:S(2)}, u32[]{:S(2)}) collective-permute-start(bf16[160,1024]{1,0:T(8,128)(2,1)} %get-tuple-element.80), channel_id=1, source_target_pairs={{0,12},{1,14},{2,8},{3,10},{4,4},{5,6},{6,0},{7,2},{8,28},{9,30},{... | collective-permute-start | bytes 983048 | tf_op jit(solution)/shard_map/ppermute | solution.py:66
  227.0 17.6 %copy-start.15 = (bf16[512,1024]{1,0:T(8,128)(2,1)S(1)}, bf16[512,1024]{1,0:T(8,128)(2,1)}, u32[]{:S(2)}) copy-start(bf16[512,1024]{1,0:T(8,128)(2,1)} %get-tuple-element.97) | copy-start | bytes 3145732
  244.6 3.5 %copy-start.21 = (bf16[640,1024]{1,0:T(8,128)(2,1)S(1)}, bf16[640,1024]{1,0:T(8,128)(2,1)}, u32[]{:S(2)}) copy-start(bf16[640,1024]{1,0:T(8,128)(2,1)} %get-tuple-element.98) | copy-start | bytes 3932164
  249.0 4.6 %copy-start.22 = (bf16[160,1024]{1,0:T(8,128)(2,1)S(1)}, bf16[160,1024]{1,0:T(8,128)(2,1)}, u32[]{:S(2)}) copy-start(bf16[160,1024]{1,0:T(8,128)(2,1)} %get-tuple-element.93) | copy-start | bytes 983044
  249.3 38.2 %collective-permute-start.28 = (bf16[1296,128]{1,0:T(8,128)(2,1)S(1)}, bf16[1296,128]{1,0:T(8,128)(2,1)S(1)}, u32[]{:S(2)}, u32[]{:S(2)}) collective-permute-start(bf16[1296,128]{1,0:T(8,128)(2,1)S(1)} %pad_maximum_fusion.8), channel_id=1, source_target_pairs={{0,6},{2,4},{4,2},{6,0},{8,14},{10,12},{12,10},{14,8},{16,22},{18,... | collective-permute-start | bytes 995336 | tf_op jit(solution)/shard_map/ppermute | solution.py:53
  249.9 12.8 %collective-permute-start.22 = (bf16[160,1024]{1,0:T(8,128)(2,1)S(1)}, bf16[160,1024]{1,0:T(8,128)(2,1)}, u32[]{:S(2)}, u32[]{:S(2)}) collective-permute-start(bf16[160,1024]{1,0:T(8,128)(2,1)S(1)} %copy-done.23), channel_id=1, source_target_pairs={{0,1},{1,3},{2,5},{3,7},{4,9},{5,11},{6,13},{7,15},{8,17},{9,19},{... | collective-permute-start | bytes 983048 | tf_op jit(solution)/shard_map/ppermute | solution.py:66
  253.5 21.1 %collective-permute-start.23 = (bf16[160,1024]{1,0:T(8,128)(2,1)S(1)}, bf16[160,1024]{1,0:T(8,128)(2,1)}, u32[]{:S(2)}, u32[]{:S(2)}) collective-permute-start(bf16[160,1024]{1,0:T(8,128)(2,1)S(1)} %copy-done.22), channel_id=1, source_target_pairs={{0,5},{1,7},{2,1},{3,3},{4,13},{5,15},{6,9},{7,11},{8,21},{9,23},{... | collective-permute-start | bytes 983048 | tf_op jit(solution)/shard_map/ppermute | solution.py:66
  257.7 29.8 %collective-permute-start.27 = (bf16[1296,128]{1,0:T(8,128)(2,1)}, bf16[1296,128]{1,0:T(8,128)(2,1)}, u32[]{:S(2)}, u32[]{:S(2)}) collective-permute-start(bf16[1296,128]{1,0:T(8,128)(2,1)} %pad_maximum_fusion.7), channel_id=1, source_target_pairs={{0,2},{2,0},{4,6},{6,4},{8,10},{10,8},{12,14},{14,12},{16,18},{18,... | collective-permute-start | bytes 995336 | tf_op jit(solution)/shard_map/ppermute | solution.py:53
  258.7 28.8 %collective-permute-start.26 = (bf16[1296,128]{1,0:T(8,128)(2,1)}, bf16[1296,128]{1,0:T(8,128)(2,1)}, u32[]{:S(2)}, u32[]{:S(2)}) collective-permute-start(bf16[1296,128]{1,0:T(8,128)(2,1)} %pad_maximum_fusion.6), channel_id=1, source_target_pairs={{0,4},{2,6},{4,0},{6,2},{8,12},{10,14},{12,8},{14,10},{16,20},{18,... | collective-permute-start | bytes 995336 | tf_op jit(solution)/shard_map/ppermute | solution.py:53
  262.7 15.2 %collective-permute-start.24 = (bf16[160,1024]{1,0:T(8,128)(2,1)}, bf16[160,1024]{1,0:T(8,128)(2,1)}, u32[]{:S(2)}, u32[]{:S(2)}) collective-permute-start(bf16[160,1024]{1,0:T(8,128)(2,1)} %get-tuple-element.94), channel_id=1, source_target_pairs={{0,9},{1,11},{2,13},{3,15},{4,1},{5,3},{6,5},{7,7},{8,25},{9,27},{... | collective-permute-start | bytes 983048 | tf_op jit(solution)/shard_map/ppermute | solution.py:66
  274.6 12.9 %collective-permute-start.25 = (bf16[160,1024]{1,0:T(8,128)(2,1)}, bf16[160,1024]{1,0:T(8,128)(2,1)}, u32[]{:S(2)}, u32[]{:S(2)}) collective-permute-start(bf16[160,1024]{1,0:T(8,128)(2,1)} %get-tuple-element.95), channel_id=1, source_target_pairs={{0,13},{1,15},{2,9},{3,11},{4,5},{5,7},{6,1},{7,3},{8,29},{9,31},{... | collective-permute-start | bytes 983048 | tf_op jit(solution)/shard_map/ppermute | solution.py:66
  291.4 17.7 %collective-permute-start.29 = (bf16[1296,64]{1,0:T(8,128)(2,1)S(1)}, bf16[1296,64]{1,0:T(8,128)(2,1)S(1)}, u32[]{:S(2)}, u32[]{:S(2)}) collective-permute-start(bf16[1296,64]{1,0:T(8,128)(2,1)S(1)} %concatenate.52), channel_id=1, source_target_pairs={{0,16},{2,18},{4,20},{6,22},{8,24},{10,26},{12,28},{14,30},{16,0},... | collective-permute-start | bytes 497672 | tf_op jit(solution)/shard_map/ppermute | solution.py:53
  310.5 1.4 collective-permute-start.30
  311.9 5.6 %collective-permute-start.31 = (bf16[2,2,2,160,32]{3,4,2,1,0:T(8,128)(2,1)S(1)}, bf16[2,2,2,160,32]{3,4,2,1,0:T(8,128)(2,1)S(1)}, u32[]{:S(2)}, u32[]{:S(2)}) collective-permute-start(bf16[2,2,2,160,32]{3,4,2,1,0:T(8,128)(2,1)S(1)} %get-tuple-element.135), channel_id=1, source_target_pairs={{0,8},{2,10},{4,12},{6,14},{8,0},{10,2},{12,4},{14,6},{16,24},{18,... | collective-permute-start | bytes 245768 | tf_op jit(solution)/shard_map/ppermute | solution.py:53
  (8 other events, 8.0 us)

commit v2 on v1

--- a/solution.py
+++ b/solution.py
@@ -70,14 +70,22 @@
     return lax.optimization_barrier((values, others))[0]
 
 
-def fold_kernel(plan, turn_plan, n_chunks, given, *refs):
+def fold_kernel(plan, turn_plan, n_chunks, keys, ready_keys, given, *refs):
+    n, n_ready = len(keys), len(ready_keys)
     n_in = 1 + max(max(p[0] for p in plan), max(p[0] for turn in turn_plan for p in turn))
-    ins, before, refs = refs[:n_in], refs[n_in : n_in + given], refs[n_in + given :]
-    outs, (together, rows, held, sums, sems) = refs[:-5], refs[-5:]
+    ins, refs = refs[:n_in], refs[n_in:]
+    before, ready, refs = refs[:given], refs[given : given + n_ready], refs[given + n_ready :]
+    outs, together, (rows, held, sums, sems) = refs[:n], refs[n:-4], refs[-4:]
     n_rows, depth = rows.shape
     width = held.shape[2]
-    size = n_rows // len(outs)
+    size = n_rows // n
     step = depth // n_chunks
+    slab = lax.axis_index("slab")
+    x, y = slab % 2, (slab // 2) % 2
+
+    def slot(key):
+        return pl.ds(pl.multiple_of(((y + key[1]) % 2 * 2 + (x + key[0]) % 2) * size, 32), size)
+
     copies, index = [], 0
     for c in range(n_chunks):
         group = []
@@ -94,17 +102,20 @@
             group.append(pltpu.make_async_copy(source, rows.at[pl.ds(place, count), columns], sems.at[index]))
             index += 1
         copies.append(group)
-    shift = before[0].shape[1] if given else 0
-    for group in copies:
+    for group in copies[:2]:
         for copy in group:
             copy.start()
+    shift = before[0].shape[1] if given else 0
+    for value, key in zip(ready, ready_keys):
+        together[0][slot(key), :] = value[...]
     for c, group in enumerate(copies):
         for copy in group:
             copy.wait()
+        for copy in copies[c + 2] if c + 2 < n_chunks else []:
+            copy.start()
         if given and not c:
-            together[:, :shift] = before[0][...]
             for i, out in enumerate(outs):
-                out[:, :shift] = before[0][i * size : (i + 1) * size]
+                out[:, :shift] = before[i][...]
         for k in range(len(turn_plan)):
             columns = slice(k * width, (k + 1) * width)
             value = jnp.dot(
@@ -118,13 +129,14 @@
                 sums[:, columns] = value
             else:
                 value = value.astype(jnp.bfloat16)
-                columns = slice(shift + k * width, shift + (k + 1) * width)
-                together[:, columns] = value
                 for i, out in enumerate(outs):
-                    out[:, columns] = value[i * size : (i + 1) * size]
-
-
-def fold(blocks, turns, before=()):
+                    out[:, shift + k * width : shift + (k + 1) * width] = value[i * size : (i + 1) * size]
+    for out, key in zip(outs, keys):
+        if key is not None:
+            together[0][slot(key), :] = out[...]
+
+
+def fold(blocks, turns, before=(), keys=None, ready=()):
     arrays, plan, turn_plan, place = [], [], [], 0
 
     def operand(value):
@@ -142,16 +154,21 @@
         begins = [sum(count for _, _, count in turn[:i]) for i in range(len(turn))]
         turn_plan.append([(operand(v), first, count, begin) for (v, first, count), begin in zip(turn, begins)])
     depth, width = blocks[0][0][0].shape[1], turns[0][0][0].shape[1]
-    n, t, n_chunks = len(blocks), len(turns), 8
-    all_width = t * width + sum(value.shape[1] for value in before)
+    n, t, n_chunks = len(blocks), len(turns), 4
+    size, all_width = place // n, t * width + (before[0].shape[1] if before else 0)
     n_copies = n_chunks * (len(plan) + 2 * sum(len(turn) for turn in turn_plan))
+    shapes = [jax.ShapeDtypeStruct((size, all_width), jnp.bfloat16)] * n
+    if keys:
+        shapes.append(jax.ShapeDtypeStruct((4 * size, all_width), jnp.bfloat16))
+    ready_values, ready_keys = [v for v, _ in ready], [k for _, k in ready]
     out = pl.pallas_call(
-        functools.partial(fold_kernel, plan, turn_plan, n_chunks, len(before)),
-        out_shape=[jax.ShapeDtypeStruct((place // n, all_width), jnp.bfloat16)] * n
-        + [jax.ShapeDtypeStruct((place, all_width), jnp.bfloat16)],
+        functools.partial(
+            fold_kernel, plan, turn_plan, n_chunks, keys or [None] * n, ready_keys, len(before)
+        ),
+        out_shape=shapes,
         in_specs=[pl.BlockSpec(memory_space=pltpu.HBM)] * len(arrays)
-        + [pl.BlockSpec(memory_space=pltpu.VMEM)] * len(before),
-        out_specs=[pl.BlockSpec(memory_space=pltpu.VMEM)] * (n + 1),
+        + [pl.BlockSpec(memory_space=pltpu.VMEM)] * (len(before) + len(ready)),
+        out_specs=[pl.BlockSpec(memory_space=pltpu.VMEM)] * len(shapes),
         scratch_shapes=[
             pltpu.VMEM((place, depth), jnp.bfloat16),
             pltpu.VMEM((t, depth, width), jnp.bfloat16),
@@ -160,8 +177,8 @@
         ],
         compiler_params=pltpu.CompilerParams(vmem_limit_bytes=60 * 1024 * 1024),
         cost_estimate=pl.CostEstimate(flops=1024, bytes_accessed=1024, transcendentals=0),
-    )(*arrays, *before)
-    return out[:-1], out[-1]
+    )(*arrays, *before, *ready_values)
+    return (out[:-1], out[-1]) if keys else out
 
 
 def place_kernel(plan, width, *refs):
@@ -213,59 +230,72 @@
     ordered = tokens.reshape(2, 2, 2, 2, own_count, width).transpose(3, 2, 0, 1, 4, 5).reshape(n_tokens, width)
     part = split(ordered, 0, core)[0]
 
-    gain_block = lax.dynamic_slice_in_dim(gain, core * depth, depth, 0)
-    turn = (rotation * gain_block[:, None]).astype(jnp.bfloat16)
-    cuts = [0, 3 * depth // 16, depth // 2, depth]
-    pieces = [turn[i:j] for i, j in zip(cuts, cuts[1:])]
-
-    def spread(values, f):
-        return [send_rows(value, f, *key) for value, key in zip(values, NEAR)]
+    gain_block = lax.dynamic_slice_in_dim(gain, core * depth, depth, 0)[:, None]
+    cuts = [0, 7 * depth // 32, 18 * depth // 32, depth]
+    first_piece = (rotation[: cuts[1]] * gain_block[: cuts[1]]).astype(jnp.bfloat16)
+    rotation, gain_block = tie((rotation, gain_block), rows)
+    turn = (rotation * gain_block).astype(jnp.bfloat16)
+    pieces = [first_piece] + [turn[i:j] for i, j in zip(cuts[1:], cuts[2:])]
+
+    def spread(values, f, keys=NEAR):
+        return [send_rows(value, f, *key) for value, key in zip(values, keys)]
 
     def check(exported):
-        return lax.dot_general(exported, checks, (((1,), (1,)), ((), ())), preferred_element_type=jnp.float32)
+        return lax.dot_general(checks, exported, (((1,), (1,)), ((), ())), preferred_element_type=jnp.float32)
 
     def three_terms(values):
         terms = []
         for _ in range(3):
             terms.append(values.astype(jnp.bfloat16).astype(jnp.float32))
             values = values - terms[-1]
-        return jnp.concatenate([jnp.stack(terms), jnp.zeros((13, values.shape[0]), jnp.float32)])
-
-    def quarter(value, dx, dy):
-        size = n_tokens // 4
-        return lax.dynamic_slice_in_dim(value, ((x ^ dx) * 2 + (y ^ dy)) * size, size, 1)
-
-    def plane(values):
-        got = {}
-        for d in NEAR:
-            value = [quarter(v, *d) for v in values]
-            got[d] = move(jnp.concatenate([v.astype(jnp.bfloat16) for v in value]), *d) if any(d) else value
-        return got
-
-    def total(sums):
-        value = sums[0].reshape(2, 2, half, -1)
-        for (dx, dy), blocks in zip(NEAR[1:], sums[1:]):
-            blocks = blocks.astype(jnp.float32).reshape(2, 2, half, -1)
-            blocks = blocks[::-1] if dy else blocks
-            value = value + (blocks[:, ::-1] if dx else blocks)
-        return value.reshape(4 * half, -1)
-
-    near_x, near_y, far_low, piece_a, turn_swapped = tie(
+        return jnp.pad(jnp.stack(terms, axis=1), ((0, 0), (0, 125)))
+
+    def halve(values, squares, bit, dx=0, dy=0, dz=0):
+        keep, give = split(values, 0, bit)
+        if dz:
+            give = jnp.roll(give, give.shape[1] // 2, axis=1)
+        keep_squares, give_squares = split(squares, 0, bit)
+        got = move(jnp.concatenate([give, three_terms(give_squares)], axis=1).astype(jnp.bfloat16), dx, dy, dz)
+        got = got.astype(jnp.float32)
+        n = values.shape[1]
+        return keep + got[:, :n], keep_squares + jnp.sum(got[:, n:], axis=1)
+
+    near_x, near_y, far_low, piece_a, pieces = tie(
         (
             move(rows, dx=1),
             move(rows, dy=1),
             move(rows[:low], dz=2),
             move(jnp.concatenate([pieces[0], part]), dz=1),
-            swap_cores(turn),
-        )
-    )
-    by_x, by_y, far_high, piece_b, swapped_a = tie(
+            pieces,
+        )
+    )
+    by_x, by_y, far_high, piece_b, turn_swapped, last_piece = tie(
         (
             move(jnp.concatenate([near_y[low:], far_low]), dx=1),
             move(jnp.concatenate([near_x[:low], far_low]), dy=1),
             move(rows[low:], dz=2),
             move(pieces[1], dz=1),
+            swap_cores(turn),
+            pieces[2],
+        )
+    )
+    cut = 3 * low // 5
+    own_turn = [(turn, 0, depth), (turn_swapped, 0, depth)]
+    early = [
+        [(rows, 0, half)],
+        [(near_x, 0, half)],
+        [(near_y, 0, half)],
+        [(by_y, 0, low), (by_x, 0, low)],
+        [(far_low, 0, low), (far_high, 0, low)],
+    ]
+    early_own, piece_c = tie((fold(early, [own_turn]), move(last_piece, dz=1)))
+    by_x3, by_y3, swapped_a, swapped_b, swapped_c = tie(
+        (
+            move(jnp.concatenate([far_high, by_y[2 * low - cut :]]), dx=1),
+            move(jnp.concatenate([far_high, by_x[low : low + cut]]), dy=1),
             swap_cores(piece_a),
+            swap_cores(piece_b),
+            swap_cores(piece_c),
         )
     )
     first = pieces[0].shape[0]
@@ -274,73 +304,55 @@
     checks = jnp.concatenate([ordered, ordered_other], axis=1)
     widened = checks.astype(jnp.float32)
     squares = jnp.sum(widened * widened, axis=1)
-    terms = three_terms(squares)
-    cut = 3 * low // 5
-    own_turn = [(turn, 0, depth), (turn_swapped, 0, depth)]
-    near = [
-        [(rows, 0, half)],
-        [(near_x, 0, half)],
-        [(near_y, 0, half)],
-        [(by_y, 0, low), (by_x, 0, low)],
-    ]
-    by_x3, by_y3, piece_c, swapped_b, near_own, checks, terms = tie(
-        (
-            move(jnp.concatenate([far_high, by_y[low + cut :]]), dx=1),
-            move(jnp.concatenate([far_high, by_x[low : low + cut]]), dy=1),
-            move(pieces[2], dz=1),
-            swap_cores(piece_b),
-            fold(near, [own_turn]),
-            checks,
-            terms,
-        )
-    )
-    swapped_c = swap_cores(piece_c)
     arrived = [piece_a, piece_b, piece_c, swapped_a, swapped_b, swapped_c]
     turn_other = [(v, 0, p.shape[0]) for v, p in zip(arrived, pieces + pieces)]
-    by_y4, by_x4, near_rows = tie(
+    by_y4, by_x4, (early_rows, near_rows) = tie(
         (
             move(by_x3[: low - cut], dy=1),
             move(by_y3[low - cut : low], dx=1),
-            fold(near, [turn_other], [near_own[1]]),
-        )
-    )
-    far = [
-        [(far_low, 0, low), (far_high, 0, low)],
+            fold(early, [turn_other], early_own, NEAR + [None]),
+        )
+    )
+    late = [
         [(by_x, low, low), (by_x3, 0, low)],
         [(by_y, low, low), (by_y3, 0, low)],
-        [(by_y3, low, cut), (by_x3, low, low - cut), (by_y4, 0, low - cut), (by_x4, 0, cut)],
+        [(by_y3, low, cut), (by_x3, 2 * cut, low - cut), (by_y4, 0, low - cut), (by_x4, 0, cut)],
     ]
-    received_near, far_rows = tie((spread(near_rows[0], 0), fold(far, [own_turn, turn_other])))
-    sums = plane([check(near_rows[1]), check(far_rows[1]), terms])
-    received_far, sums = tie((spread(far_rows[0], 1), sums))
+    received_near, received_far, (late_rows, far_rows) = tie(
+        (
+            spread(early_rows[:4], 0),
+            spread(early_rows[4:], 1),
+            fold(late, [own_turn, turn_other], (), NEAR[1:], [(early_rows[4], NEAR[0])]),
+        )
+    )
+    products = jnp.concatenate([check(near_rows), check(far_rows)], axis=1)
+
+    def quarter(value, dx, dy):
+        size = n_tokens // 4
+        return lax.dynamic_slice_in_dim(value, ((x ^ dx) * 2 + (y ^ dy)) * size, size, 0)
+
+    def to_send(d):
+        terms = three_terms(quarter(squares, *d))
+        return jnp.concatenate([quarter(products, *d).astype(jnp.bfloat16), terms.astype(jnp.bfloat16)], axis=1)
+
+    parts, received = tie(([move(to_send(d), *d) for d in NEAR[1:]], spread(late_rows[:2], 1, NEAR[1:])))
+    received_far = received_far + received
+    got = sum(v.astype(jnp.float32) for v in parts)
+    sums = quarter(products, 0, 0) + got[:, : 8 * half]
+    squares = quarter(squares, 0, 0) + jnp.sum(got[:, 8 * half :], axis=1)
+    sums, squares, received = tie(halve(sums, squares, z_hi, dz=2) + (spread(late_rows[2:], 1, NEAR[3:]),))
+    received_far = received_far + received
     placed = [((f,) + d, v) for f, values in enumerate((received_near, received_far)) for d, v in zip(NEAR, values)]
     served = whole_rows(placed, width)
 
-    rows_near, rows_far, own_squares = sums[0, 0]
-    kept = [rows_near, rows_far]
-    for f in range(2):
-        kept[f] = total([kept[f]] + [sums[d][4 * half * f : 4 * half * (f + 1)] for d in NEAR[1:]])
-    own_squares = own_squares + sum(sums[d][8 * half :].astype(jnp.float32) for d in NEAR[1:])
-    own_squares = jnp.sum(own_squares, axis=0)
-    near_keep, near_give = split(kept[0], 1, z_hi)
-    far_keep, far_give = split(kept[1], 1, z_hi)
-    keep_squares, give_squares = split(own_squares, 0, z_hi)
-    given = jnp.concatenate([near_give, far_give, three_terms(give_squares)]).astype(jnp.bfloat16)
-    got = move(given, dz=2).astype(jnp.float32)
-    own_scale = lax.rsqrt((keep_squares + jnp.sum(got[8 * half :], axis=0)) / D + EPS)
-    shape = (2, 2, half, 2 * own_count)
-    near_keep = (near_keep + got[4 * half : 8 * half]).reshape(shape)
-    far_keep = (far_keep + got[: 4 * half]).reshape(shape)
-    result = (jnp.stack([near_keep, far_keep]) * own_scale / math.sqrt(D)).astype(jnp.bfloat16)
-    keep = lax.dynamic_index_in_dim(result, z_hi ^ core, 0, keepdims=False)
-    got = swap_cores(lax.dynamic_index_in_dim(result, z_hi ^ 1 ^ core, 0, keepdims=False))
-    both = jnp.stack([keep, got], axis=2)
-    keep = lax.dynamic_slice_in_dim(both, z_lo * own_count, own_count, 4)
-    got = move(lax.dynamic_slice_in_dim(both, (1 - z_lo) * own_count, own_count, 4), dz=1)
-    whole = jnp.stack([keep, got]).reshape(16, half, own_count)
-    flip = ((z_lo * 2 + y) * 2 + x) * 2 + core
-    whole = jnp.take(whole, jnp.arange(16) ^ flip, axis=0)
-    qkv = whole.reshape(16 * half, own_count).T
+    result = (sums * lax.rsqrt(squares / D + EPS)[:, None] / math.sqrt(D)).astype(jnp.bfloat16)
+    keep, give = split(result, 1, z_hi ^ core)
+    got = swap_cores(give)
+    both = jnp.concatenate([jnp.where(core == 0, keep, got), jnp.where(core == 0, got, keep)], axis=1)
+    keep, give = split(both, 0, z_lo)
+    got = move(give, dz=1)
+    whole = jnp.stack([jnp.where(z_lo == 0, keep, got), jnp.where(z_lo == 0, got, keep)], axis=1)
+    qkv = whole.reshape(own_count, 2, 2, 4, half).transpose(0, 1, 3, 2, 4).reshape(own_count, 16 * half)
     return (served[None], qkv)
 
 

time: 320 us -> 309 us (0.966)
  other arithmetic: 21.9 us -> 12 us
  local copies, waits for them, and re-layouts: 25.9 us -> 18.9 us
  waiting for transfers between devices: 176 us -> 183 us
    ppermute x6, waiting for transfers between devices: 1.22 us -> 8.48 us  [swap_cores(): return lax.ppermute(value, 'panel', [(0, 1), (1, 0)])]
    slice x7 -> x5, local copies, waits for them, and re-layouts: 8.61 us -> 1.95 us  [the longest x2 1.8 us: shards(): pieces = [first_piece] + [turn[i:j] for i, j in zip(cuts[1:], cuts[2:])]]
    ppermute x8, waiting for transfers between devices: 24.2 us -> 28.6 us  [send_rows(): return lax.ppermute(value, ('slab', 'panel'), pairs)]
    ppermute x18, waiting for transfers between devices: 150 us -> 146 us  [move(): return lax.ppermute(value, 'slab', pairs)]
  transfers between devices with their start and end apart: 32 -> 32, of which waited for: 15 -> 14; matrix products, arithmetic and copies ran while one was open for 9% -> 6% of each run, Pallas kernels for 13% -> 14%
where the time goes in v2:
time: 309 us
  waiting for transfers between devices  183 us (59%)
  starting transfers between devices  47.8 us (15%)
  Pallas kernels  41.8 us (14%)
  local copies, waits for them, and re-layouts  18.9 us (6%)
  other arithmetic  12 us (4%)
  matrix products  3.45 us (1%)
    ppermute x18, waiting for transfers between devices, move(): return lax.ppermute(value, 'slab', pairs)  146 us
    pallas_call x3, Pallas kernels, fold(): pl.pallas_call(functools.partial(fold_kernel, plan, turn_plan, n_chunks,...  38.4 us
    ppermute x8, waiting for transfers between devices, send_rows(): return lax.ppermute(value, ('slab', 'panel'), pairs)  28.6 us
    ppermute x18, starting transfers between devices, move(): return lax.ppermute(value, 'slab', pairs)  24.2 us
    ppermute x8, starting transfers between devices, send_rows(): return lax.ppermute(value, ('slab', 'panel'), pairs)  22.5 us
    ppermute x6, waiting for transfers between devices, swap_cores(): return lax.ppermute(value, 'panel', [(0, 1), (1, 0)])  8.48 us
  transfers between devices with their start and end apart: 32, of which 14 were waited for; matrix products, arithmetic and copies ran while one was open for 6% of the time, Pallas kernels for 14%

profile of v2, /device:TPU:0, one launch (start us, length us, event | category | flops | bytes accessed | tf_op | source)
XLA Modules:
  0.0 308.7 jit_solution(15676875991612906040)
XLA Ops:
  0.6 3.0 constant_dynamic-slice_fusion.3
  4.1 1.1 copy.34
  5.3 1.8 multiply_convert_fusion.1
  7.3 2.6 collective-permute-start.4
  10.1 1.6 collective-permute-start.2
  11.7 1.5 collective-permute-start.1
  13.4 2.7 collective-permute-start.3
  17.0 1.7 slice.88
  19.3 39.5 %collective-permute-done.4.refs_7_.refs_8_ = bf16[1152,512]{1,0:T(8,128)(2,1)S(1)} collective-permute-done((bf16[1152,512]{1,0:T(8,128)(2,1)S(1)}, bf16[1152,512]{1,0:T(8,128)(2,1)S(1)}, u32[]{:S(2)}, u32[]{:S(2)}) %collective-permute-start.4) | collective-permute-done | bytes 1179680 | tf_op jit(solution)/shard_map/ppermute | solution.py:53
  58.7 14.1 %collective-permute-done.3.refs_5_ = bf16[80,8192]{1,0:T(8,128)(2,1)S(1)} collective-permute-done((bf16[80,8192]{1,0:T(8,128)(2,1)S(1)}, bf16[80,8192]{1,0:T(8,128)(2,1)S(1)}, u32[]{:S(2)}, u32[]{:S(2)}) %collective-permute-start.3) | collective-permute-done | bytes 1310752 | tf_op jit(solution)/shard_map/ppermute | solution.py:53
  72.8 1.5 copy-done.5
  74.4 1.4 copy-done.6
  77.1 1.2 collective-permute-start.5
  78.3 3.0 collective-permute-start.7
  81.4 55.2 %collective-permute-done.7.refs_6_ = bf16[80,8192]{1,0:T(8,128)(2,1)S(1)} collective-permute-done((bf16[80,8192]{1,0:T(8,128)(2,1)S(1)}, bf16[80,8192]{1,0:T(8,128)(2,1)S(1)}, u32[]{:S(2)}, u32[]{:S(2)}) %collective-permute-start.7) | collective-permute-done | bytes 1310752 | tf_op jit(solution)/shard_map/ppermute | solution.py:53
  136.6 2.2 collective-permute-done.8.refs_8_.refs_9_
  138.8 1.4 collective-permute-start.14
  140.2 2.2 copy-done.2
  142.5 2.6 pad_maximum_fusion.3
  145.4 1.4 collective-permute-start.10
  146.8 10.7 %shard_map.59 = (bf16[160,512]{1,0:T(8,128)(2,1)}, bf16[160,512]{1,0:T(8,128)(2,1)}, bf16[160,512]{1,0:T(8,128)(2,1)}, bf16[160,512]{1,0:T(8,128)(2,1)}, bf16[160,512]{1,0:T(8,128)(2,1)}) custom-call(bf16[160,8192]{1,0:T(8,128)(2,1)} %copy-done.3, bf16[160,8192]{1,0:T(8,128)(2,1)} %copy-done.6, bf16[160,8192]{1,0:T(8,128)(2,1)} %copy-done.5, ...), custom_call_target="tpu_custom_call" | custom-call | flops 1024 | bytes 1024 | tf_op jit(solution)/shard_map/pallas_call | solution.py:164
  157.5 22.4 %collective-permute-done.14.refs_9_.refs_10_ = bf16[1792,512]{1,0:T(8,128)(2,1)S(1)} collective-permute-done((bf16[1792,512]{1,0:T(8,128)(2,1)}, bf16[1792,512]{1,0:T(8,128)(2,1)S(1)}, u32[]{:S(2)}, u32[]{:S(2)}) %collective-permute-start.14) | collective-permute-done | bytes 1835040 | tf_op jit(solution)/shard_map/ppermute | solution.py:53
  180.4 7.2 %collective-permute-done.12.refs_10_.refs_11_ = bf16[1152,512]{1,0:T(8,128)(2,1)S(1)} collective-permute-done((bf16[1152,512]{1,0:T(8,128)(2,1)}, bf16[1152,512]{1,0:T(8,128)(2,1)S(1)}, u32[]{:S(2)}, u32[]{:S(2)}) %collective-permute-start.12) | collective-permute-done | bytes 1179680 | tf_op jit(solution)/shard_map/ppermute | solution.py:57
  187.7 4.1 %collective-permute-done.11.refs_3_ = bf16[128,8192]{1,0:T(8,128)(2,1)} collective-permute-done((bf16[128,8192]{1,0:T(8,128)(2,1)}, bf16[128,8192]{1,0:T(8,128)(2,1)}, u32[]{:S(2)}, u32[]{:S(2)}) %collective-permute-start.11) | collective-permute-done | bytes 2097184 | tf_op jit(solution)/shard_map/ppermute | solution.py:53
  191.9 2.1 slice.76
  194.0 1.4 collective-permute-start.17
  195.3 1.9 slice.75
  198.8 13.3 %shard_map.60 = (bf16[160,1024]{1,0:T(8,128)(2,1)}, bf16[160,1024]{1,0:T(8,128)(2,1)}, bf16[160,1024]{1,0:T(8,128)(2,1)}, bf16[160,1024]{1,0:T(8,128)(2,1)}, bf1...) custom-call(bf16[160,8192]{1,0:T(8,128)(2,1)} %copy-done.3, bf16[160,8192]{1,0:T(8,128)(2,1)} %copy-done.6, ...), custom_call_target="tpu_custom_call" | custom-call | flops 1024 | bytes 1024 | tf_op jit(solution)/shard_map/pallas_call | solution.py:164
  212.7 1.6 collective-permute-start.18
  214.3 2.4 collective-permute-start.19
  216.8 6.5 %collective-permute-start.21 = (bf16[160,1024]{1,0:T(8,128)(2,1)}, bf16[160,1024]{1,0:T(8,128)(2,1)S(1)}, u32[]{:S(2)}, u32[]{:S(2)}) collective-permute-start(bf16[160,1024]{1,0:T(8,128)(2,1)} %get-tuple-element.106), channel_id=1, source_target_pairs={{0,12},{1,14},{2,8},{3,10},{4,4},{5,6},{6,0},{7,2},{8,28},{9,30},{... | collective-permute-start | bytes 983048 | tf_op jit(solution)/shard_map/ppermute | solution.py:66
  223.3 1.3 collective-permute-start.22
  225.6 14.4 %shard_map.61 = (bf16[160,1024]{1,0:T(8,128)(2,1)}, bf16[160,1024]{1,0:T(8,128)(2,1)}, bf16[160,1024]{1,0:T(8,128)(2,1)}, bf16[640,1024]{1,0:T(8,128)(2,1)}) custom-call(bf16[160,8192]{1,0:T(8,128)(2,1)} %copy-done.2, bf16[128,8192]{1,0:T(8,128)(2,1)} %collective-permute-done.10.refs_1_, bf16[160,8192]{1,0:T(8,128)(2,1)} %copy-done.1, ...), custom_call_target="tpu_custom_call" | custom-call | flops 1024 | bytes 1024 | tf_op jit(solution)/shard_map/pallas_call | solution.py:164
  240.1 2.4 fusion.21
  242.6 9.3 %collective-permute-done.22.refs_4_ = bf16[160,1024]{1,0:T(8,128)(2,1)} collective-permute-done((bf16[160,1024]{1,0:T(8,128)(2,1)}, bf16[160,1024]{1,0:T(8,128)(2,1)}, u32[]{:S(2)}, u32[]{:S(2)}) %collective-permute-start.22) | collective-permute-done | bytes 327712 | tf_op jit(solution)/shard_map/ppermute | solution.py:66
  253.8 1.6 collective-permute-start.24
  256.9 1.9 collective-permute-start.25
  258.8 1.9 collective-permute-start.26
  260.7 5.2 %collective-permute-start.27 = (bf16[160,1024]{1,0:T(8,128)(2,1)}, bf16[160,1024]{1,0:T(8,128)(2,1)}, u32[]{:S(2)}, u32[]{:S(2)}) collective-permute-start(bf16[160,1024]{1,0:T(8,128)(2,1)} %get-tuple-element.122), channel_id=1, source_target_pairs={{0,9},{1,11},{2,13},{3,15},{4,1},{5,3},{6,5},{7,7},{8,25},{9,27},{... | collective-permute-start | bytes 983048 | tf_op jit(solution)/shard_map/ppermute | solution.py:66
  265.9 7.7 %collective-permute-done.26.refs_5_ = bf16[160,1024]{1,0:T(8,128)(2,1)} collective-permute-done((bf16[160,1024]{1,0:T(8,128)(2,1)}, bf16[160,1024]{1,0:T(8,128)(2,1)}, u32[]{:S(2)}, u32[]{:S(2)}) %collective-permute-start.26) | collective-permute-done | bytes 327712 | tf_op jit(solution)/shard_map/ppermute | solution.py:66
  273.6 6.6 %collective-permute-done.27.refs_6_ = bf16[160,1024]{1,0:T(8,128)(2,1)} collective-permute-done((bf16[160,1024]{1,0:T(8,128)(2,1)}, bf16[160,1024]{1,0:T(8,128)(2,1)}, u32[]{:S(2)}, u32[]{:S(2)}) %collective-permute-start.27) | collective-permute-done | bytes 327712 | tf_op jit(solution)/shard_map/ppermute | solution.py:66
  280.3 1.1 convert_add_fusion
  282.1 3.5 %collective-permute-start.29 = (bf16[160,1024]{1,0:T(8,128)(2,1)}, bf16[160,1024]{1,0:T(8,128)(2,1)S(1)}, u32[]{:S(2)}, u32[]{:S(2)}) collective-permute-start(bf16[160,1024]{1,0:T(8,128)(2,1)} %get-tuple-element.128), channel_id=1, source_target_pairs={{0,13},{1,15},{2,9},{3,11},{4,5},{5,7},{6,1},{7,3},{8,29},{9,31},{... | collective-permute-start | bytes 983048 | tf_op jit(solution)/shard_map/ppermute | solution.py:66
  285.6 8.7 %collective-permute-done.28 = bf16[64,1408]{1,0:T(8,128)(2,1)S(1)} collective-permute-done((bf16[64,1408]{1,0:T(8,128)(2,1)S(1)}, bf16[64,1408]{1,0:T(8,128)(2,1)S(1)}, u32[]{:S(2)}, u32[]{:S(2)}) %collective-permute-start.28) | collective-permute-done | bytes 180256 | tf_op jit(solution)/shard_map/ppermute | solution.py:53
  294.6 5.0 %collective-permute-done.29.refs_7_ = bf16[160,1024]{1,0:T(8,128)(2,1)S(1)} collective-permute-done((bf16[160,1024]{1,0:T(8,128)(2,1)}, bf16[160,1024]{1,0:T(8,128)(2,1)S(1)}, u32[]{:S(2)}, u32[]{:S(2)}) %collective-permute-start.29) | collective-permute-done | bytes 327712 | tf_op jit(solution)/shard_map/ppermute | solution.py:66
  299.8 1.2 collective-permute-done.30
  301.1 2.4 collective-permute-start.31
  303.5 3.4 %shard_map.62 = bf16[160,8192]{1,0:T(8,128)(2,1)} custom-call(bf16[160,1024]{1,0:T(8,128)(2,1)} %copy-done.19, bf16[160,1024]{1,0:T(8,128)(2,1)} %copy-done.20, bf16[160,1024]{1,0:T(8,128)(2,1)} %copy-done.21, bf16[160,1024]{1,0:T(8,128)(2,1)} %copy-done.22, bf16[160,1024]{1,0:T(8,128)(2,1)} %collective-permute-done.22.refs_4_, ...), custom_call_target="tpu_custom_call" | custom-call | flops 1024 | bytes 1024 | tf_op jit(solution)/shard_map/pallas_call | solution.py:203
  (141 shorter events, 14.6 us)
Async XLA Ops:
  3.7 6.3 %collective-permute-start = (bf16[160,4096]{1,0:T(8,128)(2,1)}, bf16[160,4096]{1,0:T(8,128)(2,1)S(1)}, u32[]{:S(2)}, u32[]{:S(2)}) collective-permute-start(bf16[160,4096]{1,0:T(8,128)(2,1)} %get-tuple-element.138), channel_id=1, source_target_pairs={{0,1},{1,0},{2,3},{3,2},{4,5},{5,4},{6,7},{7,6},{8,9},{9,8},{10,11... | collective-permute-start | bytes 3932168 | tf_op jit(solution)/shard_map/ppermute | solution.py:57
  5.3 10.7 %slice-start = ((s8[8388608]{0:T(1024)(128)(4,1)}), s8[4194304]{0:T(1024)(128)(4,1)S(1)}, s32[]{:S(2)}) async-start(s8[8388608]{0:T(1024)(128)(4,1)} %bitcast.35), calls=%async_computation | async-start | bytes 8388608
  7.3 51.5 %collective-permute-start.4 = (bf16[1152,512]{1,0:T(8,128)(2,1)S(1)}, bf16[1152,512]{1,0:T(8,128)(2,1)S(1)}, u32[]{:S(2)}, u32[]{:S(2)}) collective-permute-start(bf16[1152,512]{1,0:T(8,128)(2,1)S(1)} %pad_maximum_fusion.5), channel_id=1, source_target_pairs={{0,8},{2,10},{4,12},{6,14},{8,0},{10,2},{12,4},{14,6},{16,24},{18,... | collective-permute-start | bytes 3538952 | tf_op jit(solution)/shard_map/ppermute | solution.py:53
  10.1 62.7 %collective-permute-start.2 = (bf16[160,8192]{1,0:T(8,128)(2,1)S(1)}, bf16[160,8192]{1,0:T(8,128)(2,1)S(1)}, u32[]{:S(2)}, u32[]{:S(2)}) collective-permute-start(bf16[160,8192]{1,0:T(8,128)(2,1)S(1)} %pad_maximum_fusion.refs_0_), channel_id=1, source_target_pairs={{0,4},{2,6},{4,0},{6,2},{8,12},{10,14},{12,8},{14,10},{16,20},{18,... | collective-permute-start | bytes 7864328 | tf_op jit(solution)/shard_map/ppermute | solution.py:53
  11.7 61.1 %collective-permute-start.1 = (bf16[160,8192]{1,0:T(8,128)(2,1)S(1)}, bf16[160,8192]{1,0:T(8,128)(2,1)S(1)}, u32[]{:S(2)}, u32[]{:S(2)}) collective-permute-start(bf16[160,8192]{1,0:T(8,128)(2,1)S(1)} %pad_maximum_fusion.refs_0_), channel_id=1, source_target_pairs={{0,2},{2,0},{4,6},{6,4},{8,10},{10,8},{12,14},{14,12},{16,18},{18,... | collective-permute-start | bytes 7864328 | tf_op jit(solution)/shard_map/ppermute | solution.py:53
  13.4 59.4 %collective-permute-start.3 = (bf16[80,8192]{1,0:T(8,128)(2,1)S(1)}, bf16[80,8192]{1,0:T(8,128)(2,1)S(1)}, u32[]{:S(2)}, u32[]{:S(2)}) collective-permute-start(bf16[80,8192]{1,0:T(8,128)(2,1)S(1)} %get-tuple-element.136), channel_id=1, source_target_pairs={{0,16},{2,18},{4,20},{6,22},{8,24},{10,26},{12,28},{14,30},{16,0},... | collective-permute-start | bytes 3932168 | tf_op jit(solution)/shard_map/ppermute | solution.py:53
  16.8 122.0 %collective-permute-start.9 = (bf16[4096,512]{1,0:T(8,128)(2,1)S(1)}, bf16[4096,512]{1,0:T(8,128)(2,1)S(1)}, u32[]{:S(2)}, u32[]{:S(2)}) collective-permute-start(bf16[4096,512]{1,0:T(8,128)(2,1)S(1)} %multiply_convert_fusion.refs_7_.refs_6_), channel_id=1, source_target_pairs={{0,1},{1,0},{2,3},{3,2},{4,5},{5,4},{6,7},{7,6},{8,9},{9,8},{10,11... | collective-permute-start | bytes 12582920 | tf_op jit(solution)/shard_map/ppermute | solution.py:57
  58.7 17.8 %copy-start.10 = (bf16[1152,512]{1,0:T(8,128)(2,1)}, bf16[1152,512]{1,0:T(8,128)(2,1)S(1)}, u32[]{:S(2)}) copy-start(bf16[1152,512]{1,0:T(8,128)(2,1)S(1)} %collective-permute-done.4.refs_7_.refs_8_) | copy-start | bytes 3538948
  76.5 62.2 %collective-permute-start.6 = (bf16[160,8192]{1,0:T(8,128)(2,1)S(1)}, bf16[160,8192]{1,0:T(8,128)(2,1)S(1)}, u32[]{:S(2)}, u32[]{:S(2)}) collective-permute-start(bf16[160,8192]{1,0:T(8,128)(2,1)S(1)} %get-tuple-element.143), channel_id=1, source_target_pairs={{0,4},{2,6},{4,0},{6,2},{8,12},{10,14},{12,8},{14,10},{16,20},{18,... | collective-permute-start | bytes 7864328 | tf_op jit(solution)/shard_map/ppermute | solution.py:53
  77.1 61.7 %collective-permute-start.5 = (bf16[160,8192]{1,0:T(8,128)(2,1)S(1)}, bf16[160,8192]{1,0:T(8,128)(2,1)S(1)}, u32[]{:S(2)}, u32[]{:S(2)}) collective-permute-start(bf16[160,8192]{1,0:T(8,128)(2,1)S(1)} %get-tuple-element.144), channel_id=1, source_target_pairs={{0,2},{2,0},{4,6},{6,4},{8,10},{10,8},{12,14},{14,12},{16,18},{18,... | collective-permute-start | bytes 7864328 | tf_op jit(solution)/shard_map/ppermute | solution.py:53
  78.3 60.4 %collective-permute-start.8 = (bf16[1408,512]{1,0:T(8,128)(2,1)S(1)}, bf16[1408,512]{1,0:T(8,128)(2,1)S(1)}, u32[]{:S(2)}, u32[]{:S(2)}) collective-permute-start(bf16[1408,512]{1,0:T(8,128)(2,1)S(1)} %slice.87), channel_id=1, source_target_pairs={{0,8},{2,10},{4,12},{6,14},{8,0},{10,2},{12,4},{14,6},{16,24},{18,... | collective-permute-start | bytes 4325384 | tf_op jit(solution)/shard_map/ppermute | solution.py:53
  78.3 58.2 %collective-permute-start.7 = (bf16[80,8192]{1,0:T(8,128)(2,1)S(1)}, bf16[80,8192]{1,0:T(8,128)(2,1)S(1)}, u32[]{:S(2)}, u32[]{:S(2)}) collective-permute-start(bf16[80,8192]{1,0:T(8,128)(2,1)S(1)} %get-tuple-element.135), channel_id=1, source_target_pairs={{0,16},{2,18},{4,20},{6,22},{8,24},{10,26},{12,28},{14,30},{16,0},... | collective-permute-start | bytes 3932168 | tf_op jit(solution)/shard_map/ppermute | solution.py:53
  136.5 10.2 %copy-start.8 = (bf16[80,8192]{1,0:T(8,128)(2,1)}, bf16[80,8192]{1,0:T(8,128)(2,1)S(1)}, u32[]{:S(2)}) copy-start(bf16[80,8192]{1,0:T(8,128)(2,1)S(1)} %collective-permute-done.7.refs_6_) | copy-start | bytes 3932164
  138.7 6.6 %copy-start.12 = (bf16[1408,512]{1,0:T(8,128)(2,1)}, bf16[1408,512]{1,0:T(8,128)(2,1)S(1)}, u32[]{:S(2)}) copy-start(bf16[1408,512]{1,0:T(8,128)(2,1)S(1)} %collective-permute-done.8.refs_8_.refs_9_) | copy-start | bytes 4325380
  138.8 41.1 %collective-permute-start.14 = (bf16[1792,512]{1,0:T(8,128)(2,1)}, bf16[1792,512]{1,0:T(8,128)(2,1)S(1)}, u32[]{:S(2)}, u32[]{:S(2)}) collective-permute-start(bf16[1792,512]{1,0:T(8,128)(2,1)} %slice.88), channel_id=1, source_target_pairs={{0,8},{2,10},{4,12},{6,14},{8,0},{10,2},{12,4},{14,6},{16,24},{18,... | collective-permute-start | bytes 5505032 | tf_op jit(solution)/shard_map/ppermute | solution.py:53
  145.0 46.8 %collective-permute-start.11 = (bf16[128,8192]{1,0:T(8,128)(2,1)}, bf16[128,8192]{1,0:T(8,128)(2,1)}, u32[]{:S(2)}, u32[]{:S(2)}) collective-permute-start(bf16[128,8192]{1,0:T(8,128)(2,1)} %get-tuple-element.141), channel_id=1, source_target_pairs={{0,4},{2,6},{4,0},{6,2},{8,12},{10,14},{12,8},{14,10},{16,20},{18,... | collective-permute-start | bytes 6291464 | tf_op jit(solution)/shard_map/ppermute | solution.py:53
  145.4 46.5 %collective-permute-start.10 = (bf16[128,8192]{1,0:T(8,128)(2,1)}, bf16[128,8192]{1,0:T(8,128)(2,1)}, u32[]{:S(2)}, u32[]{:S(2)}) collective-permute-start(bf16[128,8192]{1,0:T(8,128)(2,1)} %get-tuple-element.142), channel_id=1, source_target_pairs={{0,2},{2,0},{4,6},{6,4},{8,10},{10,8},{12,14},{14,12},{16,18},{18,... | collective-permute-start | bytes 6291464 | tf_op jit(solution)/shard_map/ppermute | solution.py:53
  179.9 18.9 %copy-start.9 = (bf16[1792,512]{1,0:T(8,128)(2,1)}, bf16[1792,512]{1,0:T(8,128)(2,1)S(1)}, u32[]{:S(2)}) copy-start(bf16[1792,512]{1,0:T(8,128)(2,1)S(1)} %collective-permute-done.14.refs_9_.refs_10_) | copy-start | bytes 5505028
  179.9 12.0 %collective-permute-start.15 = (bf16[1792,512]{1,0:T(8,128)(2,1)S(1)}, bf16[1792,512]{1,0:T(8,128)(2,1)}, u32[]{:S(2)}, u32[]{:S(2)}) collective-permute-start(bf16[1792,512]{1,0:T(8,128)(2,1)S(1)} %collective-permute-done.14.refs_9_.refs_10_), channel_id=1, source_target_pairs={{0,1},{1,0},{2,3},{3,2},{4,5},{5,4},{6,7},{7,6},{8,9},{9,8},{10,11... | collective-permute-start | bytes 5505032 | tf_op jit(solution)/shard_map/ppermute | solution.py:57
  179.9 7.7 %collective-permute-start.13 = (bf16[1408,512]{1,0:T(8,128)(2,1)}, bf16[1408,512]{1,0:T(8,128)(2,1)}, u32[]{:S(2)}, u32[]{:S(2)}) collective-permute-start(bf16[1408,512]{1,0:T(8,128)(2,1)} %copy-done.12), channel_id=1, source_target_pairs={{0,1},{1,0},{2,3},{3,2},{4,5},{5,4},{6,7},{7,6},{8,9},{9,8},{10,11... | collective-permute-start | bytes 4325384 | tf_op jit(solution)/shard_map/ppermute | solution.py:57
  180.4 7.2 %collective-permute-start.12 = (bf16[1152,512]{1,0:T(8,128)(2,1)}, bf16[1152,512]{1,0:T(8,128)(2,1)S(1)}, u32[]{:S(2)}, u32[]{:S(2)}) collective-permute-start(bf16[1152,512]{1,0:T(8,128)(2,1)} %copy-done.10), channel_id=1, source_target_pairs={{0,1},{1,0},{2,3},{3,2},{4,5},{5,4},{6,7},{7,6},{8,9},{9,8},{10,11... | collective-permute-start | bytes 3538952 | tf_op jit(solution)/shard_map/ppermute | solution.py:57
  187.7 11.1 %copy-start.11 = (bf16[1152,512]{1,0:T(8,128)(2,1)}, bf16[1152,512]{1,0:T(8,128)(2,1)S(1)}, u32[]{:S(2)}) copy-start(bf16[1152,512]{1,0:T(8,128)(2,1)S(1)} %collective-permute-done.12.refs_10_.refs_11_) | copy-start | bytes 3538948
  194.0 18.7 %collective-permute-start.17 = (bf16[48,8192]{1,0:T(8,128)(2,1)}, bf16[48,8192]{1,0:T(8,128)(2,1)}, u32[]{:S(2)}, u32[]{:S(2)}) collective-permute-start(bf16[48,8192]{1,0:T(8,128)(2,1)} %slice.76), channel_id=1, source_target_pairs={{0,2},{2,0},{4,6},{6,4},{8,10},{10,8},{12,14},{14,12},{16,18},{18,... | collective-permute-start | bytes 2359304 | tf_op jit(solution)/shard_map/ppermute | solution.py:53
  197.2 15.4 %collective-permute-start.16 = (bf16[32,8192]{1,0:T(8,128)(2,1)}, bf16[32,8192]{1,0:T(8,128)(2,1)}, u32[]{:S(2)}, u32[]{:S(2)}) collective-permute-start(bf16[32,8192]{1,0:T(8,128)(2,1)} %slice.75), channel_id=1, source_target_pairs={{0,4},{2,6},{4,0},{6,2},{8,12},{10,14},{12,8},{14,10},{16,20},{18,... | collective-permute-start | bytes 1572872 | tf_op jit(solution)/shard_map/ppermute | solution.py:53
  198.8 13.4 %copy-start.15 = (bf16[256,512]{1,0:T(8,128)(2,1)}, bf16[256,512]{1,0:T(8,128)(2,1)S(1)}, u32[]{:S(2)}) copy-start(bf16[256,512]{1,0:T(8,128)(2,1)S(1)} %get-tuple-element.139) | copy-start | bytes 786436
  198.8 13.4 %copy-start.17 = (bf16[256,512]{1,0:T(8,128)(2,1)}, bf16[256,512]{1,0:T(8,128)(2,1)S(1)}, u32[]{:S(2)}) copy-start(bf16[256,512]{1,0:T(8,128)(2,1)S(1)} %get-tuple-element.140) | copy-start | bytes 786436
  198.8 13.4 %copy-start.14 = (bf16[2,2,2,2,32,512]{5,4,1,0,2,3:T(8,128)(2,1)S(1)}, bf16[2,2,2,2,32,512]{5,4,1,0,2,3:T(8,128)(2,1)}, u32[]{:S(2)}) copy-start(bf16[2,2,2,2,32,512]{5,4,1,0,2,3:T(8,128)(2,1)} %copy-done.13) | copy-start | bytes 1572868
  212.7 29.8 %collective-permute-start.18 = (bf16[160,1024]{1,0:T(8,128)(2,1)}, bf16[160,1024]{1,0:T(8,128)(2,1)S(1)}, u32[]{:S(2)}, u32[]{:S(2)}) collective-permute-start(bf16[160,1024]{1,0:T(8,128)(2,1)} %get-tuple-element.103), channel_id=1, source_target_pairs={{0,0},{1,2},{2,4},{3,6},{4,8},{5,10},{6,12},{7,14},{8,16},{9,18},{... | collective-permute-start | bytes 983048 | tf_op jit(solution)/shard_map/ppermute | solution.py:66
  214.3 28.2 %collective-permute-start.19 = (bf16[160,1024]{1,0:T(8,128)(2,1)}, bf16[160,1024]{1,0:T(8,128)(2,1)S(1)}, u32[]{:S(2)}, u32[]{:S(2)}) collective-permute-start(bf16[160,1024]{1,0:T(8,128)(2,1)} %get-tuple-element.104), channel_id=1, source_target_pairs={{0,4},{1,6},{2,0},{3,2},{4,12},{5,14},{6,8},{7,10},{8,20},{9,22},{... | collective-permute-start | bytes 983048 | tf_op jit(solution)/shard_map/ppermute | solution.py:66
  216.7 25.8 %collective-permute-start.20 = (bf16[160,1024]{1,0:T(8,128)(2,1)}, bf16[160,1024]{1,0:T(8,128)(2,1)S(1)}, u32[]{:S(2)}, u32[]{:S(2)}) collective-permute-start(bf16[160,1024]{1,0:T(8,128)(2,1)} %get-tuple-element.105), channel_id=1, source_target_pairs={{0,8},{1,10},{2,12},{3,14},{4,0},{5,2},{6,4},{7,6},{8,24},{9,26},{... | collective-permute-start | bytes 983048 | tf_op jit(solution)/shard_map/ppermute | solution.py:66
  216.8 25.8 %collective-permute-start.21 = (bf16[160,1024]{1,0:T(8,128)(2,1)}, bf16[160,1024]{1,0:T(8,128)(2,1)S(1)}, u32[]{:S(2)}, u32[]{:S(2)}) collective-permute-start(bf16[160,1024]{1,0:T(8,128)(2,1)} %get-tuple-element.106), channel_id=1, source_target_pairs={{0,12},{1,14},{2,8},{3,10},{4,4},{5,6},{6,0},{7,2},{8,28},{9,30},{... | collective-permute-start | bytes 983048 | tf_op jit(solution)/shard_map/ppermute | solution.py:66
  223.3 28.5 %collective-permute-start.22 = (bf16[160,1024]{1,0:T(8,128)(2,1)}, bf16[160,1024]{1,0:T(8,128)(2,1)}, u32[]{:S(2)}, u32[]{:S(2)}) collective-permute-start(bf16[160,1024]{1,0:T(8,128)(2,1)} %get-tuple-element.107.refs_14_), channel_id=1, source_target_pairs={{0,1},{1,3},{2,5},{3,7},{4,9},{5,11},{6,13},{7,15},{8,17},{9,19},{... | collective-permute-start | bytes 983048 | tf_op jit(solution)/shard_map/ppermute | solution.py:66
  225.6 14.4 %copy-start.16 = (bf16[256,512]{1,0:T(8,128)(2,1)S(1)}, bf16[256,512]{1,0:T(8,128)(2,1)}, u32[]{:S(2)}) copy-start(bf16[256,512]{1,0:T(8,128)(2,1)} %copy-done.15) | copy-start | bytes 786436
  225.6 14.4 %copy-start.18 = (bf16[256,512]{1,0:T(8,128)(2,1)S(1)}, bf16[256,512]{1,0:T(8,128)(2,1)}, u32[]{:S(2)}) copy-start(bf16[256,512]{1,0:T(8,128)(2,1)} %copy-done.17) | copy-start | bytes 786436
  240.1 11.8 %copy-start.26 = (bf16[640,1024]{1,0:T(8,128)(2,1)S(1)}, bf16[640,1024]{1,0:T(8,128)(2,1)}, u32[]{:S(2)}) copy-start(bf16[640,1024]{1,0:T(8,128)(2,1)} %get-tuple-element.120) | copy-start | bytes 3932164
  242.5 9.3 %copy-start.19 = (bf16[160,1024]{1,0:T(8,128)(2,1)}, bf16[160,1024]{1,0:T(8,128)(2,1)S(1)}, u32[]{:S(2)}) copy-start(bf16[160,1024]{1,0:T(8,128)(2,1)S(1)} %collective-permute-done.18.refs_0_) | copy-start | bytes 983044
  242.5 9.3 %copy-start.20 = (bf16[160,1024]{1,0:T(8,128)(2,1)}, bf16[160,1024]{1,0:T(8,128)(2,1)S(1)}, u32[]{:S(2)}) copy-start(bf16[160,1024]{1,0:T(8,128)(2,1)S(1)} %collective-permute-done.19.refs_1_) | copy-start | bytes 983044
  242.5 9.3 %copy-start.21 = (bf16[160,1024]{1,0:T(8,128)(2,1)}, bf16[160,1024]{1,0:T(8,128)(2,1)S(1)}, u32[]{:S(2)}) copy-start(bf16[160,1024]{1,0:T(8,128)(2,1)S(1)} %collective-permute-done.20.refs_2_) | copy-start | bytes 983044
  242.6 9.3 %copy-start.22 = (bf16[160,1024]{1,0:T(8,128)(2,1)}, bf16[160,1024]{1,0:T(8,128)(2,1)S(1)}, u32[]{:S(2)}) copy-start(bf16[160,1024]{1,0:T(8,128)(2,1)S(1)} %collective-permute-done.21.refs_3_) | copy-start | bytes 983044
  253.8 26.5 %collective-permute-start.24 = (bf16[128,1408]{1,0:T(8,128)(2,1)}, bf16[128,1408]{1,0:T(8,128)(2,1)S(1)}, u32[]{:S(2)}, u32[]{:S(2)}) collective-permute-start(bf16[128,1408]{1,0:T(8,128)(2,1)} %fusion.14), channel_id=1, source_target_pairs={{0,4},{2,6},{4,0},{6,2},{8,12},{10,14},{12,8},{14,10},{16,20},{18,... | collective-permute-start | bytes 1081352 | tf_op jit(solution)/shard_map/ppermute | solution.py:53
  256.1 24.2 %collective-permute-start.23 = (bf16[128,1408]{1,0:T(8,128)(2,1)}, bf16[128,1408]{1,0:T(8,128)(2,1)S(1)}, u32[]{:S(2)}, u32[]{:S(2)}) collective-permute-start(bf16[128,1408]{1,0:T(8,128)(2,1)} %fusion.13), channel_id=1, source_target_pairs={{0,2},{2,0},{4,6},{6,4},{8,10},{10,8},{12,14},{14,12},{16,18},{18,... | collective-permute-start | bytes 1081352 | tf_op jit(solution)/shard_map/ppermute | solution.py:53
  256.9 23.4 %collective-permute-start.25 = (bf16[128,1408]{1,0:T(8,128)(2,1)}, bf16[128,1408]{1,0:T(8,128)(2,1)}, u32[]{:S(2)}, u32[]{:S(2)}) collective-permute-start(bf16[128,1408]{1,0:T(8,128)(2,1)} %fusion.15), channel_id=1, source_target_pairs={{0,6},{2,4},{4,2},{6,0},{8,14},{10,12},{12,10},{14,8},{16,22},{18,... | collective-permute-start | bytes 1081352 | tf_op jit(solution)/shard_map/ppermute | solution.py:53
  258.8 14.8 %collective-permute-start.26 = (bf16[160,1024]{1,0:T(8,128)(2,1)}, bf16[160,1024]{1,0:T(8,128)(2,1)}, u32[]{:S(2)}, u32[]{:S(2)}) collective-permute-start(bf16[160,1024]{1,0:T(8,128)(2,1)} %get-tuple-element.121), channel_id=1, source_target_pairs={{0,5},{1,7},{2,1},{3,3},{4,13},{5,15},{6,9},{7,11},{8,21},{9,23},{... | collective-permute-start | bytes 983048 | tf_op jit(solution)/shard_map/ppermute | solution.py:66
  260.7 19.5 %collective-permute-start.27 = (bf16[160,1024]{1,0:T(8,128)(2,1)}, bf16[160,1024]{1,0:T(8,128)(2,1)}, u32[]{:S(2)}, u32[]{:S(2)}) collective-permute-start(bf16[160,1024]{1,0:T(8,128)(2,1)} %get-tuple-element.122), channel_id=1, source_target_pairs={{0,9},{1,11},{2,13},{3,15},{4,1},{5,3},{6,5},{7,7},{8,25},{9,27},{... | collective-permute-start | bytes 983048 | tf_op jit(solution)/shard_map/ppermute | solution.py:66
  282.0 12.3 %collective-permute-start.28 = (bf16[64,1408]{1,0:T(8,128)(2,1)S(1)}, bf16[64,1408]{1,0:T(8,128)(2,1)S(1)}, u32[]{:S(2)}, u32[]{:S(2)}) collective-permute-start(bf16[64,1408]{1,0:T(8,128)(2,1)S(1)} %fusion.17), channel_id=1, source_target_pairs={{0,16},{2,18},{4,20},{6,22},{8,24},{10,26},{12,28},{14,30},{16,0},... | collective-permute-start | bytes 540680 | tf_op jit(solution)/shard_map/ppermute | solution.py:53
  282.1 17.5 %collective-permute-start.29 = (bf16[160,1024]{1,0:T(8,128)(2,1)}, bf16[160,1024]{1,0:T(8,128)(2,1)S(1)}, u32[]{:S(2)}, u32[]{:S(2)}) collective-permute-start(bf16[160,1024]{1,0:T(8,128)(2,1)} %get-tuple-element.128), channel_id=1, source_target_pairs={{0,13},{1,15},{2,9},{3,11},{4,5},{5,7},{6,1},{7,3},{8,29},{9,31},{... | collective-permute-start | bytes 983048 | tf_op jit(solution)/shard_map/ppermute | solution.py:66
  299.7 1.3 collective-permute-start.30
  301.1 5.8 %collective-permute-start.31 = (bf16[32,1280]{1,0:T(8,128)(2,1)S(1)}, bf16[32,1280]{1,0:T(8,128)(2,1)S(1)}, u32[]{:S(2)}, u32[]{:S(2)}) collective-permute-start(bf16[32,1280]{1,0:T(8,128)(2,1)S(1)} %fusion.18), channel_id=1, source_target_pairs={{0,8},{2,10},{4,12},{6,14},{8,0},{10,2},{12,4},{14,6},{16,24},{18,... | collective-permute-start | bytes 245768 | tf_op jit(solution)/shard_map/ppermute | solution.py:53
  (14 other events, 51.4 us)

commit v3 on v2

--- a/solution.py
+++ b/solution.py
@@ -70,73 +70,77 @@
     return lax.optimization_barrier((values, others))[0]
 
 
-def fold_kernel(plan, turn_plan, n_chunks, keys, ready_keys, given, *refs):
+def fold_kernel(plan, turn_plan, steps, n_done, keys, ready_keys, n_begun, given, *refs):
     n, n_ready = len(keys), len(ready_keys)
     n_in = 1 + max(max(p[0] for p in plan), max(p[0] for turn in turn_plan for p in turn))
     ins, refs = refs[:n_in], refs[n_in:]
+    begun, refs = refs[:n_begun], refs[n_begun:]
     before, ready, refs = refs[:given], refs[given : given + n_ready], refs[given + n_ready :]
-    outs, together, (rows, held, sums, sems) = refs[:n], refs[n:-4], refs[-4:]
-    n_rows, depth = rows.shape
+    outs, more, (rows, held, sums, sems) = refs[:n], refs[n:-4], refs[-4:]
+    n_rows, _ = rows.shape
     width = held.shape[2]
     size = n_rows // n
-    step = depth // n_chunks
     slab = lax.axis_index("slab")
     x, y = slab % 2, (slab // 2) % 2
 
     def slot(key):
         return pl.ds(pl.multiple_of(((y + key[1]) % 2 * 2 + (x + key[0]) % 2) * size, 32), size)
 
-    copies, index = [], 0
-    for c in range(n_chunks):
+    copies, index, loaded = [], 0, set()
+    for k, begin, end in steps:
         group = []
-        for k, turn in enumerate(turn_plan):
-            for p, first, count, begin in turn:
-                low, high = max(begin, c * step), min(begin + count, (c + 1) * step)
-                if low < high:
-                    source = ins[p].at[pl.ds(first + low - begin, high - low)]
-                    group.append(pltpu.make_async_copy(source, held.at[k, pl.ds(low, high - low)], sems.at[index]))
-                    index += 1
-        for p, first, count, place in plan:
-            columns = pl.ds(c * step, step)
-            source = ins[p].at[pl.ds(first, count), columns]
-            group.append(pltpu.make_async_copy(source, rows.at[pl.ds(place, count), columns], sems.at[index]))
-            index += 1
+        for p, first, count, place in turn_plan[k]:
+            low, high = max(place, begin), min(place + count, end)
+            if low < high:
+                source = ins[p].at[pl.ds(first + low - place, high - low)]
+                group.append(pltpu.make_async_copy(source, held.at[k, pl.ds(low, high - low)], sems.at[index]))
+                index += 1
+        if not any(low <= begin and end <= high for low, high in loaded):
+            loaded.add((begin, end))
+            loaded.update([(low, end) for low, high in loaded if high == begin])
+            for p, first, count, place in plan:
+                columns = pl.ds(begin, end - begin)
+                source = ins[p].at[pl.ds(first, count), columns]
+                group.append(pltpu.make_async_copy(source, rows.at[pl.ds(place, count), columns], sems.at[index]))
+                index += 1
         copies.append(group)
     for group in copies[:2]:
         for copy in group:
             copy.start()
     shift = before[0].shape[1] if given else 0
     for value, key in zip(ready, ready_keys):
-        together[0][slot(key), :] = value[...]
-    for c, group in enumerate(copies):
-        for copy in group:
+        more[0][slot(key), :] = value[...]
+    last = {k: i for i, (k, _, _) in enumerate(steps)}
+    started = set(range(n_begun))
+    for i, (k, begin, end) in enumerate(steps):
+        for copy in copies[i]:
             copy.wait()
-        for copy in copies[c + 2] if c + 2 < n_chunks else []:
+        for copy in copies[i + 2] if i + 2 < len(steps) else []:
             copy.start()
-        if given and not c:
-            for i, out in enumerate(outs):
-                out[:, :shift] = before[i][...]
-        for k in range(len(turn_plan)):
-            columns = slice(k * width, (k + 1) * width)
-            value = jnp.dot(
-                rows[:, c * step : (c + 1) * step],
-                held[k, c * step : (c + 1) * step],
-                preferred_element_type=jnp.float32,
-            )
-            if c:
-                value = value + sums[:, columns]
-            if c < n_chunks - 1:
-                sums[:, columns] = value
-            else:
-                value = value.astype(jnp.bfloat16)
-                for i, out in enumerate(outs):
-                    out[:, shift + k * width : shift + (k + 1) * width] = value[i * size : (i + 1) * size]
+        if given and not i:
+            for out, value in zip(outs, before):
+                out[:, :shift] = value[...]
+        columns = slice(k * width, (k + 1) * width)
+        value = jnp.dot(rows[:, begin:end], held[k, begin:end], preferred_element_type=jnp.float32)
+        if k in started:
+            value = value + (begun[k][...] if k < n_begun and (k, 0) not in started else sums[:, columns])
+            started.add((k, 0))
+        started.add(k)
+        if i < last[k]:
+            sums[:, columns] = value
+            started.add((k, 0))
+        elif k >= n_done:
+            more[-1][...] = value
+        else:
+            value = value.astype(jnp.bfloat16)
+            for j, out in enumerate(outs):
+                out[:, shift + k * width : shift + (k + 1) * width] = value[j * size : (j + 1) * size]
     for out, key in zip(outs, keys):
         if key is not None:
-            together[0][slot(key), :] = out[...]
-
-
-def fold(blocks, turns, before=(), keys=None, ready=()):
+            more[0][slot(key), :] = out[...]
+
+
+def fold(blocks, turns, steps, before=(), keys=None, ready=(), begun=(), n_done=None):
     arrays, plan, turn_plan, place = [], [], [], 0
 
     def operand(value):
@@ -151,23 +155,25 @@
             plan.append((operand(value), first, count, place))
             place += count
     for turn in turns:
-        begins = [sum(count for _, _, count in turn[:i]) for i in range(len(turn))]
-        turn_plan.append([(operand(v), first, count, begin) for (v, first, count), begin in zip(turn, begins)])
+        turn_plan.append([(operand(v), first, count, begin) for v, first, count, begin in turn])
     depth, width = blocks[0][0][0].shape[1], turns[0][0][0].shape[1]
-    n, t, n_chunks = len(blocks), len(turns), 4
-    size, all_width = place // n, t * width + (before[0].shape[1] if before else 0)
-    n_copies = n_chunks * (len(plan) + 2 * sum(len(turn) for turn in turn_plan))
+    n, t = len(blocks), len(turns)
+    n_done = t if n_done is None else n_done
+    size, all_width = place // n, n_done * width + (before[0].shape[1] if before else 0)
+    n_copies = len(steps) * (len(plan) + sum(len(turn) for turn in turn_plan))
     shapes = [jax.ShapeDtypeStruct((size, all_width), jnp.bfloat16)] * n
     if keys:
         shapes.append(jax.ShapeDtypeStruct((4 * size, all_width), jnp.bfloat16))
+    if n_done < t:
+        shapes.append(jax.ShapeDtypeStruct((place, width), jnp.float32))
     ready_values, ready_keys = [v for v, _ in ready], [k for _, k in ready]
     out = pl.pallas_call(
         functools.partial(
-            fold_kernel, plan, turn_plan, n_chunks, keys or [None] * n, ready_keys, len(before)
+            fold_kernel, plan, turn_plan, steps, n_done, keys or [None] * n, ready_keys, len(begun), len(before)
         ),
         out_shape=shapes,
         in_specs=[pl.BlockSpec(memory_space=pltpu.HBM)] * len(arrays)
-        + [pl.BlockSpec(memory_space=pltpu.VMEM)] * (len(before) + len(ready)),
+        + [pl.BlockSpec(memory_space=pltpu.VMEM)] * (len(begun) + len(before) + len(ready)),
         out_specs=[pl.BlockSpec(memory_space=pltpu.VMEM)] * len(shapes),
         scratch_shapes=[
             pltpu.VMEM((place, depth), jnp.bfloat16),
@@ -177,8 +183,8 @@
         ],
         compiler_params=pltpu.CompilerParams(vmem_limit_bytes=60 * 1024 * 1024),
         cost_estimate=pl.CostEstimate(flops=1024, bytes_accessed=1024, transcendentals=0),
-    )(*arrays, *before, *ready_values)
-    return (out[:-1], out[-1]) if keys else out
+    )(*arrays, *begun, *before, *ready_values)
+    return out[:n], out[n:]
 
 
 def place_kernel(plan, width, *refs):
@@ -280,7 +286,11 @@
         )
     )
     cut = 3 * low // 5
-    own_turn = [(turn, 0, depth), (turn_swapped, 0, depth)]
+    own_turn = [(turn, 0, depth, 0), (turn_swapped, 0, depth, depth)]
+    quarters = [(i * depth // 2, (i + 1) * depth // 2) for i in range(4)]
+    swapped_a, swapped_b = swap_cores(piece_a), swap_cores(piece_b)
+    places = cuts[:3] + [depth + cut for cut in cuts[:3]]
+    other_turn = [(v, 0, p.shape[0], q) for v, p, q in zip([piece_a, piece_b, swapped_a, swapped_b], (pieces[:2]) * 2, [places[i] for i in (0, 1, 3, 4)])]
     early = [
         [(rows, 0, half)],
         [(near_x, 0, half)],
@@ -288,14 +298,34 @@
         [(by_y, 0, low), (by_x, 0, low)],
         [(far_low, 0, low), (far_high, 0, low)],
     ]
-    early_own, piece_c = tie((fold(early, [own_turn]), move(last_piece, dz=1)))
-    by_x3, by_y3, swapped_a, swapped_b, swapped_c = tie(
+    (early_own, early_sums), piece_c = tie(
+        (
+            fold(
+                early,
+                [own_turn, other_turn],
+                [(0,) + q for q in quarters] + [(1, 0, cuts[2]), (1, depth, depth + cuts[2])],
+                n_done=1,
+            ),
+            move(last_piece, dz=1),
+        )
+    )
+    swapped_c = swap_cores(piece_c)
+    last_turn = [(piece_c, 0, depth - cuts[2], cuts[2]), (swapped_c, 0, depth - cuts[2], depth + cuts[2])]
+    by_x3, by_y3, swapped_a, swapped_b, swapped_c, (early_rows, (near_rows,)) = tie(
         (
             move(jnp.concatenate([far_high, by_y[2 * low - cut :]]), dx=1),
             move(jnp.concatenate([far_high, by_x[low : low + cut]]), dy=1),
-            swap_cores(piece_a),
-            swap_cores(piece_b),
-            swap_cores(piece_c),
+            swapped_a,
+            swapped_b,
+            swapped_c,
+            fold(
+                early,
+                [last_turn],
+                [(0, cuts[2], depth), (0, depth + cuts[2], 2 * depth)],
+                early_own,
+                NEAR + [None],
+                begun=early_sums,
+            ),
         )
     )
     first = pieces[0].shape[0]
@@ -305,12 +335,13 @@
     widened = checks.astype(jnp.float32)
     squares = jnp.sum(widened * widened, axis=1)
     arrived = [piece_a, piece_b, piece_c, swapped_a, swapped_b, swapped_c]
-    turn_other = [(v, 0, p.shape[0]) for v, p in zip(arrived, pieces + pieces)]
-    by_y4, by_x4, (early_rows, near_rows) = tie(
+    other_turn = [(v, 0, p.shape[0], q) for v, p, q in zip(arrived, pieces + pieces, places)]
+    by_y4, by_x4, received_first, early_rows = tie(
         (
             move(by_x3[: low - cut], dy=1),
             move(by_y3[low - cut : low], dx=1),
-            fold(early, [turn_other], early_own, NEAR + [None]),
+            spread(early_rows[:1], 0),
+            early_rows,
         )
     )
     late = [
@@ -318,13 +349,21 @@
         [(by_y, low, low), (by_y3, 0, low)],
         [(by_y3, low, cut), (by_x3, 2 * cut, low - cut), (by_y4, 0, low - cut), (by_x4, 0, cut)],
     ]
-    received_near, received_far, (late_rows, far_rows) = tie(
-        (
-            spread(early_rows[:4], 0),
+    received_near, received_far, (late_rows, (far_rows,)) = tie(
+        (
+            spread(early_rows[1:4], 0, NEAR[1:]),
             spread(early_rows[4:], 1),
-            fold(late, [own_turn, turn_other], (), NEAR[1:], [(early_rows[4], NEAR[0])]),
-        )
-    )
+            fold(
+                late,
+                [own_turn, other_turn],
+                [(k,) + q for q in quarters for k in range(2)],
+                (),
+                NEAR[1:],
+                [(early_rows[4], NEAR[0])],
+            ),
+        )
+    )
+    received_near = received_first + received_near
     products = jnp.concatenate([check(near_rows), check(far_rows)], axis=1)
 
     def quarter(value, dx, dy):

time: 309 us -> 307 us (level)
  starting transfers between devices: 47.8 us -> 42.1 us
    ppermute x18, waiting for transfers between devices: 146 us -> 154 us  [move(): return lax.ppermute(value, 'slab', pairs)]
    ppermute x8, starting transfers between devices: 22.5 us -> 17.9 us  [send_rows(): return lax.ppermute(value, ('slab', 'panel'), pairs)]
    ppermute x6, waiting for transfers between devices: 8.48 us -> 5.16 us  [swap_cores(): return lax.ppermute(value, 'panel', [(0, 1), (1, 0)])]
    unnamed x58 -> x48, local copies, waits for them, and re-layouts: 5.77 us -> 6.33 us
  transfers between devices with their start and end apart: 32 -> 32, of which waited for: 14 -> 15; matrix products, arithmetic and copies ran while one was open for 6% -> 6% of each run, Pallas kernels for 14% -> 14%
where the time goes in v3:
time: 307 us; the launch traced here: 306 us
  waiting for transfers between devices  185 us (60%)
  Pallas kernels  42.5 us (14%)
  starting transfers between devices  42.1 us (14%)
  local copies, waits for them, and re-layouts  17.7 us (6%)
  other arithmetic  13.1 us (4%)
  matrix products  4.74 us (2%)
    ppermute x18, waiting for transfers between devices, move(): return lax.ppermute(value, 'slab', pairs)  154 us
    pallas_call x3, Pallas kernels, fold(): pl.pallas_call(functools.partial(fold_kernel, plan, turn_plan, steps, n_d...  39.1 us
    ppermute x8, waiting for transfers between devices, send_rows(): return lax.ppermute(value, ('slab', 'panel'), pairs)  25.6 us
    ppermute x18, starting transfers between devices, move(): return lax.ppermute(value, 'slab', pairs)  23 us
    ppermute x8, starting transfers between devices, send_rows(): return lax.ppermute(value, ('slab', 'panel'), pairs)  17.9 us
    unnamed x48, local copies, waits for them, and re-layouts  6.33 us
  transfers between devices with their start and end apart: 32, of which 15 were waited for; matrix products, arithmetic and copies ran while one was open for 6% of the time, Pallas kernels for 14%

profile of v3, /device:TPU:0, one launch (start us, length us, event | category | flops | bytes accessed | tf_op | source)
XLA Modules:
  0.0 305.8 jit_solution(6131944047728080615)
XLA Ops:
  0.6 3.0 constant_dynamic-slice_fusion.3
  4.1 1.1 copy.34
  5.3 1.8 multiply_convert_fusion.1
  7.2 2.6 collective-permute-start.4
  10.1 1.6 collective-permute-start.1
  11.6 1.5 collective-permute-start.2
  13.3 2.7 collective-permute-start.3
  16.8 1.6 slice.88
  19.3 39.5 %collective-permute-done.4.refs_9_.refs_8_ = bf16[1152,512]{1,0:T(8,128)(2,1)S(1)} collective-permute-done((bf16[1152,512]{1,0:T(8,128)(2,1)S(1)}, bf16[1152,512]{1,0:T(8,128)(2,1)S(1)}, u32[]{:S(2)}, u32[]{:S(2)}) %collective-permute-start.4) | collective-permute-done | bytes 1179680 | tf_op jit(solution)/shard_map/ppermute | solution.py:53
  58.7 14.1 %collective-permute-done.3.refs_5_ = bf16[80,8192]{1,0:T(8,128)(2,1)S(1)} collective-permute-done((bf16[80,8192]{1,0:T(8,128)(2,1)S(1)}, bf16[80,8192]{1,0:T(8,128)(2,1)S(1)}, u32[]{:S(2)}, u32[]{:S(2)}) %collective-permute-start.3) | collective-permute-done | bytes 1310752 | tf_op jit(solution)/shard_map/ppermute | solution.py:53
  72.8 2.3 copy-done.6
  76.5 1.2 collective-permute-start.6
  77.7 3.0 collective-permute-start.7
  80.8 55.2 %collective-permute-done.7.refs_6_ = bf16[80,8192]{1,0:T(8,128)(2,1)S(1)} collective-permute-done((bf16[80,8192]{1,0:T(8,128)(2,1)S(1)}, bf16[80,8192]{1,0:T(8,128)(2,1)S(1)}, u32[]{:S(2)}, u32[]{:S(2)}) %collective-permute-start.7) | collective-permute-done | bytes 1310752 | tf_op jit(solution)/shard_map/ppermute | solution.py:53
  136.0 2.2 collective-permute-done.8.refs_10_.refs_9_
  138.2 1.4 collective-permute-start.14
  140.1 1.6 copy-done.2
  141.8 2.6 pad_maximum_fusion.3
  144.8 1.4 collective-permute-start.11
  147.2 15.5 %shard_map.59 = (bf16[160,512]{1,0:T(8,128)(2,1)}, bf16[160,512]{1,0:T(8,128)(2,1)}, bf16[160,512]{1,0:T(8,128)(2,1)}, bf16[160,512]{1,0:T(8,128)(2,1)}, bf16[160,512]{1,0:T(8,128)(2,1)}, /*index=5*/f32[800,512]{1,0:T(8,128)}) custom-call(bf16[160,8192]{1,0:T(8,128)(2,1)} %copy-done.3, bf16[160,8192]{1,0:T(8,128)(2,1)} %copy-done.5, ...), custom_call_target="tpu_custom_call" | custom-call | flops 1024 | bytes 1024 | tf_op jit(solution)/shard_map/pallas_call | solution.py:170
  162.7 16.6 %collective-permute-done.14.refs_7_.refs_10_ = bf16[1792,512]{1,0:T(8,128)(2,1)S(1)} collective-permute-done((bf16[1792,512]{1,0:T(8,128)(2,1)}, bf16[1792,512]{1,0:T(8,128)(2,1)S(1)}, u32[]{:S(2)}, u32[]{:S(2)}) %collective-permute-start.14) | collective-permute-done | bytes 1835040 | tf_op jit(solution)/shard_map/ppermute | solution.py:53
  179.3 3.9 %collective-permute-done.15.refs_8_.refs_13_ = bf16[1792,512]{1,0:T(8,128)(2,1)} collective-permute-done((bf16[1792,512]{1,0:T(8,128)(2,1)S(1)}, bf16[1792,512]{1,0:T(8,128)(2,1)}, u32[]{:S(2)}, u32[]{:S(2)}) %collective-permute-start.15) | collective-permute-done | bytes 1835040 | tf_op jit(solution)/shard_map/ppermute | solution.py:57
  183.2 9.0 %shard_map.60 = (bf16[160,1024]{1,0:T(8,128)(2,1)}, bf16[160,1024]{1,0:T(8,128)(2,1)}, bf16[160,1024]{1,0:T(8,128)(2,1)}, bf16[160,1024]{1,0:T(8,128)(2,1)}, bf1...) custom-call(bf16[160,8192]{1,0:T(8,128)(2,1)} %copy-done.3, bf16[160,8192]{1,0:T(8,128)(2,1)} %copy-done.5, ...), custom_call_target="tpu_custom_call" | custom-call | flops 1024 | bytes 1024 | tf_op jit(solution)/shard_map/pallas_call | solution.py:170
  192.2 1.2 slice.76
  194.2 1.1 slice.75
  195.3 1.1 collective-permute-start.16
  196.4 1.6 collective-permute-start.18
  198.0 1.1 broadcast_select_fusion.1
  199.5 11.5 %collective-permute-done.16.refs_4_ = bf16[32,8192]{1,0:T(8,128)(2,1)S(1)} collective-permute-done((bf16[32,8192]{1,0:T(8,128)(2,1)S(1)}, bf16[32,8192]{1,0:T(8,128)(2,1)S(1)}, u32[]{:S(2)}, u32[]{:S(2)}) %collective-permute-start.16) | collective-permute-done | bytes 524320 | tf_op jit(solution)/shard_map/ppermute | solution.py:53
  211.1 5.5 %collective-permute-done.17.refs_5_ = bf16[48,8192]{1,0:T(8,128)(2,1)S(1)} collective-permute-done((bf16[48,8192]{1,0:T(8,128)(2,1)S(1)}, bf16[48,8192]{1,0:T(8,128)(2,1)S(1)}, u32[]{:S(2)}, u32[]{:S(2)}) %collective-permute-start.17) | collective-permute-done | bytes 786464 | tf_op jit(solution)/shard_map/ppermute | solution.py:53
  216.6 5.7 %collective-permute-start.19 = (bf16[160,1024]{1,0:T(8,128)(2,1)}, bf16[160,1024]{1,0:T(8,128)(2,1)}, u32[]{:S(2)}, u32[]{:S(2)}) collective-permute-start(bf16[160,1024]{1,0:T(8,128)(2,1)} %get-tuple-element.114), channel_id=1, source_target_pairs={{0,4},{1,6},{2,0},{3,2},{4,12},{5,14},{6,8},{7,10},{8,20},{9,22},{... | collective-permute-start | bytes 983048 | tf_op jit(solution)/shard_map/ppermute | solution.py:66
  222.3 2.6 collective-permute-start.21
  226.1 2.3 fusion.21
  228.4 14.6 %shard_map.61 = (bf16[160,1024]{1,0:T(8,128)(2,1)}, bf16[160,1024]{1,0:T(8,128)(2,1)}, bf16[160,1024]{1,0:T(8,128)(2,1)}, bf16[640,1024]{1,0:T(8,128)(2,1)}) custom-call(bf16[160,8192]{1,0:T(8,128)(2,1)} %copy-done.1, bf16[128,8192]{1,0:T(8,128)(2,1)} %collective-permute-done.10.refs_1_, bf16[160,8192]{1,0:T(8,128)(2,1)} %copy-done.2, ...), custom_call_target="tpu_custom_call" | custom-call | flops 1024 | bytes 1024 | tf_op jit(solution)/shard_map/pallas_call | solution.py:170
  243.1 7.0 %collective-permute-done.22.refs_4_ = bf16[160,1024]{1,0:T(8,128)(2,1)} collective-permute-done((bf16[160,1024]{1,0:T(8,128)(2,1)}, bf16[160,1024]{1,0:T(8,128)(2,1)}, u32[]{:S(2)}, u32[]{:S(2)}) %collective-permute-start.22) | collective-permute-done | bytes 327712 | tf_op jit(solution)/shard_map/ppermute | solution.py:66
  250.1 2.4 fusion.20
  254.2 1.5 collective-permute-start.24
  256.4 2.0 collective-permute-start.23
  258.4 1.9 collective-permute-start.26
  260.3 4.0 %collective-permute-start.27 = (bf16[160,1024]{1,0:T(8,128)(2,1)}, bf16[160,1024]{1,0:T(8,128)(2,1)}, u32[]{:S(2)}, u32[]{:S(2)}) collective-permute-start(bf16[160,1024]{1,0:T(8,128)(2,1)} %get-tuple-element.134), channel_id=1, source_target_pairs={{0,9},{1,11},{2,13},{3,15},{4,1},{5,3},{6,5},{7,7},{8,25},{9,27},{... | collective-permute-start | bytes 983048 | tf_op jit(solution)/shard_map/ppermute | solution.py:66
  264.4 8.7 %collective-permute-done.26.refs_5_ = bf16[160,1024]{1,0:T(8,128)(2,1)} collective-permute-done((bf16[160,1024]{1,0:T(8,128)(2,1)}, bf16[160,1024]{1,0:T(8,128)(2,1)}, u32[]{:S(2)}, u32[]{:S(2)}) %collective-permute-start.26) | collective-permute-done | bytes 327712 | tf_op jit(solution)/shard_map/ppermute | solution.py:66
  273.1 4.6 %collective-permute-done.27.refs_6_ = bf16[160,1024]{1,0:T(8,128)(2,1)} collective-permute-done((bf16[160,1024]{1,0:T(8,128)(2,1)}, bf16[160,1024]{1,0:T(8,128)(2,1)}, u32[]{:S(2)}, u32[]{:S(2)}) %collective-permute-start.27) | collective-permute-done | bytes 327712 | tf_op jit(solution)/shard_map/ppermute | solution.py:66
  277.7 1.1 convert_add_fusion
  280.6 1.9 collective-permute-start.29
  282.5 8.8 %collective-permute-done.28 = bf16[64,1408]{1,0:T(8,128)(2,1)S(1)} collective-permute-done((bf16[64,1408]{1,0:T(8,128)(2,1)S(1)}, bf16[64,1408]{1,0:T(8,128)(2,1)S(1)}, u32[]{:S(2)}, u32[]{:S(2)}) %collective-permute-start.28) | collective-permute-done | bytes 180256 | tf_op jit(solution)/shard_map/ppermute | solution.py:53
  292.6 5.3 %collective-permute-done.29.refs_7_ = bf16[160,1024]{1,0:T(8,128)(2,1)S(1)} collective-permute-done((bf16[160,1024]{1,0:T(8,128)(2,1)S(1)}, bf16[160,1024]{1,0:T(8,128)(2,1)S(1)}, u32[]{:S(2)}, u32[]{:S(2)}) %collective-permute-start.29) | collective-permute-done | bytes 327712 | tf_op jit(solution)/shard_map/ppermute | solution.py:66
  298.1 1.2 collective-permute-done.30
  300.3 3.4 %shard_map.62 = bf16[160,8192]{1,0:T(8,128)(2,1)} custom-call(bf16[160,1024]{1,0:T(8,128)(2,1)} %copy-done.17, bf16[160,1024]{1,0:T(8,128)(2,1)} %collective-permute-done.19.refs_1_, bf16[160,1024]{1,0:T(8,128)(2,1)} %collective-permute-done.20.refs_2_, bf16[160,1024]{1,0:T(8,128)(2,1)} %collective-permute-done.21.refs_3_, ...), custom_call_target="tpu_custom_call" | custom-call | flops 1024 | bytes 1024 | tf_op jit(solution)/shard_map/pallas_call | solution.py:209
  (131 shorter events, 17.0 us)
Async XLA Ops:
  0.6 4.6 %copy-start.20 = (f32[8192]{0:T(1024)S(1)}, f32[8192]{0:T(1024)}, u32[]{:S(2)}) copy-start(f32[8192]{0:T(1024)} %param.5) | copy-start | bytes 98308
  3.7 6.2 %collective-permute-start = (bf16[160,4096]{1,0:T(8,128)(2,1)}, bf16[160,4096]{1,0:T(8,128)(2,1)S(1)}, u32[]{:S(2)}, u32[]{:S(2)}) collective-permute-start(bf16[160,4096]{1,0:T(8,128)(2,1)} %get-tuple-element.150), channel_id=1, source_target_pairs={{0,1},{1,0},{2,3},{3,2},{4,5},{5,4},{6,7},{7,6},{8,9},{9,8},{10,11... | collective-permute-start | bytes 3932168 | tf_op jit(solution)/shard_map/ppermute | solution.py:57
  5.3 10.7 %slice-start = ((s8[8388608]{0:T(1024)(128)(4,1)}), s8[4194304]{0:T(1024)(128)(4,1)S(1)}, s32[]{:S(2)}) async-start(s8[8388608]{0:T(1024)(128)(4,1)} %bitcast.35), calls=%async_computation | async-start | bytes 8388608
  7.2 51.5 %collective-permute-start.4 = (bf16[1152,512]{1,0:T(8,128)(2,1)S(1)}, bf16[1152,512]{1,0:T(8,128)(2,1)S(1)}, u32[]{:S(2)}, u32[]{:S(2)}) collective-permute-start(bf16[1152,512]{1,0:T(8,128)(2,1)S(1)} %pad_maximum_fusion.5), channel_id=1, source_target_pairs={{0,8},{2,10},{4,12},{6,14},{8,0},{10,2},{12,4},{14,6},{16,24},{18,... | collective-permute-start | bytes 3538952 | tf_op jit(solution)/shard_map/ppermute | solution.py:53
  9.9 6.1 %slice-start.1 = ((s8[8388608]{0:T(1024)(128)(4,1)}), s8[4194304]{0:T(1024)(128)(4,1)S(1)}, s32[]{:S(2)}) async-start(s8[8388608]{0:T(1024)(128)(4,1)} %bitcast.35), calls=%async_computation.1 | async-start | bytes 8388608
  10.1 3.3 %copy-start.3 = (bf16[160,8192]{1,0:T(8,128)(2,1)}, bf16[160,8192]{1,0:T(8,128)(2,1)S(1)}, u32[]{:S(2)}) copy-start(bf16[160,8192]{1,0:T(8,128)(2,1)S(1)} %pad_maximum_fusion.refs_0_) | copy-start | bytes 7864324
  10.1 62.7 %collective-permute-start.1 = (bf16[160,8192]{1,0:T(8,128)(2,1)S(1)}, bf16[160,8192]{1,0:T(8,128)(2,1)S(1)}, u32[]{:S(2)}, u32[]{:S(2)}) collective-permute-start(bf16[160,8192]{1,0:T(8,128)(2,1)S(1)} %pad_maximum_fusion.refs_0_), channel_id=1, source_target_pairs={{0,2},{2,0},{4,6},{6,4},{8,10},{10,8},{12,14},{14,12},{16,18},{18,... | collective-permute-start | bytes 7864328 | tf_op jit(solution)/shard_map/ppermute | solution.py:53
  11.6 61.2 %collective-permute-start.2 = (bf16[160,8192]{1,0:T(8,128)(2,1)S(1)}, bf16[160,8192]{1,0:T(8,128)(2,1)S(1)}, u32[]{:S(2)}, u32[]{:S(2)}) collective-permute-start(bf16[160,8192]{1,0:T(8,128)(2,1)S(1)} %pad_maximum_fusion.refs_0_), channel_id=1, source_target_pairs={{0,4},{2,6},{4,0},{6,2},{8,12},{10,14},{12,8},{14,10},{16,20},{18,... | collective-permute-start | bytes 7864328 | tf_op jit(solution)/shard_map/ppermute | solution.py:53
  13.3 59.4 %collective-permute-start.3 = (bf16[80,8192]{1,0:T(8,128)(2,1)S(1)}, bf16[80,8192]{1,0:T(8,128)(2,1)S(1)}, u32[]{:S(2)}, u32[]{:S(2)}) collective-permute-start(bf16[80,8192]{1,0:T(8,128)(2,1)S(1)} %get-tuple-element.148), channel_id=1, source_target_pairs={{0,16},{2,18},{4,20},{6,22},{8,24},{10,26},{12,28},{14,30},{16,0},... | collective-permute-start | bytes 3932168 | tf_op jit(solution)/shard_map/ppermute | solution.py:53
  16.8 121.4 %collective-permute-start.9 = (bf16[4096,512]{1,0:T(8,128)(2,1)S(1)}, bf16[4096,512]{1,0:T(8,128)(2,1)S(1)}, u32[]{:S(2)}, u32[]{:S(2)}) collective-permute-start(bf16[4096,512]{1,0:T(8,128)(2,1)S(1)} %multiply_convert_fusion.refs_7_.refs_6_), channel_id=1, source_target_pairs={{0,1},{1,0},{2,3},{3,2},{4,5},{5,4},{6,7},{7,6},{8,9},{9,8},{10,11... | collective-permute-start | bytes 12582920 | tf_op jit(solution)/shard_map/ppermute | solution.py:57
  58.7 80.9 %copy-start.10 = (bf16[1152,512]{1,0:T(8,128)(2,1)}, bf16[1152,512]{1,0:T(8,128)(2,1)S(1)}, u32[]{:S(2)}) copy-start(bf16[1152,512]{1,0:T(8,128)(2,1)S(1)} %collective-permute-done.4.refs_9_.refs_8_) | copy-start | bytes 3538948
  72.8 3.1 %copy-start.7 = (bf16[80,8192]{1,0:T(8,128)(2,1)}, bf16[80,8192]{1,0:T(8,128)(2,1)S(1)}, u32[]{:S(2)}) copy-start(bf16[80,8192]{1,0:T(8,128)(2,1)S(1)} %collective-permute-done.3.refs_5_) | copy-start | bytes 3932164
  75.9 62.2 %collective-permute-start.5 = (bf16[160,8192]{1,0:T(8,128)(2,1)S(1)}, bf16[160,8192]{1,0:T(8,128)(2,1)S(1)}, u32[]{:S(2)}, u32[]{:S(2)}) collective-permute-start(bf16[160,8192]{1,0:T(8,128)(2,1)S(1)} %get-tuple-element.156), channel_id=1, source_target_pairs={{0,2},{2,0},{4,6},{6,4},{8,10},{10,8},{12,14},{14,12},{16,18},{18,... | collective-permute-start | bytes 7864328 | tf_op jit(solution)/shard_map/ppermute | solution.py:53
  76.5 61.6 %collective-permute-start.6 = (bf16[160,8192]{1,0:T(8,128)(2,1)S(1)}, bf16[160,8192]{1,0:T(8,128)(2,1)S(1)}, u32[]{:S(2)}, u32[]{:S(2)}) collective-permute-start(bf16[160,8192]{1,0:T(8,128)(2,1)S(1)} %get-tuple-element.155), channel_id=1, source_target_pairs={{0,4},{2,6},{4,0},{6,2},{8,12},{10,14},{12,8},{14,10},{16,20},{18,... | collective-permute-start | bytes 7864328 | tf_op jit(solution)/shard_map/ppermute | solution.py:53
  77.7 60.4 %collective-permute-start.8 = (bf16[1408,512]{1,0:T(8,128)(2,1)S(1)}, bf16[1408,512]{1,0:T(8,128)(2,1)S(1)}, u32[]{:S(2)}, u32[]{:S(2)}) collective-permute-start(bf16[1408,512]{1,0:T(8,128)(2,1)S(1)} %slice.87), channel_id=1, source_target_pairs={{0,8},{2,10},{4,12},{6,14},{8,0},{10,2},{12,4},{14,6},{16,24},{18,... | collective-permute-start | bytes 4325384 | tf_op jit(solution)/shard_map/ppermute | solution.py:53
  77.7 58.2 %collective-permute-start.7 = (bf16[80,8192]{1,0:T(8,128)(2,1)S(1)}, bf16[80,8192]{1,0:T(8,128)(2,1)S(1)}, u32[]{:S(2)}, u32[]{:S(2)}) collective-permute-start(bf16[80,8192]{1,0:T(8,128)(2,1)S(1)} %get-tuple-element.147), channel_id=1, source_target_pairs={{0,16},{2,18},{4,20},{6,22},{8,24},{10,26},{12,28},{14,30},{16,0},... | collective-permute-start | bytes 3932168 | tf_op jit(solution)/shard_map/ppermute | solution.py:53
  136.0 11.2 %copy-start.8 = (bf16[80,8192]{1,0:T(8,128)(2,1)}, bf16[80,8192]{1,0:T(8,128)(2,1)S(1)}, u32[]{:S(2)}) copy-start(bf16[80,8192]{1,0:T(8,128)(2,1)S(1)} %collective-permute-done.7.refs_6_) | copy-start | bytes 3932164
  138.2 8.0 %copy-start.12 = (bf16[1408,512]{1,0:T(8,128)(2,1)}, bf16[1408,512]{1,0:T(8,128)(2,1)S(1)}, u32[]{:S(2)}) copy-start(bf16[1408,512]{1,0:T(8,128)(2,1)S(1)} %collective-permute-done.8.refs_10_.refs_9_) | copy-start | bytes 4325380
  138.2 6.2 %copy-start.4 = (bf16[4096,512]{1,0:T(8,128)(2,1)}, bf16[4096,512]{1,0:T(8,128)(2,1)S(1)}, u32[]{:S(2)}) copy-start(bf16[4096,512]{1,0:T(8,128)(2,1)S(1)} %collective-permute-done.9.refs_8_.refs_7_) | copy-start | bytes 12582916
  138.2 6.2 %copy-start.1 = (bf16[160,8192]{1,0:T(8,128)(2,1)}, bf16[160,8192]{1,0:T(8,128)(2,1)S(1)}, u32[]{:S(2)}) copy-start(bf16[160,8192]{1,0:T(8,128)(2,1)S(1)} %collective-permute-done.5.refs_4_.refs_0_) | copy-start | bytes 7864324
  138.2 3.5 %copy-start.2 = (bf16[160,8192]{1,0:T(8,128)(2,1)}, bf16[160,8192]{1,0:T(8,128)(2,1)S(1)}, u32[]{:S(2)}) copy-start(bf16[160,8192]{1,0:T(8,128)(2,1)S(1)} %collective-permute-done.6.refs_3_.refs_2_) | copy-start | bytes 7864324
  138.2 41.1 %collective-permute-start.14 = (bf16[1792,512]{1,0:T(8,128)(2,1)}, bf16[1792,512]{1,0:T(8,128)(2,1)S(1)}, u32[]{:S(2)}, u32[]{:S(2)}) collective-permute-start(bf16[1792,512]{1,0:T(8,128)(2,1)} %slice.88), channel_id=1, source_target_pairs={{0,8},{2,10},{4,12},{6,14},{8,0},{10,2},{12,4},{14,6},{16,24},{18,... | collective-permute-start | bytes 5505032 | tf_op jit(solution)/shard_map/ppermute | solution.py:53
  139.6 7.6 %collective-permute-start.13 = (bf16[1408,512]{1,0:T(8,128)(2,1)S(1)}, bf16[1408,512]{1,0:T(8,128)(2,1)}, u32[]{:S(2)}, u32[]{:S(2)}) collective-permute-start(bf16[1408,512]{1,0:T(8,128)(2,1)S(1)} %collective-permute-done.8.refs_10_.refs_9_), channel_id=1, source_target_pairs={{0,1},{1,0},{2,3},{3,2},{4,5},{5,4},{6,7},{7,6},{8,9},{9,8},{10,11... | collective-permute-start | bytes 4325384 | tf_op jit(solution)/shard_map/ppermute | solution.py:57
  139.6 6.5 %collective-permute-start.12 = (bf16[1152,512]{1,0:T(8,128)(2,1)S(1)}, bf16[1152,512]{1,0:T(8,128)(2,1)S(1)}, u32[]{:S(2)}, u32[]{:S(2)}) collective-permute-start(bf16[1152,512]{1,0:T(8,128)(2,1)S(1)} %collective-permute-done.4.refs_9_.refs_8_), channel_id=1, source_target_pairs={{0,1},{1,0},{2,3},{3,2},{4,5},{5,4},{6,7},{7,6},{8,9},{9,8},{10,11... | collective-permute-start | bytes 3538952 | tf_op jit(solution)/shard_map/ppermute | solution.py:57
  144.4 47.8 %collective-permute-start.10 = (bf16[128,8192]{1,0:T(8,128)(2,1)}, bf16[128,8192]{1,0:T(8,128)(2,1)}, u32[]{:S(2)}, u32[]{:S(2)}) collective-permute-start(bf16[128,8192]{1,0:T(8,128)(2,1)} %get-tuple-element.154), channel_id=1, source_target_pairs={{0,2},{2,0},{4,6},{6,4},{8,10},{10,8},{12,14},{14,12},{16,18},{18,... | collective-permute-start | bytes 6291464 | tf_op jit(solution)/shard_map/ppermute | solution.py:53
  144.8 47.5 %collective-permute-start.11 = (bf16[128,8192]{1,0:T(8,128)(2,1)}, bf16[128,8192]{1,0:T(8,128)(2,1)}, u32[]{:S(2)}, u32[]{:S(2)}) collective-permute-start(bf16[128,8192]{1,0:T(8,128)(2,1)} %get-tuple-element.153), channel_id=1, source_target_pairs={{0,4},{2,6},{4,0},{6,2},{8,12},{10,14},{12,8},{14,10},{16,20},{18,... | collective-permute-start | bytes 6291464 | tf_op jit(solution)/shard_map/ppermute | solution.py:53
  179.3 3.9 %copy-start.9 = (bf16[1792,512]{1,0:T(8,128)(2,1)}, bf16[1792,512]{1,0:T(8,128)(2,1)S(1)}, u32[]{:S(2)}) copy-start(bf16[1792,512]{1,0:T(8,128)(2,1)S(1)} %collective-permute-done.14.refs_7_.refs_10_) | copy-start | bytes 5505028
  179.3 3.9 %collective-permute-start.15 = (bf16[1792,512]{1,0:T(8,128)(2,1)S(1)}, bf16[1792,512]{1,0:T(8,128)(2,1)}, u32[]{:S(2)}, u32[]{:S(2)}) collective-permute-start(bf16[1792,512]{1,0:T(8,128)(2,1)S(1)} %collective-permute-done.14.refs_7_.refs_10_), channel_id=1, source_target_pairs={{0,1},{1,0},{2,3},{3,2},{4,5},{5,4},{6,7},{7,6},{8,9},{9,8},{10,11... | collective-permute-start | bytes 5505032 | tf_op jit(solution)/shard_map/ppermute | solution.py:57
  193.4 23.2 %collective-permute-start.17 = (bf16[48,8192]{1,0:T(8,128)(2,1)S(1)}, bf16[48,8192]{1,0:T(8,128)(2,1)S(1)}, u32[]{:S(2)}, u32[]{:S(2)}) collective-permute-start(bf16[48,8192]{1,0:T(8,128)(2,1)S(1)} %slice.76), channel_id=1, source_target_pairs={{0,2},{2,0},{4,6},{6,4},{8,10},{10,8},{12,14},{14,12},{16,18},{18,... | collective-permute-start | bytes 2359304 | tf_op jit(solution)/shard_map/ppermute | solution.py:53
  195.3 15.8 %collective-permute-start.16 = (bf16[32,8192]{1,0:T(8,128)(2,1)S(1)}, bf16[32,8192]{1,0:T(8,128)(2,1)S(1)}, u32[]{:S(2)}, u32[]{:S(2)}) collective-permute-start(bf16[32,8192]{1,0:T(8,128)(2,1)S(1)} %slice.75), channel_id=1, source_target_pairs={{0,4},{2,6},{4,0},{6,2},{8,12},{10,14},{12,8},{14,10},{16,20},{18,... | collective-permute-start | bytes 1572872 | tf_op jit(solution)/shard_map/ppermute | solution.py:53
  196.4 3.2 %collective-permute-start.18 = (bf16[160,1024]{1,0:T(8,128)(2,1)}, bf16[160,1024]{1,0:T(8,128)(2,1)S(1)}, u32[]{:S(2)}, u32[]{:S(2)}) collective-permute-start(bf16[160,1024]{1,0:T(8,128)(2,1)} %get-tuple-element.108), channel_id=1, source_target_pairs={{0,0},{1,2},{2,4},{3,6},{4,8},{5,10},{6,12},{7,14},{8,16},{9,18},{... | collective-permute-start | bytes 983048 | tf_op jit(solution)/shard_map/ppermute | solution.py:66
  199.1 29.4 %copy-start.14 = (bf16[256,512]{1,0:T(8,128)(2,1)}, bf16[256,512]{1,0:T(8,128)(2,1)S(1)}, u32[]{:S(2)}) copy-start(bf16[256,512]{1,0:T(8,128)(2,1)S(1)} %get-tuple-element.152) | copy-start | bytes 786436
  199.5 17.0 %copy-start.17 = (bf16[160,1024]{1,0:T(8,128)(2,1)}, bf16[160,1024]{1,0:T(8,128)(2,1)S(1)}, u32[]{:S(2)}) copy-start(bf16[160,1024]{1,0:T(8,128)(2,1)S(1)} %collective-permute-done.18.refs_0_) | copy-start | bytes 983044
  211.1 14.9 %copy-start.16 = (bf16[32,8192]{1,0:T(8,128)(2,1)}, bf16[32,8192]{1,0:T(8,128)(2,1)S(1)}, u32[]{:S(2)}) copy-start(bf16[32,8192]{1,0:T(8,128)(2,1)S(1)} %collective-permute-done.16.refs_4_) | copy-start | bytes 1572868
  216.6 11.9 %copy-start.15 = (bf16[48,8192]{1,0:T(8,128)(2,1)}, bf16[48,8192]{1,0:T(8,128)(2,1)S(1)}, u32[]{:S(2)}) copy-start(bf16[48,8192]{1,0:T(8,128)(2,1)S(1)} %collective-permute-done.17.refs_5_) | copy-start | bytes 2359300
  216.6 26.5 %collective-permute-start.19 = (bf16[160,1024]{1,0:T(8,128)(2,1)}, bf16[160,1024]{1,0:T(8,128)(2,1)}, u32[]{:S(2)}, u32[]{:S(2)}) collective-permute-start(bf16[160,1024]{1,0:T(8,128)(2,1)} %get-tuple-element.114), channel_id=1, source_target_pairs={{0,4},{1,6},{2,0},{3,2},{4,12},{5,14},{6,8},{7,10},{8,20},{9,22},{... | collective-permute-start | bytes 983048 | tf_op jit(solution)/shard_map/ppermute | solution.py:66
  222.3 20.8 %collective-permute-start.20 = (bf16[160,1024]{1,0:T(8,128)(2,1)}, bf16[160,1024]{1,0:T(8,128)(2,1)}, u32[]{:S(2)}, u32[]{:S(2)}) collective-permute-start(bf16[160,1024]{1,0:T(8,128)(2,1)} %get-tuple-element.115), channel_id=1, source_target_pairs={{0,8},{1,10},{2,12},{3,14},{4,0},{5,2},{6,4},{7,6},{8,24},{9,26},{... | collective-permute-start | bytes 983048 | tf_op jit(solution)/shard_map/ppermute | solution.py:66
  222.3 20.8 %collective-permute-start.21 = (bf16[160,1024]{1,0:T(8,128)(2,1)}, bf16[160,1024]{1,0:T(8,128)(2,1)}, u32[]{:S(2)}, u32[]{:S(2)}) collective-permute-start(bf16[160,1024]{1,0:T(8,128)(2,1)} %get-tuple-element.116), channel_id=1, source_target_pairs={{0,12},{1,14},{2,8},{3,10},{4,4},{5,6},{6,0},{7,2},{8,28},{9,30},{... | collective-permute-start | bytes 983048 | tf_op jit(solution)/shard_map/ppermute | solution.py:66
  225.0 25.1 %collective-permute-start.22 = (bf16[160,1024]{1,0:T(8,128)(2,1)}, bf16[160,1024]{1,0:T(8,128)(2,1)}, u32[]{:S(2)}, u32[]{:S(2)}) collective-permute-start(bf16[160,1024]{1,0:T(8,128)(2,1)} %get-tuple-element.117.refs_14_), channel_id=1, source_target_pairs={{0,1},{1,3},{2,5},{3,7},{4,9},{5,11},{6,13},{7,15},{8,17},{9,19},{... | collective-permute-start | bytes 983048 | tf_op jit(solution)/shard_map/ppermute | solution.py:66
  253.4 24.3 %collective-permute-start.25 = (bf16[128,1408]{1,0:T(8,128)(2,1)}, bf16[128,1408]{1,0:T(8,128)(2,1)S(1)}, u32[]{:S(2)}, u32[]{:S(2)}) collective-permute-start(bf16[128,1408]{1,0:T(8,128)(2,1)} %fusion.15), channel_id=1, source_target_pairs={{0,6},{2,4},{4,2},{6,0},{8,14},{10,12},{12,10},{14,8},{16,22},{18,... | collective-permute-start | bytes 1081352 | tf_op jit(solution)/shard_map/ppermute | solution.py:53
  254.2 23.5 %collective-permute-start.24 = (bf16[128,1408]{1,0:T(8,128)(2,1)}, bf16[128,1408]{1,0:T(8,128)(2,1)}, u32[]{:S(2)}, u32[]{:S(2)}) collective-permute-start(bf16[128,1408]{1,0:T(8,128)(2,1)} %fusion.14), channel_id=1, source_target_pairs={{0,4},{2,6},{4,0},{6,2},{8,12},{10,14},{12,8},{14,10},{16,20},{18,... | collective-permute-start | bytes 1081352 | tf_op jit(solution)/shard_map/ppermute | solution.py:53
  256.4 21.3 %collective-permute-start.23 = (bf16[128,1408]{1,0:T(8,128)(2,1)}, bf16[128,1408]{1,0:T(8,128)(2,1)S(1)}, u32[]{:S(2)}, u32[]{:S(2)}) collective-permute-start(bf16[128,1408]{1,0:T(8,128)(2,1)} %fusion.13), channel_id=1, source_target_pairs={{0,2},{2,0},{4,6},{6,4},{8,10},{10,8},{12,14},{14,12},{16,18},{18,... | collective-permute-start | bytes 1081352 | tf_op jit(solution)/shard_map/ppermute | solution.py:53
  258.4 14.6 %collective-permute-start.26 = (bf16[160,1024]{1,0:T(8,128)(2,1)}, bf16[160,1024]{1,0:T(8,128)(2,1)}, u32[]{:S(2)}, u32[]{:S(2)}) collective-permute-start(bf16[160,1024]{1,0:T(8,128)(2,1)} %get-tuple-element.133), channel_id=1, source_target_pairs={{0,5},{1,7},{2,1},{3,3},{4,13},{5,15},{6,9},{7,11},{8,21},{9,23},{... | collective-permute-start | bytes 983048 | tf_op jit(solution)/shard_map/ppermute | solution.py:66
  260.3 17.3 %collective-permute-start.27 = (bf16[160,1024]{1,0:T(8,128)(2,1)}, bf16[160,1024]{1,0:T(8,128)(2,1)}, u32[]{:S(2)}, u32[]{:S(2)}) collective-permute-start(bf16[160,1024]{1,0:T(8,128)(2,1)} %get-tuple-element.134), channel_id=1, source_target_pairs={{0,9},{1,11},{2,13},{3,15},{4,1},{5,3},{6,5},{7,7},{8,25},{9,27},{... | collective-permute-start | bytes 983048 | tf_op jit(solution)/shard_map/ppermute | solution.py:66
  280.0 11.3 %collective-permute-start.28 = (bf16[64,1408]{1,0:T(8,128)(2,1)S(1)}, bf16[64,1408]{1,0:T(8,128)(2,1)S(1)}, u32[]{:S(2)}, u32[]{:S(2)}) collective-permute-start(bf16[64,1408]{1,0:T(8,128)(2,1)S(1)} %fusion.17), channel_id=1, source_target_pairs={{0,16},{2,18},{4,20},{6,22},{8,24},{10,26},{12,28},{14,30},{16,0},... | collective-permute-start | bytes 540680 | tf_op jit(solution)/shard_map/ppermute | solution.py:53
  280.6 17.3 %collective-permute-start.29 = (bf16[160,1024]{1,0:T(8,128)(2,1)S(1)}, bf16[160,1024]{1,0:T(8,128)(2,1)S(1)}, u32[]{:S(2)}, u32[]{:S(2)}) collective-permute-start(bf16[160,1024]{1,0:T(8,128)(2,1)S(1)} %copy-done.21), channel_id=1, source_target_pairs={{0,13},{1,15},{2,9},{3,11},{4,5},{5,7},{6,1},{7,3},{8,29},{9,31},{... | collective-permute-start | bytes 983048 | tf_op jit(solution)/shard_map/ppermute | solution.py:66
  298.0 1.3 collective-permute-start.30
  299.4 4.6 %collective-permute-start.31 = (bf16[32,1280]{1,0:T(8,128)(2,1)S(1)}, bf16[32,1280]{1,0:T(8,128)(2,1)S(1)}, u32[]{:S(2)}, u32[]{:S(2)}) collective-permute-start(bf16[32,1280]{1,0:T(8,128)(2,1)S(1)} %fusion.18), channel_id=1, source_target_pairs={{0,8},{2,10},{4,12},{6,14},{8,0},{10,2},{12,4},{14,6},{16,24},{18,... | collective-permute-start | bytes 245768 | tf_op jit(solution)/shard_map/ppermute | solution.py:53
  (9 other events, 16.9 us)

commit v4 on v3

--- a/solution.py
+++ b/solution.py
@@ -379,17 +379,17 @@
     got = sum(v.astype(jnp.float32) for v in parts)
     sums = quarter(products, 0, 0) + got[:, : 8 * half]
     squares = quarter(squares, 0, 0) + jnp.sum(got[:, 8 * half :], axis=1)
-    sums, squares, received = tie(halve(sums, squares, z_hi, dz=2) + (spread(late_rows[2:], 1, NEAR[3:]),))
-    received_far = received_far + received
-    placed = [((f,) + d, v) for f, values in enumerate((received_near, received_far)) for d, v in zip(NEAR, values)]
-    served = whole_rows(placed, width)
-
+    sums, squares = halve(sums, squares, z_hi, dz=2)
     result = (sums * lax.rsqrt(squares / D + EPS)[:, None] / math.sqrt(D)).astype(jnp.bfloat16)
     keep, give = split(result, 1, z_hi ^ core)
     got = swap_cores(give)
     both = jnp.concatenate([jnp.where(core == 0, keep, got), jnp.where(core == 0, got, keep)], axis=1)
     keep, give = split(both, 0, z_lo)
-    got = move(give, dz=1)
+    keep, got, received = tie((keep, move(give, dz=1), spread(late_rows[2:], 1, NEAR[3:])))
+    received_far = received_far + received
+    placed = [((f,) + d, v) for f, values in enumerate((received_near, received_far)) for d, v in zip(NEAR, values)]
+    served = whole_rows(placed, width)
+
     whole = jnp.stack([jnp.where(z_lo == 0, keep, got), jnp.where(z_lo == 0, got, keep)], axis=1)
     qkv = whole.reshape(own_count, 2, 2, 4, half).transpose(0, 1, 3, 2, 4).reshape(own_count, 16 * half)
     return (served[None], qkv)

time: 307 us -> 311 us (1.013)
    ppermute x8, waiting for transfers between devices: 25.6 us -> 29.3 us  [send_rows(): return lax.ppermute(value, ('slab', 'panel'), pairs)]
  transfers between devices with their start and end apart: 32 -> 32, of which waited for: 15 -> 14; matrix products, arithmetic and copies ran while one was open for 6% -> 5% of each run, Pallas kernels for 14% -> 13%
where the time goes in v4:
time: 311 us; the launch traced here: 310 us
  waiting for transfers between devices  188 us (60%)
  Pallas kernels  42.5 us (14%)
  starting transfers between devices  42.3 us (14%)
  local copies, waits for them, and re-layouts  17.7 us (6%)
  other arithmetic  13 us (4%)
  matrix products  4.75 us (2%)
    ppermute x18, waiting for transfers between devices, move(): return lax.ppermute(value, 'slab', pairs)  154 us
    pallas_call x3, Pallas kernels, fold(): pl.pallas_call(functools.partial(fold_kernel, plan, turn_plan, steps, n_d...  39.1 us
    ppermute x8, waiting for transfers between devices, send_rows(): return lax.ppermute(value, ('slab', 'panel'), pairs)  29.3 us
    ppermute x18, starting transfers between devices, move(): return lax.ppermute(value, 'slab', pairs)  24.8 us
    ppermute x8, starting transfers between devices, send_rows(): return lax.ppermute(value, ('slab', 'panel'), pairs)  16.4 us
    unnamed x48, local copies, waits for them, and re-layouts  6.34 us
  transfers between devices with their start and end apart: 32, of which 14 were waited for; matrix products, arithmetic and copies ran while one was open for 5% of the time, Pallas kernels for 13%

profile of v4, /device:TPU:0, one launch (start us, length us, event | category | flops | bytes accessed | tf_op | source)
XLA Modules:
  0.0 309.9 jit_solution(17040862539339785544)
XLA Ops:
  0.6 3.0 constant_dynamic-slice_fusion.3
  4.1 1.1 copy.34
  5.3 1.8 multiply_convert_fusion.1
  7.2 2.6 collective-permute-start.4
  10.1 1.6 collective-permute-start.1
  11.6 1.5 collective-permute-start.2
  13.3 2.7 collective-permute-start.3
  16.8 1.6 slice.88
  19.3 39.5 %collective-permute-done.4.refs_9_.refs_8_ = bf16[1152,512]{1,0:T(8,128)(2,1)S(1)} collective-permute-done((bf16[1152,512]{1,0:T(8,128)(2,1)S(1)}, bf16[1152,512]{1,0:T(8,128)(2,1)S(1)}, u32[]{:S(2)}, u32[]{:S(2)}) %collective-permute-start.4) | collective-permute-done | bytes 1179680 | tf_op jit(solution)/shard_map/ppermute | solution.py:53
  58.7 14.1 %collective-permute-done.3.refs_5_ = bf16[80,8192]{1,0:T(8,128)(2,1)S(1)} collective-permute-done((bf16[80,8192]{1,0:T(8,128)(2,1)S(1)}, bf16[80,8192]{1,0:T(8,128)(2,1)S(1)}, u32[]{:S(2)}, u32[]{:S(2)}) %collective-permute-start.3) | collective-permute-done | bytes 1310752 | tf_op jit(solution)/shard_map/ppermute | solution.py:53
  72.8 2.3 copy-done.6
  76.5 1.2 collective-permute-start.6
  77.7 3.0 collective-permute-start.7
  80.8 55.2 %collective-permute-done.7.refs_6_ = bf16[80,8192]{1,0:T(8,128)(2,1)S(1)} collective-permute-done((bf16[80,8192]{1,0:T(8,128)(2,1)S(1)}, bf16[80,8192]{1,0:T(8,128)(2,1)S(1)}, u32[]{:S(2)}, u32[]{:S(2)}) %collective-permute-start.7) | collective-permute-done | bytes 1310752 | tf_op jit(solution)/shard_map/ppermute | solution.py:53
  136.0 2.2 collective-permute-done.8.refs_10_.refs_9_
  138.2 1.4 collective-permute-start.14
  140.1 1.6 copy-done.2
  141.8 2.6 pad_maximum_fusion.3
  144.8 1.4 collective-permute-start.11
  147.2 15.5 %shard_map.59 = (bf16[160,512]{1,0:T(8,128)(2,1)}, bf16[160,512]{1,0:T(8,128)(2,1)}, bf16[160,512]{1,0:T(8,128)(2,1)}, bf16[160,512]{1,0:T(8,128)(2,1)}, bf16[160,512]{1,0:T(8,128)(2,1)}, /*index=5*/f32[800,512]{1,0:T(8,128)}) custom-call(bf16[160,8192]{1,0:T(8,128)(2,1)} %copy-done.3, bf16[160,8192]{1,0:T(8,128)(2,1)} %copy-done.5, ...), custom_call_target="tpu_custom_call" | custom-call | flops 1024 | bytes 1024 | tf_op jit(solution)/shard_map/pallas_call | solution.py:170
  162.7 16.6 %collective-permute-done.14.refs_7_.refs_10_ = bf16[1792,512]{1,0:T(8,128)(2,1)S(1)} collective-permute-done((bf16[1792,512]{1,0:T(8,128)(2,1)}, bf16[1792,512]{1,0:T(8,128)(2,1)S(1)}, u32[]{:S(2)}, u32[]{:S(2)}) %collective-permute-start.14) | collective-permute-done | bytes 1835040 | tf_op jit(solution)/shard_map/ppermute | solution.py:53
  179.3 3.9 %collective-permute-done.15.refs_8_.refs_13_ = bf16[1792,512]{1,0:T(8,128)(2,1)} collective-permute-done((bf16[1792,512]{1,0:T(8,128)(2,1)S(1)}, bf16[1792,512]{1,0:T(8,128)(2,1)}, u32[]{:S(2)}, u32[]{:S(2)}) %collective-permute-start.15) | collective-permute-done | bytes 1835040 | tf_op jit(solution)/shard_map/ppermute | solution.py:57
  183.2 9.0 %shard_map.60 = (bf16[160,1024]{1,0:T(8,128)(2,1)}, bf16[160,1024]{1,0:T(8,128)(2,1)}, bf16[160,1024]{1,0:T(8,128)(2,1)}, bf16[160,1024]{1,0:T(8,128)(2,1)}, bf1...) custom-call(bf16[160,8192]{1,0:T(8,128)(2,1)} %copy-done.3, bf16[160,8192]{1,0:T(8,128)(2,1)} %copy-done.5, ...), custom_call_target="tpu_custom_call" | custom-call | flops 1024 | bytes 1024 | tf_op jit(solution)/shard_map/pallas_call | solution.py:170
  192.2 1.2 slice.76
  194.2 1.1 slice.75
  195.3 1.1 collective-permute-start.16
  196.4 1.6 collective-permute-start.18
  198.0 1.1 broadcast_select_fusion.1
  199.6 11.5 %collective-permute-done.16.refs_4_ = bf16[32,8192]{1,0:T(8,128)(2,1)S(1)} collective-permute-done((bf16[32,8192]{1,0:T(8,128)(2,1)S(1)}, bf16[32,8192]{1,0:T(8,128)(2,1)S(1)}, u32[]{:S(2)}, u32[]{:S(2)}) %collective-permute-start.16) | collective-permute-done | bytes 524320 | tf_op jit(solution)/shard_map/ppermute | solution.py:53
  211.1 5.5 %collective-permute-done.17.refs_5_ = bf16[48,8192]{1,0:T(8,128)(2,1)S(1)} collective-permute-done((bf16[48,8192]{1,0:T(8,128)(2,1)S(1)}, bf16[48,8192]{1,0:T(8,128)(2,1)S(1)}, u32[]{:S(2)}, u32[]{:S(2)}) %collective-permute-start.17) | collective-permute-done | bytes 786464 | tf_op jit(solution)/shard_map/ppermute | solution.py:53
  216.6 5.7 %collective-permute-start.19 = (bf16[160,1024]{1,0:T(8,128)(2,1)}, bf16[160,1024]{1,0:T(8,128)(2,1)}, u32[]{:S(2)}, u32[]{:S(2)}) collective-permute-start(bf16[160,1024]{1,0:T(8,128)(2,1)} %get-tuple-element.114), channel_id=1, source_target_pairs={{0,4},{1,6},{2,0},{3,2},{4,12},{5,14},{6,8},{7,10},{8,20},{9,22},{... | collective-permute-start | bytes 983048 | tf_op jit(solution)/shard_map/ppermute | solution.py:66
  222.3 2.6 collective-permute-start.21
  226.1 2.3 fusion.24
  228.5 14.6 %shard_map.61 = (bf16[160,1024]{1,0:T(8,128)(2,1)}, bf16[160,1024]{1,0:T(8,128)(2,1)}, bf16[160,1024]{1,0:T(8,128)(2,1)}, bf16[640,1024]{1,0:T(8,128)(2,1)}) custom-call(bf16[160,8192]{1,0:T(8,128)(2,1)} %copy-done.1, bf16[128,8192]{1,0:T(8,128)(2,1)} %collective-permute-done.10.refs_1_, bf16[160,8192]{1,0:T(8,128)(2,1)} %copy-done.2, ...), custom_call_target="tpu_custom_call" | custom-call | flops 1024 | bytes 1024 | tf_op jit(solution)/shard_map/pallas_call | solution.py:170
  243.1 7.0 %collective-permute-done.22.refs_4_ = bf16[160,1024]{1,0:T(8,128)(2,1)} collective-permute-done((bf16[160,1024]{1,0:T(8,128)(2,1)}, bf16[160,1024]{1,0:T(8,128)(2,1)}, u32[]{:S(2)}, u32[]{:S(2)}) %collective-permute-start.22) | collective-permute-done | bytes 327712 | tf_op jit(solution)/shard_map/ppermute | solution.py:66
  250.1 2.4 fusion.23
  254.2 1.5 collective-permute-start.24
  256.4 2.0 collective-permute-start.23
  258.4 1.9 collective-permute-start.26
  260.4 4.0 %collective-permute-start.27 = (bf16[160,1024]{1,0:T(8,128)(2,1)}, bf16[160,1024]{1,0:T(8,128)(2,1)}, u32[]{:S(2)}, u32[]{:S(2)}) collective-permute-start(bf16[160,1024]{1,0:T(8,128)(2,1)} %get-tuple-element.134), channel_id=1, source_target_pairs={{0,9},{1,11},{2,13},{3,15},{4,1},{5,3},{6,5},{7,7},{8,25},{9,27},{... | collective-permute-start | bytes 983048 | tf_op jit(solution)/shard_map/ppermute | solution.py:66
  264.4 8.7 %collective-permute-done.26.refs_5_ = bf16[160,1024]{1,0:T(8,128)(2,1)} collective-permute-done((bf16[160,1024]{1,0:T(8,128)(2,1)}, bf16[160,1024]{1,0:T(8,128)(2,1)}, u32[]{:S(2)}, u32[]{:S(2)}) %collective-permute-start.26) | collective-permute-done | bytes 327712 | tf_op jit(solution)/shard_map/ppermute | solution.py:66
  273.1 4.6 %collective-permute-done.27.refs_6_ = bf16[160,1024]{1,0:T(8,128)(2,1)} collective-permute-done((bf16[160,1024]{1,0:T(8,128)(2,1)}, bf16[160,1024]{1,0:T(8,128)(2,1)}, u32[]{:S(2)}, u32[]{:S(2)}) %collective-permute-start.27) | collective-permute-done | bytes 327712 | tf_op jit(solution)/shard_map/ppermute | solution.py:66
  277.7 1.1 convert_add_fusion
  280.6 9.5 %collective-permute-done.28 = bf16[64,1408]{1,0:T(8,128)(2,1)S(1)} collective-permute-done((bf16[64,1408]{1,0:T(8,128)(2,1)S(1)}, bf16[64,1408]{1,0:T(8,128)(2,1)S(1)}, u32[]{:S(2)}, u32[]{:S(2)}) %collective-permute-start.28) | collective-permute-done | bytes 180256 | tf_op jit(solution)/shard_map/ppermute | solution.py:53
  290.3 1.1 fusion.19
  292.9 2.6 collective-permute-start.30
  295.4 9.1 %collective-permute-done.31.refs_7_ = bf16[160,1024]{1,0:T(8,128)(2,1)S(1)} collective-permute-done((bf16[160,1024]{1,0:T(8,128)(2,1)S(1)}, bf16[160,1024]{1,0:T(8,128)(2,1)S(1)}, u32[]{:S(2)}, u32[]{:S(2)}) %collective-permute-start.31) | collective-permute-done | bytes 327712 | tf_op jit(solution)/shard_map/ppermute | solution.py:66
  306.3 3.4 %shard_map.62 = bf16[160,8192]{1,0:T(8,128)(2,1)} custom-call(bf16[160,1024]{1,0:T(8,128)(2,1)} %copy-done.17, bf16[160,1024]{1,0:T(8,128)(2,1)} %collective-permute-done.19.refs_1_, bf16[160,1024]{1,0:T(8,128)(2,1)} %collective-permute-done.20.refs_2_, bf16[160,1024]{1,0:T(8,128)(2,1)} %collective-permute-done.21.refs_3_, ...), custom_call_target="tpu_custom_call" | custom-call | flops 1024 | bytes 1024 | tf_op jit(solution)/shard_map/pallas_call | solution.py:209
  (129 shorter events, 16.0 us)
Async XLA Ops:
  0.6 4.6 %copy-start.20 = (f32[8192]{0:T(1024)S(1)}, f32[8192]{0:T(1024)}, u32[]{:S(2)}) copy-start(f32[8192]{0:T(1024)} %param.5) | copy-start | bytes 98308
  3.7 6.2 %collective-permute-start = (bf16[160,4096]{1,0:T(8,128)(2,1)}, bf16[160,4096]{1,0:T(8,128)(2,1)S(1)}, u32[]{:S(2)}, u32[]{:S(2)}) collective-permute-start(bf16[160,4096]{1,0:T(8,128)(2,1)} %get-tuple-element.150), channel_id=1, source_target_pairs={{0,1},{1,0},{2,3},{3,2},{4,5},{5,4},{6,7},{7,6},{8,9},{9,8},{10,11... | collective-permute-start | bytes 3932168 | tf_op jit(solution)/shard_map/ppermute | solution.py:57
  5.3 10.7 %slice-start = ((s8[8388608]{0:T(1024)(128)(4,1)}), s8[4194304]{0:T(1024)(128)(4,1)S(1)}, s32[]{:S(2)}) async-start(s8[8388608]{0:T(1024)(128)(4,1)} %bitcast.35), calls=%async_computation | async-start | bytes 8388608
  7.2 51.5 %collective-permute-start.4 = (bf16[1152,512]{1,0:T(8,128)(2,1)S(1)}, bf16[1152,512]{1,0:T(8,128)(2,1)S(1)}, u32[]{:S(2)}, u32[]{:S(2)}) collective-permute-start(bf16[1152,512]{1,0:T(8,128)(2,1)S(1)} %pad_maximum_fusion.5), channel_id=1, source_target_pairs={{0,8},{2,10},{4,12},{6,14},{8,0},{10,2},{12,4},{14,6},{16,24},{18,... | collective-permute-start | bytes 3538952 | tf_op jit(solution)/shard_map/ppermute | solution.py:53
  9.9 6.1 %slice-start.1 = ((s8[8388608]{0:T(1024)(128)(4,1)}), s8[4194304]{0:T(1024)(128)(4,1)S(1)}, s32[]{:S(2)}) async-start(s8[8388608]{0:T(1024)(128)(4,1)} %bitcast.35), calls=%async_computation.1 | async-start | bytes 8388608
  10.1 3.3 %copy-start.3 = (bf16[160,8192]{1,0:T(8,128)(2,1)}, bf16[160,8192]{1,0:T(8,128)(2,1)S(1)}, u32[]{:S(2)}) copy-start(bf16[160,8192]{1,0:T(8,128)(2,1)S(1)} %pad_maximum_fusion.refs_0_) | copy-start | bytes 7864324
  10.1 62.7 %collective-permute-start.1 = (bf16[160,8192]{1,0:T(8,128)(2,1)S(1)}, bf16[160,8192]{1,0:T(8,128)(2,1)S(1)}, u32[]{:S(2)}, u32[]{:S(2)}) collective-permute-start(bf16[160,8192]{1,0:T(8,128)(2,1)S(1)} %pad_maximum_fusion.refs_0_), channel_id=1, source_target_pairs={{0,2},{2,0},{4,6},{6,4},{8,10},{10,8},{12,14},{14,12},{16,18},{18,... | collective-permute-start | bytes 7864328 | tf_op jit(solution)/shard_map/ppermute | solution.py:53
  11.6 61.2 %collective-permute-start.2 = (bf16[160,8192]{1,0:T(8,128)(2,1)S(1)}, bf16[160,8192]{1,0:T(8,128)(2,1)S(1)}, u32[]{:S(2)}, u32[]{:S(2)}) collective-permute-start(bf16[160,8192]{1,0:T(8,128)(2,1)S(1)} %pad_maximum_fusion.refs_0_), channel_id=1, source_target_pairs={{0,4},{2,6},{4,0},{6,2},{8,12},{10,14},{12,8},{14,10},{16,20},{18,... | collective-permute-start | bytes 7864328 | tf_op jit(solution)/shard_map/ppermute | solution.py:53
  13.3 59.4 %collective-permute-start.3 = (bf16[80,8192]{1,0:T(8,128)(2,1)S(1)}, bf16[80,8192]{1,0:T(8,128)(2,1)S(1)}, u32[]{:S(2)}, u32[]{:S(2)}) collective-permute-start(bf16[80,8192]{1,0:T(8,128)(2,1)S(1)} %get-tuple-element.148), channel_id=1, source_target_pairs={{0,16},{2,18},{4,20},{6,22},{8,24},{10,26},{12,28},{14,30},{16,0},... | collective-permute-start | bytes 3932168 | tf_op jit(solution)/shard_map/ppermute | solution.py:53
  16.8 121.4 %collective-permute-start.9 = (bf16[4096,512]{1,0:T(8,128)(2,1)S(1)}, bf16[4096,512]{1,0:T(8,128)(2,1)S(1)}, u32[]{:S(2)}, u32[]{:S(2)}) collective-permute-start(bf16[4096,512]{1,0:T(8,128)(2,1)S(1)} %multiply_convert_fusion.refs_7_.refs_6_), channel_id=1, source_target_pairs={{0,1},{1,0},{2,3},{3,2},{4,5},{5,4},{6,7},{7,6},{8,9},{9,8},{10,11... | collective-permute-start | bytes 12582920 | tf_op jit(solution)/shard_map/ppermute | solution.py:57
  58.7 80.9 %copy-start.10 = (bf16[1152,512]{1,0:T(8,128)(2,1)}, bf16[1152,512]{1,0:T(8,128)(2,1)S(1)}, u32[]{:S(2)}) copy-start(bf16[1152,512]{1,0:T(8,128)(2,1)S(1)} %collective-permute-done.4.refs_9_.refs_8_) | copy-start | bytes 3538948
  75.9 62.2 %collective-permute-start.5 = (bf16[160,8192]{1,0:T(8,128)(2,1)S(1)}, bf16[160,8192]{1,0:T(8,128)(2,1)S(1)}, u32[]{:S(2)}, u32[]{:S(2)}) collective-permute-start(bf16[160,8192]{1,0:T(8,128)(2,1)S(1)} %get-tuple-element.156), channel_id=1, source_target_pairs={{0,2},{2,0},{4,6},{6,4},{8,10},{10,8},{12,14},{14,12},{16,18},{18,... | collective-permute-start | bytes 7864328 | tf_op jit(solution)/shard_map/ppermute | solution.py:53
  76.5 61.6 %collective-permute-start.6 = (bf16[160,8192]{1,0:T(8,128)(2,1)S(1)}, bf16[160,8192]{1,0:T(8,128)(2,1)S(1)}, u32[]{:S(2)}, u32[]{:S(2)}) collective-permute-start(bf16[160,8192]{1,0:T(8,128)(2,1)S(1)} %get-tuple-element.155), channel_id=1, source_target_pairs={{0,4},{2,6},{4,0},{6,2},{8,12},{10,14},{12,8},{14,10},{16,20},{18,... | collective-permute-start | bytes 7864328 | tf_op jit(solution)/shard_map/ppermute | solution.py:53
  77.7 60.4 %collective-permute-start.8 = (bf16[1408,512]{1,0:T(8,128)(2,1)S(1)}, bf16[1408,512]{1,0:T(8,128)(2,1)S(1)}, u32[]{:S(2)}, u32[]{:S(2)}) collective-permute-start(bf16[1408,512]{1,0:T(8,128)(2,1)S(1)} %slice.87), channel_id=1, source_target_pairs={{0,8},{2,10},{4,12},{6,14},{8,0},{10,2},{12,4},{14,6},{16,24},{18,... | collective-permute-start | bytes 4325384 | tf_op jit(solution)/shard_map/ppermute | solution.py:53
  77.7 58.2 %collective-permute-start.7 = (bf16[80,8192]{1,0:T(8,128)(2,1)S(1)}, bf16[80,8192]{1,0:T(8,128)(2,1)S(1)}, u32[]{:S(2)}, u32[]{:S(2)}) collective-permute-start(bf16[80,8192]{1,0:T(8,128)(2,1)S(1)} %get-tuple-element.147), channel_id=1, source_target_pairs={{0,16},{2,18},{4,20},{6,22},{8,24},{10,26},{12,28},{14,30},{16,0},... | collective-permute-start | bytes 3932168 | tf_op jit(solution)/shard_map/ppermute | solution.py:53
  136.0 11.2 %copy-start.8 = (bf16[80,8192]{1,0:T(8,128)(2,1)}, bf16[80,8192]{1,0:T(8,128)(2,1)S(1)}, u32[]{:S(2)}) copy-start(bf16[80,8192]{1,0:T(8,128)(2,1)S(1)} %collective-permute-done.7.refs_6_) | copy-start | bytes 3932164
  138.1 8.0 %copy-start.12 = (bf16[1408,512]{1,0:T(8,128)(2,1)}, bf16[1408,512]{1,0:T(8,128)(2,1)S(1)}, u32[]{:S(2)}) copy-start(bf16[1408,512]{1,0:T(8,128)(2,1)S(1)} %collective-permute-done.8.refs_10_.refs_9_) | copy-start | bytes 4325380
  138.2 6.2 %copy-start.4 = (bf16[4096,512]{1,0:T(8,128)(2,1)}, bf16[4096,512]{1,0:T(8,128)(2,1)S(1)}, u32[]{:S(2)}) copy-start(bf16[4096,512]{1,0:T(8,128)(2,1)S(1)} %collective-permute-done.9.refs_8_.refs_7_) | copy-start | bytes 12582916
  138.2 6.2 %copy-start.1 = (bf16[160,8192]{1,0:T(8,128)(2,1)}, bf16[160,8192]{1,0:T(8,128)(2,1)S(1)}, u32[]{:S(2)}) copy-start(bf16[160,8192]{1,0:T(8,128)(2,1)S(1)} %collective-permute-done.5.refs_4_.refs_0_) | copy-start | bytes 7864324
  138.2 3.5 %copy-start.2 = (bf16[160,8192]{1,0:T(8,128)(2,1)}, bf16[160,8192]{1,0:T(8,128)(2,1)S(1)}, u32[]{:S(2)}) copy-start(bf16[160,8192]{1,0:T(8,128)(2,1)S(1)} %collective-permute-done.6.refs_3_.refs_2_) | copy-start | bytes 7864324
  138.2 41.1 %collective-permute-start.14 = (bf16[1792,512]{1,0:T(8,128)(2,1)}, bf16[1792,512]{1,0:T(8,128)(2,1)S(1)}, u32[]{:S(2)}, u32[]{:S(2)}) collective-permute-start(bf16[1792,512]{1,0:T(8,128)(2,1)} %slice.88), channel_id=1, source_target_pairs={{0,8},{2,10},{4,12},{6,14},{8,0},{10,2},{12,4},{14,6},{16,24},{18,... | collective-permute-start | bytes 5505032 | tf_op jit(solution)/shard_map/ppermute | solution.py:53
  139.6 7.6 %collective-permute-start.13 = (bf16[1408,512]{1,0:T(8,128)(2,1)S(1)}, bf16[1408,512]{1,0:T(8,128)(2,1)}, u32[]{:S(2)}, u32[]{:S(2)}) collective-permute-start(bf16[1408,512]{1,0:T(8,128)(2,1)S(1)} %collective-permute-done.8.refs_10_.refs_9_), channel_id=1, source_target_pairs={{0,1},{1,0},{2,3},{3,2},{4,5},{5,4},{6,7},{7,6},{8,9},{9,8},{10,11... | collective-permute-start | bytes 4325384 | tf_op jit(solution)/shard_map/ppermute | solution.py:57
  139.6 6.6 %collective-permute-start.12 = (bf16[1152,512]{1,0:T(8,128)(2,1)S(1)}, bf16[1152,512]{1,0:T(8,128)(2,1)S(1)}, u32[]{:S(2)}, u32[]{:S(2)}) collective-permute-start(bf16[1152,512]{1,0:T(8,128)(2,1)S(1)} %collective-permute-done.4.refs_9_.refs_8_), channel_id=1, source_target_pairs={{0,1},{1,0},{2,3},{3,2},{4,5},{5,4},{6,7},{7,6},{8,9},{9,8},{10,11... | collective-permute-start | bytes 3538952 | tf_op jit(solution)/shard_map/ppermute | solution.py:57
  144.4 47.8 %collective-permute-start.10 = (bf16[128,8192]{1,0:T(8,128)(2,1)}, bf16[128,8192]{1,0:T(8,128)(2,1)}, u32[]{:S(2)}, u32[]{:S(2)}) collective-permute-start(bf16[128,8192]{1,0:T(8,128)(2,1)} %get-tuple-element.154), channel_id=1, source_target_pairs={{0,2},{2,0},{4,6},{6,4},{8,10},{10,8},{12,14},{14,12},{16,18},{18,... | collective-permute-start | bytes 6291464 | tf_op jit(solution)/shard_map/ppermute | solution.py:53
  144.8 47.5 %collective-permute-start.11 = (bf16[128,8192]{1,0:T(8,128)(2,1)}, bf16[128,8192]{1,0:T(8,128)(2,1)}, u32[]{:S(2)}, u32[]{:S(2)}) collective-permute-start(bf16[128,8192]{1,0:T(8,128)(2,1)} %get-tuple-element.153), channel_id=1, source_target_pairs={{0,4},{2,6},{4,0},{6,2},{8,12},{10,14},{12,8},{14,10},{16,20},{18,... | collective-permute-start | bytes 6291464 | tf_op jit(solution)/shard_map/ppermute | solution.py:53
  179.3 3.9 %copy-start.9 = (bf16[1792,512]{1,0:T(8,128)(2,1)}, bf16[1792,512]{1,0:T(8,128)(2,1)S(1)}, u32[]{:S(2)}) copy-start(bf16[1792,512]{1,0:T(8,128)(2,1)S(1)} %collective-permute-done.14.refs_7_.refs_10_) | copy-start | bytes 5505028
  179.3 3.9 %collective-permute-start.15 = (bf16[1792,512]{1,0:T(8,128)(2,1)S(1)}, bf16[1792,512]{1,0:T(8,128)(2,1)}, u32[]{:S(2)}, u32[]{:S(2)}) collective-permute-start(bf16[1792,512]{1,0:T(8,128)(2,1)S(1)} %collective-permute-done.14.refs_7_.refs_10_), channel_id=1, source_target_pairs={{0,1},{1,0},{2,3},{3,2},{4,5},{5,4},{6,7},{7,6},{8,9},{9,8},{10,11... | collective-permute-start | bytes 5505032 | tf_op jit(solution)/shard_map/ppermute | solution.py:57
  193.4 23.2 %collective-permute-start.17 = (bf16[48,8192]{1,0:T(8,128)(2,1)S(1)}, bf16[48,8192]{1,0:T(8,128)(2,1)S(1)}, u32[]{:S(2)}, u32[]{:S(2)}) collective-permute-start(bf16[48,8192]{1,0:T(8,128)(2,1)S(1)} %slice.76), channel_id=1, source_target_pairs={{0,2},{2,0},{4,6},{6,4},{8,10},{10,8},{12,14},{14,12},{16,18},{18,... | collective-permute-start | bytes 2359304 | tf_op jit(solution)/shard_map/ppermute | solution.py:53
  195.3 15.8 %collective-permute-start.16 = (bf16[32,8192]{1,0:T(8,128)(2,1)S(1)}, bf16[32,8192]{1,0:T(8,128)(2,1)S(1)}, u32[]{:S(2)}, u32[]{:S(2)}) collective-permute-start(bf16[32,8192]{1,0:T(8,128)(2,1)S(1)} %slice.75), channel_id=1, source_target_pairs={{0,4},{2,6},{4,0},{6,2},{8,12},{10,14},{12,8},{14,10},{16,20},{18,... | collective-permute-start | bytes 1572872 | tf_op jit(solution)/shard_map/ppermute | solution.py:53
  196.4 3.2 %collective-permute-start.18 = (bf16[160,1024]{1,0:T(8,128)(2,1)}, bf16[160,1024]{1,0:T(8,128)(2,1)S(1)}, u32[]{:S(2)}, u32[]{:S(2)}) collective-permute-start(bf16[160,1024]{1,0:T(8,128)(2,1)} %get-tuple-element.108), channel_id=1, source_target_pairs={{0,0},{1,2},{2,4},{3,6},{4,8},{5,10},{6,12},{7,14},{8,16},{9,18},{... | collective-permute-start | bytes 983048 | tf_op jit(solution)/shard_map/ppermute | solution.py:66
  199.1 29.4 %copy-start.14 = (bf16[256,512]{1,0:T(8,128)(2,1)}, bf16[256,512]{1,0:T(8,128)(2,1)S(1)}, u32[]{:S(2)}) copy-start(bf16[256,512]{1,0:T(8,128)(2,1)S(1)} %get-tuple-element.152) | copy-start | bytes 786436
  199.6 17.0 %copy-start.17 = (bf16[160,1024]{1,0:T(8,128)(2,1)}, bf16[160,1024]{1,0:T(8,128)(2,1)S(1)}, u32[]{:S(2)}) copy-start(bf16[160,1024]{1,0:T(8,128)(2,1)S(1)} %collective-permute-done.18.refs_0_) | copy-start | bytes 983044
  211.1 14.9 %copy-start.16 = (bf16[32,8192]{1,0:T(8,128)(2,1)}, bf16[32,8192]{1,0:T(8,128)(2,1)S(1)}, u32[]{:S(2)}) copy-start(bf16[32,8192]{1,0:T(8,128)(2,1)S(1)} %collective-permute-done.16.refs_4_) | copy-start | bytes 1572868
  216.6 11.8 %copy-start.15 = (bf16[48,8192]{1,0:T(8,128)(2,1)}, bf16[48,8192]{1,0:T(8,128)(2,1)S(1)}, u32[]{:S(2)}) copy-start(bf16[48,8192]{1,0:T(8,128)(2,1)S(1)} %collective-permute-done.17.refs_5_) | copy-start | bytes 2359300
  216.6 26.5 %collective-permute-start.19 = (bf16[160,1024]{1,0:T(8,128)(2,1)}, bf16[160,1024]{1,0:T(8,128)(2,1)}, u32[]{:S(2)}, u32[]{:S(2)}) collective-permute-start(bf16[160,1024]{1,0:T(8,128)(2,1)} %get-tuple-element.114), channel_id=1, source_target_pairs={{0,4},{1,6},{2,0},{3,2},{4,12},{5,14},{6,8},{7,10},{8,20},{9,22},{... | collective-permute-start | bytes 983048 | tf_op jit(solution)/shard_map/ppermute | solution.py:66
  222.3 20.8 %collective-permute-start.20 = (bf16[160,1024]{1,0:T(8,128)(2,1)}, bf16[160,1024]{1,0:T(8,128)(2,1)}, u32[]{:S(2)}, u32[]{:S(2)}) collective-permute-start(bf16[160,1024]{1,0:T(8,128)(2,1)} %get-tuple-element.115), channel_id=1, source_target_pairs={{0,8},{1,10},{2,12},{3,14},{4,0},{5,2},{6,4},{7,6},{8,24},{9,26},{... | collective-permute-start | bytes 983048 | tf_op jit(solution)/shard_map/ppermute | solution.py:66
  222.3 20.8 %collective-permute-start.21 = (bf16[160,1024]{1,0:T(8,128)(2,1)}, bf16[160,1024]{1,0:T(8,128)(2,1)}, u32[]{:S(2)}, u32[]{:S(2)}) collective-permute-start(bf16[160,1024]{1,0:T(8,128)(2,1)} %get-tuple-element.116), channel_id=1, source_target_pairs={{0,12},{1,14},{2,8},{3,10},{4,4},{5,6},{6,0},{7,2},{8,28},{9,30},{... | collective-permute-start | bytes 983048 | tf_op jit(solution)/shard_map/ppermute | solution.py:66
  225.0 25.1 %collective-permute-start.22 = (bf16[160,1024]{1,0:T(8,128)(2,1)}, bf16[160,1024]{1,0:T(8,128)(2,1)}, u32[]{:S(2)}, u32[]{:S(2)}) collective-permute-start(bf16[160,1024]{1,0:T(8,128)(2,1)} %get-tuple-element.117.refs_14_), channel_id=1, source_target_pairs={{0,1},{1,3},{2,5},{3,7},{4,9},{5,11},{6,13},{7,15},{8,17},{9,19},{... | collective-permute-start | bytes 983048 | tf_op jit(solution)/shard_map/ppermute | solution.py:66
  253.4 24.3 %collective-permute-start.25 = (bf16[128,1408]{1,0:T(8,128)(2,1)}, bf16[128,1408]{1,0:T(8,128)(2,1)S(1)}, u32[]{:S(2)}, u32[]{:S(2)}) collective-permute-start(bf16[128,1408]{1,0:T(8,128)(2,1)} %fusion.15), channel_id=1, source_target_pairs={{0,6},{2,4},{4,2},{6,0},{8,14},{10,12},{12,10},{14,8},{16,22},{18,... | collective-permute-start | bytes 1081352 | tf_op jit(solution)/shard_map/ppermute | solution.py:53
  254.2 23.5 %collective-permute-start.24 = (bf16[128,1408]{1,0:T(8,128)(2,1)}, bf16[128,1408]{1,0:T(8,128)(2,1)}, u32[]{:S(2)}, u32[]{:S(2)}) collective-permute-start(bf16[128,1408]{1,0:T(8,128)(2,1)} %fusion.14), channel_id=1, source_target_pairs={{0,4},{2,6},{4,0},{6,2},{8,12},{10,14},{12,8},{14,10},{16,20},{18,... | collective-permute-start | bytes 1081352 | tf_op jit(solution)/shard_map/ppermute | solution.py:53
  256.4 21.3 %collective-permute-start.23 = (bf16[128,1408]{1,0:T(8,128)(2,1)}, bf16[128,1408]{1,0:T(8,128)(2,1)S(1)}, u32[]{:S(2)}, u32[]{:S(2)}) collective-permute-start(bf16[128,1408]{1,0:T(8,128)(2,1)} %fusion.13), channel_id=1, source_target_pairs={{0,2},{2,0},{4,6},{6,4},{8,10},{10,8},{12,14},{14,12},{16,18},{18,... | collective-permute-start | bytes 1081352 | tf_op jit(solution)/shard_map/ppermute | solution.py:53
  258.4 14.6 %collective-permute-start.26 = (bf16[160,1024]{1,0:T(8,128)(2,1)}, bf16[160,1024]{1,0:T(8,128)(2,1)}, u32[]{:S(2)}, u32[]{:S(2)}) collective-permute-start(bf16[160,1024]{1,0:T(8,128)(2,1)} %get-tuple-element.133), channel_id=1, source_target_pairs={{0,5},{1,7},{2,1},{3,3},{4,13},{5,15},{6,9},{7,11},{8,21},{9,23},{... | collective-permute-start | bytes 983048 | tf_op jit(solution)/shard_map/ppermute | solution.py:66
  260.4 17.3 %collective-permute-start.27 = (bf16[160,1024]{1,0:T(8,128)(2,1)}, bf16[160,1024]{1,0:T(8,128)(2,1)}, u32[]{:S(2)}, u32[]{:S(2)}) collective-permute-start(bf16[160,1024]{1,0:T(8,128)(2,1)} %get-tuple-element.134), channel_id=1, source_target_pairs={{0,9},{1,11},{2,13},{3,15},{4,1},{5,3},{6,5},{7,7},{8,25},{9,27},{... | collective-permute-start | bytes 983048 | tf_op jit(solution)/shard_map/ppermute | solution.py:66
  279.0 12.6 %copy-start.21 = (bf16[160,1024]{1,0:T(8,128)(2,1)S(1)}, bf16[160,1024]{1,0:T(8,128)(2,1)}, u32[]{:S(2)}) copy-start(bf16[160,1024]{1,0:T(8,128)(2,1)} %get-tuple-element.140) | copy-start | bytes 983044
  280.0 10.1 %collective-permute-start.28 = (bf16[64,1408]{1,0:T(8,128)(2,1)S(1)}, bf16[64,1408]{1,0:T(8,128)(2,1)S(1)}, u32[]{:S(2)}, u32[]{:S(2)}) collective-permute-start(bf16[64,1408]{1,0:T(8,128)(2,1)S(1)} %fusion.20), channel_id=1, source_target_pairs={{0,16},{2,18},{4,20},{6,22},{8,24},{10,26},{12,28},{14,30},{16,0},... | collective-permute-start | bytes 540680 | tf_op jit(solution)/shard_map/ppermute | solution.py:53
  291.5 1.3 collective-permute-start.29
  291.6 12.9 %collective-permute-start.31 = (bf16[160,1024]{1,0:T(8,128)(2,1)S(1)}, bf16[160,1024]{1,0:T(8,128)(2,1)S(1)}, u32[]{:S(2)}, u32[]{:S(2)}) collective-permute-start(bf16[160,1024]{1,0:T(8,128)(2,1)S(1)} %copy-done.21), channel_id=1, source_target_pairs={{0,13},{1,15},{2,9},{3,11},{4,5},{5,7},{6,1},{7,3},{8,29},{9,31},{... | collective-permute-start | bytes 983048 | tf_op jit(solution)/shard_map/ppermute | solution.py:66
  292.9 11.6 %collective-permute-start.30 = (bf16[32,1280]{1,0:T(8,128)(2,1)S(1)}, bf16[32,1280]{1,0:T(8,128)(2,1)S(1)}, u32[]{:S(2)}, u32[]{:S(2)}) collective-permute-start(bf16[32,1280]{1,0:T(8,128)(2,1)S(1)} %get-tuple-element.161), channel_id=1, source_target_pairs={{0,8},{2,10},{4,12},{6,14},{8,0},{10,2},{12,4},{14,6},{16,24},{18,... | collective-permute-start | bytes 245768 | tf_op jit(solution)/shard_map/ppermute | solution.py:53
  (9 other events, 17.8 us)

commit v5 on v3

--- a/solution.py
+++ b/solution.py
@@ -237,7 +237,7 @@
     part = split(ordered, 0, core)[0]
 
     gain_block = lax.dynamic_slice_in_dim(gain, core * depth, depth, 0)[:, None]
-    cuts = [0, 7 * depth // 32, 18 * depth // 32, depth]
+    cuts = [0, 7 * depth // 32, 17 * depth // 32, depth]
     first_piece = (rotation[: cuts[1]] * gain_block[: cuts[1]]).astype(jnp.bfloat16)
     rotation, gain_block = tie((rotation, gain_block), rows)
     turn = (rotation * gain_block).astype(jnp.bfloat16)

time: 307 us -> 309 us (level)
  starting transfers between devices: 42.1 us -> 38.7 us
where the time goes in v5:
time: 309 us; the launch traced here: 308 us
  waiting for transfers between devices  188 us (61%)
  Pallas kernels  43 us (14%)
  starting transfers between devices  38.7 us (13%)
  local copies, waits for them, and re-layouts  19 us (6%)
  other arithmetic  13.1 us (4%)
  matrix products  4.75 us (2%)
    ppermute x18, waiting for transfers between devices, move(): return lax.ppermute(value, 'slab', pairs)  156 us
    pallas_call x3, Pallas kernels, fold(): pl.pallas_call(functools.partial(fold_kernel, plan, turn_plan, steps, n_d...  39.6 us
    ppermute x8, waiting for transfers between devices, send_rows(): return lax.ppermute(value, ('slab', 'panel'), pairs)  27.5 us
    ppermute x18, starting transfers between devices, move(): return lax.ppermute(value, 'slab', pairs)  21.7 us
    ppermute x8, starting transfers between devices, send_rows(): return lax.ppermute(value, ('slab', 'panel'), pairs)  15.9 us
    unnamed x48, local copies, waits for them, and re-layouts  7.68 us
  transfers between devices with their start and end apart: 32, of which 15 were waited for; matrix products, arithmetic and copies ran while one was open for 6% of the time, Pallas kernels for 14%

profile of v5, /device:TPU:0, one launch (start us, length us, event | category | flops | bytes accessed | tf_op | source)
XLA Modules:
  0.0 308.4 jit_solution(16491611070623469987)
XLA Ops:
  0.6 3.0 constant_dynamic-slice_fusion.3
  4.1 1.1 copy.34
  5.3 1.8 multiply_convert_fusion.1
  7.2 2.6 collective-permute-start.4
  10.1 1.6 collective-permute-start.1
  11.6 1.5 collective-permute-start.2
  13.3 2.7 collective-permute-start.3
  16.8 1.7 slice.88
  19.3 39.4 %collective-permute-done.4.refs_9_.refs_8_ = bf16[1152,512]{1,0:T(8,128)(2,1)S(1)} collective-permute-done((bf16[1152,512]{1,0:T(8,128)(2,1)S(1)}, bf16[1152,512]{1,0:T(8,128)(2,1)S(1)}, u32[]{:S(2)}, u32[]{:S(2)}) %collective-permute-start.4) | collective-permute-done | bytes 1179680 | tf_op jit(solution)/shard_map/ppermute | solution.py:53
  58.7 14.1 %collective-permute-done.3.refs_5_ = bf16[80,8192]{1,0:T(8,128)(2,1)S(1)} collective-permute-done((bf16[80,8192]{1,0:T(8,128)(2,1)S(1)}, bf16[80,8192]{1,0:T(8,128)(2,1)S(1)}, u32[]{:S(2)}, u32[]{:S(2)}) %collective-permute-start.3) | collective-permute-done | bytes 1310752 | tf_op jit(solution)/shard_map/ppermute | solution.py:53
  72.8 2.3 copy-done.6
  76.5 1.2 collective-permute-start.6
  77.9 2.8 collective-permute-start.8
  80.8 55.4 %collective-permute-done.7.refs_6_ = bf16[80,8192]{1,0:T(8,128)(2,1)S(1)} collective-permute-done((bf16[80,8192]{1,0:T(8,128)(2,1)S(1)}, bf16[80,8192]{1,0:T(8,128)(2,1)S(1)}, u32[]{:S(2)}, u32[]{:S(2)}) %collective-permute-start.7) | collective-permute-done | bytes 1310752 | tf_op jit(solution)/shard_map/ppermute | solution.py:53
  137.1 3.0 copy-done.2
  140.1 2.6 pad_maximum_fusion.3
  143.1 1.4 collective-permute-start.11
  144.4 1.0 copy-done.11
  145.5 15.5 %shard_map.59 = (bf16[160,512]{1,0:T(8,128)(2,1)}, bf16[160,512]{1,0:T(8,128)(2,1)}, bf16[160,512]{1,0:T(8,128)(2,1)}, bf16[160,512]{1,0:T(8,128)(2,1)}, bf16[160,512]{1,0:T(8,128)(2,1)}, /*index=5*/f32[800,512]{1,0:T(8,128)}) custom-call(bf16[160,8192]{1,0:T(8,128)(2,1)} %copy-done.3, bf16[160,8192]{1,0:T(8,128)(2,1)} %copy-done.5, ...), custom_call_target="tpu_custom_call" | custom-call | flops 1024 | bytes 1024 | tf_op jit(solution)/shard_map/pallas_call | solution.py:170
  161.0 20.2 %collective-permute-done.14.refs_7_.refs_10_ = bf16[1920,512]{1,0:T(8,128)(2,1)S(1)} collective-permute-done((bf16[1920,512]{1,0:T(8,128)(2,1)}, bf16[1920,512]{1,0:T(8,128)(2,1)S(1)}, u32[]{:S(2)}, u32[]{:S(2)}) %collective-permute-start.14) | collective-permute-done | bytes 1966112 | tf_op jit(solution)/shard_map/ppermute | solution.py:53
  181.2 4.1 %collective-permute-done.15.refs_8_.refs_13_ = bf16[1920,512]{1,0:T(8,128)(2,1)} collective-permute-done((bf16[1920,512]{1,0:T(8,128)(2,1)S(1)}, bf16[1920,512]{1,0:T(8,128)(2,1)}, u32[]{:S(2)}, u32[]{:S(2)}) %collective-permute-start.15) | collective-permute-done | bytes 1966112 | tf_op jit(solution)/shard_map/ppermute | solution.py:57
  185.3 9.5 %shard_map.60 = (bf16[160,1024]{1,0:T(8,128)(2,1)}, bf16[160,1024]{1,0:T(8,128)(2,1)}, bf16[160,1024]{1,0:T(8,128)(2,1)}, bf16[160,1024]{1,0:T(8,128)(2,1)}, bf1...) custom-call(bf16[160,8192]{1,0:T(8,128)(2,1)} %copy-done.3, bf16[160,8192]{1,0:T(8,128)(2,1)} %copy-done.5, ...), custom_call_target="tpu_custom_call" | custom-call | flops 1024 | bytes 1024 | tf_op jit(solution)/shard_map/pallas_call | solution.py:170
  194.8 1.2 slice.76
  196.4 1.1 slice.75
  197.5 1.4 collective-permute-start.16
  199.0 1.6 collective-permute-start.18
  200.6 1.1 broadcast_select_fusion.1
  202.1 11.5 %collective-permute-done.16.refs_4_ = bf16[32,8192]{1,0:T(8,128)(2,1)S(1)} collective-permute-done((bf16[32,8192]{1,0:T(8,128)(2,1)S(1)}, bf16[32,8192]{1,0:T(8,128)(2,1)S(1)}, u32[]{:S(2)}, u32[]{:S(2)}) %collective-permute-start.16) | collective-permute-done | bytes 524320 | tf_op jit(solution)/shard_map/ppermute | solution.py:53
  213.7 5.5 %collective-permute-done.17.refs_5_ = bf16[48,8192]{1,0:T(8,128)(2,1)S(1)} collective-permute-done((bf16[48,8192]{1,0:T(8,128)(2,1)S(1)}, bf16[48,8192]{1,0:T(8,128)(2,1)S(1)}, u32[]{:S(2)}, u32[]{:S(2)}) %collective-permute-start.17) | collective-permute-done | bytes 786464 | tf_op jit(solution)/shard_map/ppermute | solution.py:53
  219.2 5.7 %collective-permute-start.19 = (bf16[160,1024]{1,0:T(8,128)(2,1)}, bf16[160,1024]{1,0:T(8,128)(2,1)}, u32[]{:S(2)}, u32[]{:S(2)}) collective-permute-start(bf16[160,1024]{1,0:T(8,128)(2,1)} %get-tuple-element.114), channel_id=1, source_target_pairs={{0,4},{1,6},{2,0},{3,2},{4,12},{5,14},{6,8},{7,10},{8,20},{9,22},{... | collective-permute-start | bytes 983048 | tf_op jit(solution)/shard_map/ppermute | solution.py:66
  224.9 1.9 collective-permute-start.21
  227.9 2.3 fusion.21
  230.2 14.6 %shard_map.61 = (bf16[160,1024]{1,0:T(8,128)(2,1)}, bf16[160,1024]{1,0:T(8,128)(2,1)}, bf16[160,1024]{1,0:T(8,128)(2,1)}, bf16[640,1024]{1,0:T(8,128)(2,1)}) custom-call(bf16[160,8192]{1,0:T(8,128)(2,1)} %copy-done.1, bf16[128,8192]{1,0:T(8,128)(2,1)} %collective-permute-done.10.refs_1_, bf16[160,8192]{1,0:T(8,128)(2,1)} %copy-done.2, ...), custom_call_target="tpu_custom_call" | custom-call | flops 1024 | bytes 1024 | tf_op jit(solution)/shard_map/pallas_call | solution.py:170
  244.9 6.9 %collective-permute-done.22.refs_4_ = bf16[160,1024]{1,0:T(8,128)(2,1)} collective-permute-done((bf16[160,1024]{1,0:T(8,128)(2,1)}, bf16[160,1024]{1,0:T(8,128)(2,1)}, u32[]{:S(2)}, u32[]{:S(2)}) %collective-permute-start.22) | collective-permute-done | bytes 327712 | tf_op jit(solution)/shard_map/ppermute | solution.py:66
  251.8 2.4 fusion.20
  255.9 1.5 collective-permute-start.24
  258.1 2.0 collective-permute-start.23
  260.1 1.9 collective-permute-start.26
  262.0 3.9 %collective-permute-start.27 = (bf16[160,1024]{1,0:T(8,128)(2,1)}, bf16[160,1024]{1,0:T(8,128)(2,1)}, u32[]{:S(2)}, u32[]{:S(2)}) collective-permute-start(bf16[160,1024]{1,0:T(8,128)(2,1)} %get-tuple-element.134), channel_id=1, source_target_pairs={{0,9},{1,11},{2,13},{3,15},{4,1},{5,3},{6,5},{7,7},{8,25},{9,27},{... | collective-permute-start | bytes 983048 | tf_op jit(solution)/shard_map/ppermute | solution.py:66
  266.0 8.8 %collective-permute-done.26.refs_5_ = bf16[160,1024]{1,0:T(8,128)(2,1)} collective-permute-done((bf16[160,1024]{1,0:T(8,128)(2,1)}, bf16[160,1024]{1,0:T(8,128)(2,1)}, u32[]{:S(2)}, u32[]{:S(2)}) %collective-permute-start.26) | collective-permute-done | bytes 327712 | tf_op jit(solution)/shard_map/ppermute | solution.py:66
  274.8 5.5 %collective-permute-done.27.refs_6_ = bf16[160,1024]{1,0:T(8,128)(2,1)} collective-permute-done((bf16[160,1024]{1,0:T(8,128)(2,1)}, bf16[160,1024]{1,0:T(8,128)(2,1)}, u32[]{:S(2)}, u32[]{:S(2)}) %collective-permute-start.27) | collective-permute-done | bytes 327712 | tf_op jit(solution)/shard_map/ppermute | solution.py:66
  280.3 1.1 convert_add_fusion
  284.1 8.9 %collective-permute-done.28 = bf16[64,1408]{1,0:T(8,128)(2,1)S(1)} collective-permute-done((bf16[64,1408]{1,0:T(8,128)(2,1)S(1)}, bf16[64,1408]{1,0:T(8,128)(2,1)S(1)}, u32[]{:S(2)}, u32[]{:S(2)}) %collective-permute-start.28) | collective-permute-done | bytes 180256 | tf_op jit(solution)/shard_map/ppermute | solution.py:53
  293.0 1.0 slice_add_fusion
  294.2 6.3 %collective-permute-done.29.refs_7_ = bf16[160,1024]{1,0:T(8,128)(2,1)S(1)} collective-permute-done((bf16[160,1024]{1,0:T(8,128)(2,1)S(1)}, bf16[160,1024]{1,0:T(8,128)(2,1)S(1)}, u32[]{:S(2)}, u32[]{:S(2)}) %collective-permute-start.29) | collective-permute-done | bytes 327712 | tf_op jit(solution)/shard_map/ppermute | solution.py:66
  300.8 1.2 collective-permute-done.30
  302.8 3.4 %shard_map.62 = bf16[160,8192]{1,0:T(8,128)(2,1)} custom-call(bf16[160,1024]{1,0:T(8,128)(2,1)} %copy-done.17, bf16[160,1024]{1,0:T(8,128)(2,1)} %collective-permute-done.19.refs_1_, bf16[160,1024]{1,0:T(8,128)(2,1)} %collective-permute-done.20.refs_2_, bf16[160,1024]{1,0:T(8,128)(2,1)} %collective-permute-done.21.refs_3_, ...), custom_call_target="tpu_custom_call" | custom-call | flops 1024 | bytes 1024 | tf_op jit(solution)/shard_map/pallas_call | solution.py:209
  307.4 1.0 reshape.23
  (131 shorter events, 14.9 us)
Async XLA Ops:
  0.6 4.6 %copy-start.20 = (f32[8192]{0:T(1024)S(1)}, f32[8192]{0:T(1024)}, u32[]{:S(2)}) copy-start(f32[8192]{0:T(1024)} %param.5) | copy-start | bytes 98308
  3.7 6.2 %collective-permute-start = (bf16[160,4096]{1,0:T(8,128)(2,1)}, bf16[160,4096]{1,0:T(8,128)(2,1)S(1)}, u32[]{:S(2)}, u32[]{:S(2)}) collective-permute-start(bf16[160,4096]{1,0:T(8,128)(2,1)} %get-tuple-element.150), channel_id=1, source_target_pairs={{0,1},{1,0},{2,3},{3,2},{4,5},{5,4},{6,7},{7,6},{8,9},{9,8},{10,11... | collective-permute-start | bytes 3932168 | tf_op jit(solution)/shard_map/ppermute | solution.py:57
  5.3 10.7 %slice-start = ((s8[8388608]{0:T(1024)(128)(4,1)}), s8[4194304]{0:T(1024)(128)(4,1)S(1)}, s32[]{:S(2)}) async-start(s8[8388608]{0:T(1024)(128)(4,1)} %bitcast.35), calls=%async_computation | async-start | bytes 8388608
  7.2 51.5 %collective-permute-start.4 = (bf16[1152,512]{1,0:T(8,128)(2,1)S(1)}, bf16[1152,512]{1,0:T(8,128)(2,1)S(1)}, u32[]{:S(2)}, u32[]{:S(2)}) collective-permute-start(bf16[1152,512]{1,0:T(8,128)(2,1)S(1)} %pad_maximum_fusion.5), channel_id=1, source_target_pairs={{0,8},{2,10},{4,12},{6,14},{8,0},{10,2},{12,4},{14,6},{16,24},{18,... | collective-permute-start | bytes 3538952 | tf_op jit(solution)/shard_map/ppermute | solution.py:53
  9.9 6.1 %slice-start.1 = ((s8[8388608]{0:T(1024)(128)(4,1)}), s8[4194304]{0:T(1024)(128)(4,1)S(1)}, s32[]{:S(2)}) async-start(s8[8388608]{0:T(1024)(128)(4,1)} %bitcast.35), calls=%async_computation.1 | async-start | bytes 8388608
  10.1 3.3 %copy-start.3 = (bf16[160,8192]{1,0:T(8,128)(2,1)}, bf16[160,8192]{1,0:T(8,128)(2,1)S(1)}, u32[]{:S(2)}) copy-start(bf16[160,8192]{1,0:T(8,128)(2,1)S(1)} %pad_maximum_fusion.refs_0_) | copy-start | bytes 7864324
  10.1 62.7 %collective-permute-start.1 = (bf16[160,8192]{1,0:T(8,128)(2,1)S(1)}, bf16[160,8192]{1,0:T(8,128)(2,1)S(1)}, u32[]{:S(2)}, u32[]{:S(2)}) collective-permute-start(bf16[160,8192]{1,0:T(8,128)(2,1)S(1)} %pad_maximum_fusion.refs_0_), channel_id=1, source_target_pairs={{0,2},{2,0},{4,6},{6,4},{8,10},{10,8},{12,14},{14,12},{16,18},{18,... | collective-permute-start | bytes 7864328 | tf_op jit(solution)/shard_map/ppermute | solution.py:53
  11.6 61.2 %collective-permute-start.2 = (bf16[160,8192]{1,0:T(8,128)(2,1)S(1)}, bf16[160,8192]{1,0:T(8,128)(2,1)S(1)}, u32[]{:S(2)}, u32[]{:S(2)}) collective-permute-start(bf16[160,8192]{1,0:T(8,128)(2,1)S(1)} %pad_maximum_fusion.refs_0_), channel_id=1, source_target_pairs={{0,4},{2,6},{4,0},{6,2},{8,12},{10,14},{12,8},{14,10},{16,20},{18,... | collective-permute-start | bytes 7864328 | tf_op jit(solution)/shard_map/ppermute | solution.py:53
  13.3 59.4 %collective-permute-start.3 = (bf16[80,8192]{1,0:T(8,128)(2,1)S(1)}, bf16[80,8192]{1,0:T(8,128)(2,1)S(1)}, u32[]{:S(2)}, u32[]{:S(2)}) collective-permute-start(bf16[80,8192]{1,0:T(8,128)(2,1)S(1)} %get-tuple-element.148), channel_id=1, source_target_pairs={{0,16},{2,18},{4,20},{6,22},{8,24},{10,26},{12,28},{14,30},{16,0},... | collective-permute-start | bytes 3932168 | tf_op jit(solution)/shard_map/ppermute | solution.py:53
  16.8 119.6 %collective-permute-start.9 = (bf16[4096,512]{1,0:T(8,128)(2,1)S(1)}, bf16[4096,512]{1,0:T(8,128)(2,1)S(1)}, u32[]{:S(2)}, u32[]{:S(2)}) collective-permute-start(bf16[4096,512]{1,0:T(8,128)(2,1)S(1)} %multiply_convert_fusion.refs_7_.refs_6_), channel_id=1, source_target_pairs={{0,1},{1,0},{2,3},{3,2},{4,5},{5,4},{6,7},{7,6},{8,9},{9,8},{10,11... | collective-permute-start | bytes 12582920 | tf_op jit(solution)/shard_map/ppermute | solution.py:57
  58.7 77.8 %copy-start.10 = (bf16[1152,512]{1,0:T(8,128)(2,1)}, bf16[1152,512]{1,0:T(8,128)(2,1)S(1)}, u32[]{:S(2)}) copy-start(bf16[1152,512]{1,0:T(8,128)(2,1)S(1)} %collective-permute-done.4.refs_9_.refs_8_) | copy-start | bytes 3538948
  72.8 3.1 %copy-start.7 = (bf16[80,8192]{1,0:T(8,128)(2,1)}, bf16[80,8192]{1,0:T(8,128)(2,1)S(1)}, u32[]{:S(2)}) copy-start(bf16[80,8192]{1,0:T(8,128)(2,1)S(1)} %collective-permute-done.3.refs_5_) | copy-start | bytes 3932164
  75.9 60.4 %collective-permute-start.5 = (bf16[160,8192]{1,0:T(8,128)(2,1)S(1)}, bf16[160,8192]{1,0:T(8,128)(2,1)S(1)}, u32[]{:S(2)}, u32[]{:S(2)}) collective-permute-start(bf16[160,8192]{1,0:T(8,128)(2,1)S(1)} %get-tuple-element.156), channel_id=1, source_target_pairs={{0,2},{2,0},{4,6},{6,4},{8,10},{10,8},{12,14},{14,12},{16,18},{18,... | collective-permute-start | bytes 7864328 | tf_op jit(solution)/shard_map/ppermute | solution.py:53
  76.5 59.8 %collective-permute-start.6 = (bf16[160,8192]{1,0:T(8,128)(2,1)S(1)}, bf16[160,8192]{1,0:T(8,128)(2,1)S(1)}, u32[]{:S(2)}, u32[]{:S(2)}) collective-permute-start(bf16[160,8192]{1,0:T(8,128)(2,1)S(1)} %get-tuple-element.155), channel_id=1, source_target_pairs={{0,4},{2,6},{4,0},{6,2},{8,12},{10,14},{12,8},{14,10},{16,20},{18,... | collective-permute-start | bytes 7864328 | tf_op jit(solution)/shard_map/ppermute | solution.py:53
  77.7 58.5 %collective-permute-start.7 = (bf16[80,8192]{1,0:T(8,128)(2,1)S(1)}, bf16[80,8192]{1,0:T(8,128)(2,1)S(1)}, u32[]{:S(2)}, u32[]{:S(2)}) collective-permute-start(bf16[80,8192]{1,0:T(8,128)(2,1)S(1)} %get-tuple-element.147), channel_id=1, source_target_pairs={{0,16},{2,18},{4,20},{6,22},{8,24},{10,26},{12,28},{14,30},{16,0},... | collective-permute-start | bytes 3932168 | tf_op jit(solution)/shard_map/ppermute | solution.py:53
  77.9 58.4 %collective-permute-start.8 = (bf16[1280,512]{1,0:T(8,128)(2,1)S(1)}, bf16[1280,512]{1,0:T(8,128)(2,1)S(1)}, u32[]{:S(2)}, u32[]{:S(2)}) collective-permute-start(bf16[1280,512]{1,0:T(8,128)(2,1)S(1)} %slice.87), channel_id=1, source_target_pairs={{0,8},{2,10},{4,12},{6,14},{8,0},{10,2},{12,4},{14,6},{16,24},{18,... | collective-permute-start | bytes 3932168 | tf_op jit(solution)/shard_map/ppermute | solution.py:53
  136.2 9.3 %copy-start.8 = (bf16[80,8192]{1,0:T(8,128)(2,1)}, bf16[80,8192]{1,0:T(8,128)(2,1)S(1)}, u32[]{:S(2)}) copy-start(bf16[80,8192]{1,0:T(8,128)(2,1)S(1)} %collective-permute-done.7.refs_6_) | copy-start | bytes 3932164
  136.3 8.1 %copy-start.12 = (bf16[1280,512]{1,0:T(8,128)(2,1)}, bf16[1280,512]{1,0:T(8,128)(2,1)S(1)}, u32[]{:S(2)}) copy-start(bf16[1280,512]{1,0:T(8,128)(2,1)S(1)} %collective-permute-done.8.refs_10_.refs_9_) | copy-start | bytes 3932164
  136.4 6.3 %copy-start.4 = (bf16[4096,512]{1,0:T(8,128)(2,1)}, bf16[4096,512]{1,0:T(8,128)(2,1)S(1)}, u32[]{:S(2)}) copy-start(bf16[4096,512]{1,0:T(8,128)(2,1)S(1)} %collective-permute-done.9.refs_8_.refs_7_) | copy-start | bytes 12582916
  136.4 6.3 %copy-start.1 = (bf16[160,8192]{1,0:T(8,128)(2,1)}, bf16[160,8192]{1,0:T(8,128)(2,1)S(1)}, u32[]{:S(2)}) copy-start(bf16[160,8192]{1,0:T(8,128)(2,1)S(1)} %collective-permute-done.5.refs_4_.refs_0_) | copy-start | bytes 7864324
  136.4 3.6 %copy-start.2 = (bf16[160,8192]{1,0:T(8,128)(2,1)}, bf16[160,8192]{1,0:T(8,128)(2,1)S(1)}, u32[]{:S(2)}) copy-start(bf16[160,8192]{1,0:T(8,128)(2,1)S(1)} %collective-permute-done.6.refs_3_.refs_2_) | copy-start | bytes 7864324
  136.4 44.8 %collective-permute-start.14 = (bf16[1920,512]{1,0:T(8,128)(2,1)}, bf16[1920,512]{1,0:T(8,128)(2,1)S(1)}, u32[]{:S(2)}, u32[]{:S(2)}) collective-permute-start(bf16[1920,512]{1,0:T(8,128)(2,1)} %slice.88), channel_id=1, source_target_pairs={{0,8},{2,10},{4,12},{6,14},{8,0},{10,2},{12,4},{14,6},{16,24},{18,... | collective-permute-start | bytes 5898248 | tf_op jit(solution)/shard_map/ppermute | solution.py:53
  136.5 9.0 %collective-permute-start.13 = (bf16[1280,512]{1,0:T(8,128)(2,1)S(1)}, bf16[1280,512]{1,0:T(8,128)(2,1)}, u32[]{:S(2)}, u32[]{:S(2)}) collective-permute-start(bf16[1280,512]{1,0:T(8,128)(2,1)S(1)} %collective-permute-done.8.refs_10_.refs_9_), channel_id=1, source_target_pairs={{0,1},{1,0},{2,3},{3,2},{4,5},{5,4},{6,7},{7,6},{8,9},{9,8},{10,11... | collective-permute-start | bytes 3932168 | tf_op jit(solution)/shard_map/ppermute | solution.py:57
  136.6 7.9 %collective-permute-start.12 = (bf16[1152,512]{1,0:T(8,128)(2,1)S(1)}, bf16[1152,512]{1,0:T(8,128)(2,1)S(1)}, u32[]{:S(2)}, u32[]{:S(2)}) collective-permute-start(bf16[1152,512]{1,0:T(8,128)(2,1)S(1)} %collective-permute-done.4.refs_9_.refs_8_), channel_id=1, source_target_pairs={{0,1},{1,0},{2,3},{3,2},{4,5},{5,4},{6,7},{7,6},{8,9},{9,8},{10,11... | collective-permute-start | bytes 3538952 | tf_op jit(solution)/shard_map/ppermute | solution.py:57
  142.7 52.1 %collective-permute-start.10 = (bf16[128,8192]{1,0:T(8,128)(2,1)}, bf16[128,8192]{1,0:T(8,128)(2,1)}, u32[]{:S(2)}, u32[]{:S(2)}) collective-permute-start(bf16[128,8192]{1,0:T(8,128)(2,1)} %get-tuple-element.154), channel_id=1, source_target_pairs={{0,2},{2,0},{4,6},{6,4},{8,10},{10,8},{12,14},{14,12},{16,18},{18,... | collective-permute-start | bytes 6291464 | tf_op jit(solution)/shard_map/ppermute | solution.py:53
  143.1 51.8 %collective-permute-start.11 = (bf16[128,8192]{1,0:T(8,128)(2,1)}, bf16[128,8192]{1,0:T(8,128)(2,1)}, u32[]{:S(2)}, u32[]{:S(2)}) collective-permute-start(bf16[128,8192]{1,0:T(8,128)(2,1)} %get-tuple-element.153), channel_id=1, source_target_pairs={{0,4},{2,6},{4,0},{6,2},{8,12},{10,14},{12,8},{14,10},{16,20},{18,... | collective-permute-start | bytes 6291464 | tf_op jit(solution)/shard_map/ppermute | solution.py:53
  181.2 4.1 %copy-start.9 = (bf16[1920,512]{1,0:T(8,128)(2,1)}, bf16[1920,512]{1,0:T(8,128)(2,1)S(1)}, u32[]{:S(2)}) copy-start(bf16[1920,512]{1,0:T(8,128)(2,1)S(1)} %collective-permute-done.14.refs_7_.refs_10_) | copy-start | bytes 5898244
  181.2 4.1 %collective-permute-start.15 = (bf16[1920,512]{1,0:T(8,128)(2,1)S(1)}, bf16[1920,512]{1,0:T(8,128)(2,1)}, u32[]{:S(2)}, u32[]{:S(2)}) collective-permute-start(bf16[1920,512]{1,0:T(8,128)(2,1)S(1)} %collective-permute-done.14.refs_7_.refs_10_), channel_id=1, source_target_pairs={{0,1},{1,0},{2,3},{3,2},{4,5},{5,4},{6,7},{7,6},{8,9},{9,8},{10,11... | collective-permute-start | bytes 5898248 | tf_op jit(solution)/shard_map/ppermute | solution.py:57
  196.0 23.2 %collective-permute-start.17 = (bf16[48,8192]{1,0:T(8,128)(2,1)S(1)}, bf16[48,8192]{1,0:T(8,128)(2,1)S(1)}, u32[]{:S(2)}, u32[]{:S(2)}) collective-permute-start(bf16[48,8192]{1,0:T(8,128)(2,1)S(1)} %slice.76), channel_id=1, source_target_pairs={{0,2},{2,0},{4,6},{6,4},{8,10},{10,8},{12,14},{14,12},{16,18},{18,... | collective-permute-start | bytes 2359304 | tf_op jit(solution)/shard_map/ppermute | solution.py:53
  197.5 16.2 %collective-permute-start.16 = (bf16[32,8192]{1,0:T(8,128)(2,1)S(1)}, bf16[32,8192]{1,0:T(8,128)(2,1)S(1)}, u32[]{:S(2)}, u32[]{:S(2)}) collective-permute-start(bf16[32,8192]{1,0:T(8,128)(2,1)S(1)} %slice.75), channel_id=1, source_target_pairs={{0,4},{2,6},{4,0},{6,2},{8,12},{10,14},{12,8},{14,10},{16,20},{18,... | collective-permute-start | bytes 1572872 | tf_op jit(solution)/shard_map/ppermute | solution.py:53
  199.0 3.2 %collective-permute-start.18 = (bf16[160,1024]{1,0:T(8,128)(2,1)}, bf16[160,1024]{1,0:T(8,128)(2,1)S(1)}, u32[]{:S(2)}, u32[]{:S(2)}) collective-permute-start(bf16[160,1024]{1,0:T(8,128)(2,1)} %get-tuple-element.108), channel_id=1, source_target_pairs={{0,0},{1,2},{2,4},{3,6},{4,8},{5,10},{6,12},{7,14},{8,16},{9,18},{... | collective-permute-start | bytes 983048 | tf_op jit(solution)/shard_map/ppermute | solution.py:66
  201.6 28.6 %copy-start.14 = (bf16[256,512]{1,0:T(8,128)(2,1)}, bf16[256,512]{1,0:T(8,128)(2,1)S(1)}, u32[]{:S(2)}) copy-start(bf16[256,512]{1,0:T(8,128)(2,1)S(1)} %get-tuple-element.152) | copy-start | bytes 786436
  202.1 17.0 %copy-start.17 = (bf16[160,1024]{1,0:T(8,128)(2,1)}, bf16[160,1024]{1,0:T(8,128)(2,1)S(1)}, u32[]{:S(2)}) copy-start(bf16[160,1024]{1,0:T(8,128)(2,1)S(1)} %collective-permute-done.18.refs_0_) | copy-start | bytes 983044
  213.7 14.1 %copy-start.16 = (bf16[32,8192]{1,0:T(8,128)(2,1)}, bf16[32,8192]{1,0:T(8,128)(2,1)S(1)}, u32[]{:S(2)}) copy-start(bf16[32,8192]{1,0:T(8,128)(2,1)S(1)} %collective-permute-done.16.refs_4_) | copy-start | bytes 1572868
  219.2 11.1 %copy-start.15 = (bf16[48,8192]{1,0:T(8,128)(2,1)}, bf16[48,8192]{1,0:T(8,128)(2,1)S(1)}, u32[]{:S(2)}) copy-start(bf16[48,8192]{1,0:T(8,128)(2,1)S(1)} %collective-permute-done.17.refs_5_) | copy-start | bytes 2359300
  219.2 25.7 %collective-permute-start.19 = (bf16[160,1024]{1,0:T(8,128)(2,1)}, bf16[160,1024]{1,0:T(8,128)(2,1)}, u32[]{:S(2)}, u32[]{:S(2)}) collective-permute-start(bf16[160,1024]{1,0:T(8,128)(2,1)} %get-tuple-element.114), channel_id=1, source_target_pairs={{0,4},{1,6},{2,0},{3,2},{4,12},{5,14},{6,8},{7,10},{8,20},{9,22},{... | collective-permute-start | bytes 983048 | tf_op jit(solution)/shard_map/ppermute | solution.py:66
  224.9 20.0 %collective-permute-start.20 = (bf16[160,1024]{1,0:T(8,128)(2,1)}, bf16[160,1024]{1,0:T(8,128)(2,1)}, u32[]{:S(2)}, u32[]{:S(2)}) collective-permute-start(bf16[160,1024]{1,0:T(8,128)(2,1)} %get-tuple-element.115), channel_id=1, source_target_pairs={{0,8},{1,10},{2,12},{3,14},{4,0},{5,2},{6,4},{7,6},{8,24},{9,26},{... | collective-permute-start | bytes 983048 | tf_op jit(solution)/shard_map/ppermute | solution.py:66
  224.9 20.0 %collective-permute-start.21 = (bf16[160,1024]{1,0:T(8,128)(2,1)}, bf16[160,1024]{1,0:T(8,128)(2,1)}, u32[]{:S(2)}, u32[]{:S(2)}) collective-permute-start(bf16[160,1024]{1,0:T(8,128)(2,1)} %get-tuple-element.116), channel_id=1, source_target_pairs={{0,12},{1,14},{2,8},{3,10},{4,4},{5,6},{6,0},{7,2},{8,28},{9,30},{... | collective-permute-start | bytes 983048 | tf_op jit(solution)/shard_map/ppermute | solution.py:66
  226.8 25.0 %collective-permute-start.22 = (bf16[160,1024]{1,0:T(8,128)(2,1)}, bf16[160,1024]{1,0:T(8,128)(2,1)}, u32[]{:S(2)}, u32[]{:S(2)}) collective-permute-start(bf16[160,1024]{1,0:T(8,128)(2,1)} %get-tuple-element.117.refs_14_), channel_id=1, source_target_pairs={{0,1},{1,3},{2,5},{3,7},{4,9},{5,11},{6,13},{7,15},{8,17},{9,19},{... | collective-permute-start | bytes 983048 | tf_op jit(solution)/shard_map/ppermute | solution.py:66
  255.1 25.2 %collective-permute-start.25 = (bf16[128,1408]{1,0:T(8,128)(2,1)}, bf16[128,1408]{1,0:T(8,128)(2,1)S(1)}, u32[]{:S(2)}, u32[]{:S(2)}) collective-permute-start(bf16[128,1408]{1,0:T(8,128)(2,1)} %fusion.15), channel_id=1, source_target_pairs={{0,6},{2,4},{4,2},{6,0},{8,14},{10,12},{12,10},{14,8},{16,22},{18,... | collective-permute-start | bytes 1081352 | tf_op jit(solution)/shard_map/ppermute | solution.py:53
  255.9 24.4 %collective-permute-start.24 = (bf16[128,1408]{1,0:T(8,128)(2,1)}, bf16[128,1408]{1,0:T(8,128)(2,1)}, u32[]{:S(2)}, u32[]{:S(2)}) collective-permute-start(bf16[128,1408]{1,0:T(8,128)(2,1)} %fusion.14), channel_id=1, source_target_pairs={{0,4},{2,6},{4,0},{6,2},{8,12},{10,14},{12,8},{14,10},{16,20},{18,... | collective-permute-start | bytes 1081352 | tf_op jit(solution)/shard_map/ppermute | solution.py:53
  258.1 22.1 %collective-permute-start.23 = (bf16[128,1408]{1,0:T(8,128)(2,1)}, bf16[128,1408]{1,0:T(8,128)(2,1)S(1)}, u32[]{:S(2)}, u32[]{:S(2)}) collective-permute-start(bf16[128,1408]{1,0:T(8,128)(2,1)} %fusion.13), channel_id=1, source_target_pairs={{0,2},{2,0},{4,6},{6,4},{8,10},{10,8},{12,14},{14,12},{16,18},{18,... | collective-permute-start | bytes 1081352 | tf_op jit(solution)/shard_map/ppermute | solution.py:53
  260.1 14.6 %collective-permute-start.26 = (bf16[160,1024]{1,0:T(8,128)(2,1)}, bf16[160,1024]{1,0:T(8,128)(2,1)}, u32[]{:S(2)}, u32[]{:S(2)}) collective-permute-start(bf16[160,1024]{1,0:T(8,128)(2,1)} %get-tuple-element.133), channel_id=1, source_target_pairs={{0,5},{1,7},{2,1},{3,3},{4,13},{5,15},{6,9},{7,11},{8,21},{9,23},{... | collective-permute-start | bytes 983048 | tf_op jit(solution)/shard_map/ppermute | solution.py:66
  262.0 18.2 %collective-permute-start.27 = (bf16[160,1024]{1,0:T(8,128)(2,1)}, bf16[160,1024]{1,0:T(8,128)(2,1)}, u32[]{:S(2)}, u32[]{:S(2)}) collective-permute-start(bf16[160,1024]{1,0:T(8,128)(2,1)} %get-tuple-element.134), channel_id=1, source_target_pairs={{0,9},{1,11},{2,13},{3,15},{4,1},{5,3},{6,5},{7,7},{8,25},{9,27},{... | collective-permute-start | bytes 983048 | tf_op jit(solution)/shard_map/ppermute | solution.py:66
  282.6 10.3 %collective-permute-start.28 = (bf16[64,1408]{1,0:T(8,128)(2,1)S(1)}, bf16[64,1408]{1,0:T(8,128)(2,1)S(1)}, u32[]{:S(2)}, u32[]{:S(2)}) collective-permute-start(bf16[64,1408]{1,0:T(8,128)(2,1)S(1)} %fusion.17), channel_id=1, source_target_pairs={{0,16},{2,18},{4,20},{6,22},{8,24},{10,26},{12,28},{14,30},{16,0},... | collective-permute-start | bytes 540680 | tf_op jit(solution)/shard_map/ppermute | solution.py:53
  283.2 17.3 %collective-permute-start.29 = (bf16[160,1024]{1,0:T(8,128)(2,1)S(1)}, bf16[160,1024]{1,0:T(8,128)(2,1)S(1)}, u32[]{:S(2)}, u32[]{:S(2)}) collective-permute-start(bf16[160,1024]{1,0:T(8,128)(2,1)S(1)} %copy-done.21), channel_id=1, source_target_pairs={{0,13},{1,15},{2,9},{3,11},{4,5},{5,7},{6,1},{7,3},{8,29},{9,31},{... | collective-permute-start | bytes 983048 | tf_op jit(solution)/shard_map/ppermute | solution.py:66
  300.6 1.3 collective-permute-start.30
  302.1 4.6 %collective-permute-start.31 = (bf16[32,1280]{1,0:T(8,128)(2,1)S(1)}, bf16[32,1280]{1,0:T(8,128)(2,1)S(1)}, u32[]{:S(2)}, u32[]{:S(2)}) collective-permute-start(bf16[32,1280]{1,0:T(8,128)(2,1)S(1)} %fusion.18), channel_id=1, source_target_pairs={{0,8},{2,10},{4,12},{6,14},{8,0},{10,2},{12,4},{14,6},{16,24},{18,... | collective-permute-start | bytes 245768 | tf_op jit(solution)/shard_map/ppermute | solution.py:53
  (9 other events, 16.9 us)
